TPU v7x, 512 devices: a whole 4x4x16 slice. The times are simulated.
512 devices in a mesh: dp: 16 (over x, y), expert: 32 (over z, core).
Axes of the slice: x: 4, y: 4, z: 16, core: 2. Of those that a mesh axis runs over, the one named last changes fastest.
Arguments:
- tokens: bfloat16 [1024, 2048], P('dp'), may hold values from -6 to 6
- d_mixed: bfloat16 [1024, 2048], P('dp'), may hold values from -6 to 6
- route_ids: int32 [1024, 6], replicated, may hold values from 0 to 63, all different within a row; in each aligned block of 64 rows (0 to 63, 64 to 127, ...) at most 30 rows name the same one
- route_weight: float32 [1024, 6], replicated, may hold values from 0.05 to 1
- gate_weight: bfloat16 [512, 176, 2048], P(('expert', 'dp')), may hold values from -0.125 to 0.125
- up_weight: bfloat16 [512, 176, 2048], P(('expert', 'dp')), may hold values from -0.125 to 0.125
- down_weight: bfloat16 [512, 176, 2048], P(('expert', 'dp')), may hold values from -0.15625 to 0.15625
Outputs:
- mixed: bfloat16 [1024, 2048], P('dp')
- d_route: float32 [1024, 6], P('dp')
- d_tokens: bfloat16 [1024, 2048], P('dp')
- grad_gate: bfloat16 [512, 176, 2048], P(('expert', 'dp'))
- grad_up: bfloat16 [512, 176, 2048], P(('expert', 'dp'))
- grad_down: bfloat16 [512, 176, 2048], P(('expert', 'dp'))
Inputs may be any that keep to these rules, and one draw needn't show every extreme that they name: `route_ids`: each row names 6 different experts. In each aligned block of 64 rows (the tokens of one index of dp) no expert is named by more than 30 rows, and in every draw some expert is named by exactly 30 rows of some block.
All inputs are finite; a program needn't handle non-finite values.
Results may differ from a plain program's by a relative error of at most 0.0064.
Values may be sent and summed in bfloat16 or wider, within the bound.
No kernel may reach another device: no remote copies, remote signals or barrier semaphores. Data moves between devices by JAX's collectives and lax.ppermute only.
A program may use at most 64 MiB of HBM per device.

v0:
```python
import jax
import jax.numpy as jnp
from jax import lax
from jax.sharding import PartitionSpec as P

EXP_DEV = 2


def slot_table(block_ids, expert_count):
    flat_ids = block_ids.reshape(-1)
    one_hot = (flat_ids[:, None] == jnp.arange(expert_count, dtype=jnp.int32)[None, :]).astype(
        jnp.int32
    )
    earlier = jnp.cumsum(one_hot, axis=0) - one_hot
    return jnp.sum(earlier * one_hot, axis=1)


def selection(block_ids, block_weight, first_expert, expert_span, capacity, expert_count):
    flat_ids = block_ids.reshape(-1)
    slot_numbers = slot_table(block_ids, expert_count)
    offset_ids = flat_ids - first_expert
    inside_mask = (offset_ids >= 0) & (offset_ids < expert_span)
    target_row = jnp.where(inside_mask, offset_ids * capacity + slot_numbers, -1)
    matches = (
        target_row[None, :] == jnp.arange(expert_span * capacity, dtype=jnp.int32)[:, None]
    ).astype(jnp.float32)
    matches = matches.reshape(expert_span * capacity, block_ids.shape[0], block_ids.shape[1])
    chosen = jnp.sum(matches, axis=2)
    weighted = jnp.sum(matches * block_weight[None, :, :], axis=2)
    return (matches, chosen, weighted)


def contract_first(left, right):
    return lax.dot_general(
        left, right, (((0,), (0,)), ((), ())), preferred_element_type=jnp.float32
    )


def contract_last(left, right):
    return lax.dot_general(
        left, right, (((1,), (1,)), ((), ())), preferred_element_type=jnp.float32
    )


def body(tokens, d_mixed, route_ids, route_weight, gate_weight, up_weight, down_weight):
    dp_count = lax.axis_size("dp")
    dp_index = lax.axis_index("dp")
    column_index = lax.axis_index("expert")
    expert_count = EXP_DEV * lax.axis_size("expert")
    pieces = dp_count // EXP_DEV
    token_count = tokens.shape[0]
    model_width = tokens.shape[1]
    choice_count = route_ids.shape[1]
    capacity = min(token_count, max(8, 5 * token_count * choice_count // expert_count))
    which_local = dp_index // pieces
    first_expert = column_index * EXP_DEV
    id_blocks = route_ids.reshape(dp_count, token_count, choice_count)
    weight_blocks = route_weight.reshape(dp_count, token_count, choice_count)
    own_ids = lax.dynamic_index_in_dim(id_blocks, dp_index, 0, keepdims=False)
    own_weight = lax.dynamic_index_in_dim(weight_blocks, dp_index, 0, keepdims=False)
    matches, chosen, weighted = selection(
        own_ids, own_weight, first_expert, EXP_DEV, capacity, expert_count
    )
    row_total = dp_count * capacity
    all_in, all_grad = (
        lax.all_gather(tokens, "dp", axis=0, tiled=True),
        lax.all_gather(d_mixed, "dp", axis=0, tiled=True),
    )

    def pick_rows(block_ids, block_weight):
        unused, picked, picked_weight = selection(
            block_ids, block_weight, first_expert + which_local, 1, capacity, expert_count
        )
        return (picked, jnp.sum(picked_weight, axis=1))

    chosen_all, scale_all = jax.vmap(pick_rows)(id_blocks, weight_blocks)
    chosen_all = chosen_all.astype(jnp.bfloat16)
    in_blocks = all_in.reshape(dp_count, token_count, model_width)
    grad_blocks = all_grad.reshape(dp_count, token_count, model_width)
    routed_in = jnp.einsum(
        "sct,std->scd", chosen_all, in_blocks, preferred_element_type=jnp.float32
    )
    routed_in = routed_in.astype(jnp.bfloat16).reshape(row_total, model_width)
    routed_grad = scale_all[:, :, None] * jnp.einsum(
        "sct,std->scd", chosen_all, grad_blocks, preferred_element_type=jnp.float32
    )
    routed_grad = routed_grad.astype(jnp.bfloat16).reshape(row_total, model_width)
    gate_piece = gate_weight[0]
    up_piece = up_weight[0]
    down_piece = down_weight[0]
    gate_value = contract_last(routed_in, gate_piece)
    up_value = contract_last(routed_in, up_piece)
    sigmoid_gate = jax.nn.sigmoid(gate_value)
    activated = gate_value * sigmoid_gate
    hidden = (activated * up_value).astype(jnp.bfloat16)
    part_out = jnp.dot(hidden, down_piece, preferred_element_type=jnp.float32).astype(jnp.bfloat16)
    returned = lax.all_to_all(
        part_out.reshape(dp_count, capacity, model_width),
        "dp",
        split_axis=0,
        concat_axis=0,
        tiled=True,
    )
    expert_out = jnp.sum(
        returned.reshape(EXP_DEV, pieces, capacity, model_width).astype(jnp.float32), axis=1
    )
    expert_out = expert_out.reshape(EXP_DEV * capacity, model_width)
    mixed_part = jnp.dot(weighted.T, expert_out, precision=lax.Precision.HIGHEST)
    paired = jnp.dot(expert_out, d_mixed.astype(jnp.float32).T, precision=lax.Precision.HIGHEST)
    route_part = jnp.sum(matches * paired[:, :, None], axis=0)
    mixed_sum, route_sum = lax.psum((mixed_part, route_part), "expert")
    d_hidden = contract_last(routed_grad, down_piece)
    grad_down = contract_first(hidden, routed_grad).astype(jnp.bfloat16)
    d_gate_pre = (
        d_hidden * up_value * sigmoid_gate * (1.0 + gate_value * (1.0 - sigmoid_gate))
    ).astype(jnp.bfloat16)
    d_up_pre = (d_hidden * activated).astype(jnp.bfloat16)
    grad_gate = contract_first(d_gate_pre, routed_in).astype(jnp.bfloat16)
    grad_up = contract_first(d_up_pre, routed_in).astype(jnp.bfloat16)
    part_in = (
        jnp.dot(d_gate_pre, gate_piece, preferred_element_type=jnp.float32)
        + jnp.dot(d_up_pre, up_piece, preferred_element_type=jnp.float32)
    ).astype(jnp.bfloat16)
    returned_in = lax.all_to_all(
        part_in.reshape(dp_count, capacity, model_width),
        "dp",
        split_axis=0,
        concat_axis=0,
        tiled=True,
    )
    expert_in = jnp.sum(
        returned_in.reshape(EXP_DEV, pieces, capacity, model_width).astype(jnp.float32), axis=1
    )
    expert_in = expert_in.reshape(EXP_DEV * capacity, model_width)
    token_part = jnp.dot(chosen.T, expert_in, precision=lax.Precision.HIGHEST)
    token_sum = lax.psum(token_part, "expert")
    return (
        mixed_sum.astype(jnp.bfloat16),
        route_sum,
        token_sum.astype(jnp.bfloat16),
        grad_gate[None],
        grad_up[None],
        grad_down[None],
    )


def solution(mesh):
    in_specs = (
        P("dp", None),
        P("dp", None),
        P(),
        P(),
        P(("expert", "dp"), None, None),
        P(("expert", "dp"), None, None),
        P(("expert", "dp"), None, None),
    )
    out_specs = (
        P("dp", None),
        P("dp", None),
        P("dp", None),
        P(("expert", "dp"), None, None),
        P(("expert", "dp"), None, None),
        P(("expert", "dp"), None, None),
    )
    return jax.shard_map(body, mesh=mesh, in_specs=in_specs, out_specs=out_specs, check_vma=False)
```

profile of v0, /device:TPU:1, one launch (start us, length us, event | category | flops | bytes accessed | tf_op | source)
XLA Modules:
  0.0 346.4 jit_solution(9046672223902121454)
XLA Ops:
  7.2 0.7 all-gather.3.cloned.1.call-update
  8.0 0.7 all-gather.5.cloned.1.call-update
  8.7 1.0 copy.49
  10.3 1.4 fusion.6
  11.8 25.6 %reduce-window.16 = s32[16,64,3,128]{3,1,2,0:T(8,128)S(1)} reduce-window(s32[16,64,3,128]{3,1,2,0:T(8,128)} %fusion.6, s32[]{:T(128)} %constant.49.clone.1), window={size=1x1x1x128 pad=0_0x0_0x0_0x127_0}, to_apply=%region_4.5 | reduce-window | flops 49938432 | bytes 3145732 | tf_op jit(solution)/shard_map/reduce-window.2
  37.3 1.7 slice.17
  39.0 1.9 copy.54
  43.0 40.2 %all-gather.3.cloned.1.call-done = bf16[1024,2048]{1,0:T(8,128)(2,1)} async-done(((bf16[64,2048]{1,0:T(8,128)(2,1)}), bf16[1024,2048]{1,0:T(8,128)(2,1)}) %all-gather.3.cloned.1.call-update) | async-done | bytes 4194320 | tf_op jit(solution)/shard_map/all_gather | solution.py:66
  83.2 4.3 %convolution_convert_fusion = bf16[16,30,2048]{2,1,0:T(8,128)(2,1)} fusion(bf16[16,64,2048]{2,1,0:T(8,128)(2,1)} %bitcast.109, bf16[16,30,64]{2,0,1:T(8,128)(2,1)S(1)} %get-tuple-element.7), kind=kOutput, calls=%fused_computation.4 | convolution fusion | flops 126812160 | bytes 6221824 | tf_op jit(solution)/shard_map/sct,std->scd/dot_general | solution.py:80
  87.5 1.8 reshape.137
  89.4 2.7 fusion.15
  92.0 1.5 fusion.11
  93.5 59.4 %all-gather.5.cloned.1.call-done = bf16[1024,2048]{1,0:T(8,128)(2,1)} async-done(((bf16[64,2048]{1,0:T(8,128)(2,1)}), bf16[1024,2048]{1,0:T(8,128)(2,1)}) %all-gather.5.cloned.1.call-update) | async-done | bytes 4194320 | tf_op jit(solution)/shard_map/all_gather | solution.py:67
  152.9 4.2 %multiply_convert_fusion = bf16[16,30,2048]{2,1,0:T(8,128)(2,1)} fusion(bf16[16,64,2048]{2,1,0:T(8,128)(2,1)} %bitcast.108, f32[16,30]{1,0:T(8,128)S(1)} %copy.61, bf16[16,30,64]{2,0,1:T(8,128)(2,1)S(1)} %get-tuple-element.7), kind=kOutput, calls=%fused_computation.2 | convolution fusion | flops 127795200 | bytes 6223744 | tf_op jit(solution)/shard_map/sct,std->scd/dot_general | solution.py:84
  157.1 2.8 reshape.141
  159.9 3.1 multiply_convert_fusion.1
  163.7 2.0 convolution_convert_fusion.1
  165.7 2.8 reshape.138
  168.5 5.0 %all-to-all-start = ((bf16[16,30,2048]{2,1,0:T(8,128)(2,1)}), bf16[16,30,2048]{2,1,0:T(8,128)(2,1)}, u32[]{:S(2)}, u32[]{:S(2)}) async-start(bf16[16,30,2048]{2,1,0:T(8,128)(2,1)} %reshape.138), calls=%async_computation | async-start | bytes 4194304 | tf_op jit(solution)/shard_map/all_to_all | solution.py:97
  174.5 2.1 reduce-window.14
  176.8 2.0 fusion.13
  178.8 2.1 add_convert_fusion
  180.9 2.8 reshape.142
  183.7 17.8 %all-to-all-done = bf16[16,30,2048]{2,1,0:T(8,128)(2,1)} async-done(((bf16[16,30,2048]{2,1,0:T(8,128)(2,1)}), bf16[16,30,2048]{2,1,0:T(8,128)(2,1)}, u32[]{:S(2)}, u32[]{:S(2)}) %all-to-all-start) | async-done | bytes 1966112 | tf_op jit(solution)/shard_map/all_to_all | solution.py:97
  201.4 4.6 %all-to-all-start.1 = ((bf16[16,30,2048]{2,1,0:T(8,128)(2,1)}), bf16[16,30,2048]{2,1,0:T(8,128)(2,1)}, u32[]{:S(2)}, u32[]{:S(2)}) async-start(bf16[16,30,2048]{2,1,0:T(8,128)(2,1)} %reshape.142), calls=%async_computation.1 | async-start | bytes 4194304 | tf_op jit(solution)/shard_map/all_to_all | solution.py:124
  206.4 2.3 fusion
  208.8 1.4 fusion.1
  210.5 1.4 fusion.2
  211.9 2.0 convert_reduce_fusion.1
  215.1 15.9 %all-to-all-done.1 = bf16[16,30,2048]{2,1,0:T(8,128)(2,1)} async-done(((bf16[16,30,2048]{2,1,0:T(8,128)(2,1)}), bf16[16,30,2048]{2,1,0:T(8,128)(2,1)}, u32[]{:S(2)}, u32[]{:S(2)}) %all-to-all-start.1) | async-done | bytes 1966112 | tf_op jit(solution)/shard_map/all_to_all | solution.py:124
  231.0 2.0 convert_reduce_fusion
  233.7 105.9 %all-reduce.2 = (bf16[64,2048]{1,0:T(8,128)(2,1)}, f32[64,6]{0,1:T(8,128)}, bf16[64,2048]{1,0:T(8,128)(2,1)}) all-reduce(f32[64,2048]{1,0:T(8,128)S(1)} %fusion.27, f32[64,6]{0,1:T(8,128)S(1)} %get-tuple-element.9, f32[64,2048]{1,0:T(8,128)S(1)} %fusion.29), channel_id=1, replica_groups=mesh['dp'=16,'expert'=32] {'expert'}, use_global_device_ids=true, to_apply=%region_9.10 | all-reduce | flops 262528 | bytes 1575936 | tf_op jit(solution)/shard_map/psum | solution.py:111
  (48 shorter events, 7.1 us)
Async XLA Ops:
  7.2 152.7 %copy-start = (bf16[1,176,2048]{2,1,0:T(8,128)(2,1)S(1)}, bf16[1,176,2048]{2,1,0:T(8,128)(2,1)}, u32[]{:S(2)}) copy-start(bf16[1,176,2048]{2,1,0:T(8,128)(2,1)} %param.13) | copy-start | bytes 2162692
  7.2 3.1 copy-start.7
  7.2 76.0 %all-gather.3.cloned.1.call-start = ((), (), s32[]{:S(2)}) async-start(), calls=%async_computation.2 | async-start | bytes 4456448 | tf_op jit(solution)/shard_map/all_gather | solution.py:66
  7.9 145.0 %all-gather.5.cloned.1.call-start = ((), (), s32[]{:S(2)}) async-start(), calls=%async_computation.3 | async-start | bytes 4456448 | tf_op jit(solution)/shard_map/all_gather | solution.py:67
  89.4 2.7 copy-start.3
  163.0 0.7 copy-start.5
  168.5 33.0 %all-to-all-start = ((bf16[16,30,2048]{2,1,0:T(8,128)(2,1)}), bf16[16,30,2048]{2,1,0:T(8,128)(2,1)}, u32[]{:S(2)}, u32[]{:S(2)}) async-start(bf16[16,30,2048]{2,1,0:T(8,128)(2,1)} %reshape.138), calls=%async_computation | async-start | bytes 4194304 | tf_op jit(solution)/shard_map/all_to_all | solution.py:97
  176.8 2.0 copy-start.4
  201.4 29.6 %all-to-all-start.1 = ((bf16[16,30,2048]{2,1,0:T(8,128)(2,1)}), bf16[16,30,2048]{2,1,0:T(8,128)(2,1)}, u32[]{:S(2)}, u32[]{:S(2)}) async-start(bf16[16,30,2048]{2,1,0:T(8,128)(2,1)} %reshape.142), calls=%async_computation.1 | async-start | bytes 4194304 | tf_op jit(solution)/shard_map/all_to_all | solution.py:124
  208.8 1.6 copy-start.1
  208.8 1.7 copy-start.6
  211.9 2.1 copy-start.2
Sparse Core Ops, SparseCore 0:
  11.0 72.1 all-gather.2
  86.2 66.6 all-gather.4
where the time goes:
time: 351 us; the launch traced here: 346 us
  waiting for transfers between devices  135 us (38%)
  blocking collectives  106 us (30%)
  other arithmetic  35.2 us (10%)
  matrix products  28.6 us (8%)
  local copies, waits for them, and re-layouts  18.1 us (5%)
  between operations  14.3 us (4%)
  starting transfers between devices  9.72 us (3%)
    psum x1, blocking collectives, body(): mixed_sum, route_sum = lax.psum((mixed_part, route_part), 'expert')  106 us
    all_gather x1, waiting for transfers between devices, body(): lax.all_gather(d_mixed, 'dp', axis=0, tiled=True)  59.4 us
    all_gather x1, waiting for transfers between devices, body(): lax.all_gather(tokens, 'dp', axis=0, tiled=True)  40.2 us
    another operation x4, other arithmetic  27.8 us
    all_to_all x1, waiting for transfers between devices, body(): lax.all_to_all(part_out.reshape(dp_count, capacity, model_width), 'dp', s...  17.8 us
    all_to_all x1, waiting for transfers between devices, body(): lax.all_to_all(part_in.reshape(dp_count, capacity, model_width), 'dp', sp...  15.9 us
    dot_general x3, matrix products, contract_last(): lax.dot_general(left, right, (((1,), (1,)), ((), ())), preferred_element_...  7.31 us
  transfers between devices with their start and end apart: 4, of which 4 were waited for; matrix products, arithmetic and copies ran while one was open for 18% of the time, Pallas kernels for 0%

commit v1 on v0

v1 whole, which is shorter than its diff:
```python
import jax
import jax.numpy as jnp
from jax import lax
from jax.experimental import pallas as pl
from jax.experimental.pallas import tpu as pltpu
from jax.sharding import Mesh, PartitionSpec as P

CORES = 2
EXP_DEV = 2
SLOTS = 32
LANES = 128
BF = jnp.bfloat16
F32 = jnp.float32


def dot(left, right, left_dim=1, right_dim=0):
    return lax.dot_general(
        left, right, (((left_dim,), (right_dim,)), ((), ())), preferred_element_type=F32
    )


def iota(shape, dim):
    return lax.broadcasted_iota(jnp.int32, shape, dim)


def earlier_rows(count):
    return (iota((count, count), 1) < iota((count, count), 0)).astype(BF)


def named(ids, lane_expert):
    hit = ids[:, 0:1] == lane_expert
    for k in range(1, ids.shape[1]):
        hit = jnp.logical_or(hit, ids[:, k : k + 1] == lane_expert)
    return hit


def named_weight(ids, weight, lane_expert):
    total = jnp.where(ids[:, 0:1] == lane_expert, weight[:, 0:1], 0.0)
    for k in range(1, ids.shape[1]):
        total = total + jnp.where(ids[:, k : k + 1] == lane_expert, weight[:, k : k + 1], 0.0)
    return total


def placed(hit, slot_lane):
    flag = hit.astype(F32)
    slot = dot(earlier_rows(hit.shape[0]), flag.astype(BF))
    return jnp.where(slot == slot_lane.astype(F32), flag, 0.0)


def split(value):
    high = value.astype(BF)
    return high, (value - high.astype(F32)).astype(BF)


def call(kernel, outs, scalars, *arrays, scratch=()):
    vmem = pl.BlockSpec(memory_space=pltpu.VMEM)
    return pl.pallas_call(
        kernel,
        out_shape=[jax.ShapeDtypeStruct(shape, kind) for shape, kind in outs],
        in_specs=[pl.BlockSpec(memory_space=pltpu.SMEM)] + [vmem] * len(arrays),
        out_specs=[vmem] * len(outs),
        scratch_shapes=list(scratch),
        compiler_params=pltpu.CompilerParams(vmem_limit_bytes=48 << 20),
    )(jnp.stack(scalars).astype(jnp.int32), *arrays)


def send_kernel(where, ids, tokens, out):
    first_expert = where[0]
    dp_count = out.shape[0]
    rows = tokens.shape[0]
    lane = iota((rows, EXP_DEV * SLOTS), 1)
    hit = named(ids[...], first_expert + lane // SLOTS)
    pick = placed(hit, lane % SLOTS).astype(BF)
    picked = dot(pick, tokens[...], 0, 0).astype(BF)
    for d in range(dp_count):
        j = d // (dp_count // EXP_DEV)
        out[d] = picked[j * SLOTS : (j + 1) * SLOTS]


def table_kernel(where, ids, weight, place, scale):
    expert = where[0]
    block = where_rows = 64
    total = ids.shape[0]
    lane = iota((block, SLOTS), 1)
    scale[...] = named_weight(ids[...], weight[...], jnp.full((total, 1), expert, jnp.int32))
    for b in range(total // block):
        part = ids[b * block : (b + 1) * block, :]
        hit = named(part, jnp.full((block, SLOTS), expert, jnp.int32))
        place[b * block : (b + 1) * block, :] = placed(hit, lane).astype(BF)


def forward_kernel(where, rows_in, gate_w, up_w, down_w, out, gate, up, hidden):
    x = rows_in[...]
    g = dot(x, gate_w[...], 1, 1)
    u = dot(x, up_w[...], 1, 1)
    gate[...] = g
    up[...] = u
    h = (g * jax.nn.sigmoid(g) * u).astype(BF)
    hidden[...] = h
    half = out.shape[2]
    for c in range(CORES):
        piece = dot(h, down_w[:, c * half : (c + 1) * half]).astype(BF)
        for d in range(out.shape[0] // CORES):
            out[CORES * d + c] = piece[d * SLOTS : (d + 1) * SLOTS]


def backward_kernel(
    where, d_mixed, place, scale, gate, up, gate_w, up_w, down_w, out, d_gate, d_up, d_hidden
):
    block = 64
    tall = dot(d_mixed[...], down_w[...], 1, 1) * scale[...]
    for b in range(tall.shape[0] // block):
        high, low = split(tall[b * block : (b + 1) * block])
        pick = place[b * block : (b + 1) * block, :]
        d_hidden[b * SLOTS : (b + 1) * SLOTS, :] = dot(pick, high, 0, 0) + dot(pick, low, 0, 0)
    dh = d_hidden[...]
    g = gate[...]
    sig = jax.nn.sigmoid(g)
    dg = (dh * up[...] * sig * (1.0 + g * (1.0 - sig))).astype(BF)
    du = (dh * (g * sig)).astype(BF)
    d_gate[...] = dg
    d_up[...] = du
    half = out.shape[2]
    for c in range(CORES):
        cols = slice(c * half, (c + 1) * half)
        piece = (dot(dg, gate_w[:, cols]) + dot(du, up_w[:, cols])).astype(BF)
        for d in range(out.shape[0] // CORES):
            out[CORES * d + c] = piece[d * SLOTS : (d + 1) * SLOTS]


def grads_kernel(
    where, rows_in, d_mixed, place, scale, hidden, d_gate, d_up, g_gate, g_up, g_down, spread
):
    block = 64
    for b in range(d_mixed.shape[0] // block):
        part = dot(place[b * block : (b + 1) * block, :], hidden[b * SLOTS : (b + 1) * SLOTS, :])
        spread[b * block : (b + 1) * block, :] = (
            part * scale[b * block : (b + 1) * block, :]
        ).astype(BF)
    g_down[...] = dot(spread[...], d_mixed[...], 0, 0).astype(BF)
    g_gate[...] = dot(d_gate[...], rows_in[...], 0, 0).astype(BF)
    g_up[...] = dot(d_up[...], rows_in[...], 0, 0).astype(BF)


def combine_kernel(where, returned, ids, weight, d_mixed, mixed, route, place):
    first_expert, core = where[0], where[1]
    rows = ids.shape[0]
    count, half = returned.shape
    lane = iota((rows, count), 1)
    source = lane // SLOTS
    sources_per_expert = count // SLOTS // EXP_DEV
    expert = first_expert + (source % CORES) * EXP_DEV + source // sources_per_expert
    all_ids = ids[...]
    pick = placed(named(all_ids, expert), lane % SLOTS)
    place[...] = pick.astype(BF)
    weighted = pick * named_weight(all_ids, weight[...], expert)
    high, low = split(weighted)
    back = returned[...]
    mixed[...] = dot(high, back) + dot(low, back)
    own_grad = d_mixed[:, pl.ds(pl.multiple_of(core * half, LANES), half)]
    paired = dot(own_grad, back, 1, 1) * pick
    spot = iota((rows, LANES), 1)
    result = jnp.zeros((rows, LANES), F32)
    for k in range(ids.shape[1]):
        mine = jnp.where(all_ids[:, k : k + 1] == expert, paired, 0.0)
        result = jnp.where(spot % 8 == k, jnp.sum(mine, axis=1, keepdims=True), result)
    route[...] = result


def pack_kernel(where, returned, place, mixed, route, out):
    back = dot(place[...], returned[...])
    high, low = split(route[...])
    half = returned.shape[1]
    for i in range(out.shape[0] // 2):
        rows = slice(8 * i, 8 * i + 8)
        out[2 * i, :, :half] = mixed[rows, :].astype(BF)
        out[2 * i, :, half:] = high.astype(F32)[rows].astype(BF)
        out[2 * i + 1, :, :half] = back[rows].astype(BF)
        out[2 * i + 1, :, half:] = low.astype(F32)[rows].astype(BF)


def total_kernel(where, parts, out):
    total = parts[0].astype(F32)
    for i in range(1, parts.shape[0]):
        total = total + parts[i].astype(F32)
    width = total.shape[1] - LANES
    tail = total[:, width:]
    high, low = split(tail)
    spot = iota(tail.shape, 1)
    tail = jnp.where(spot < 8, high.astype(F32), low.astype(F32)).astype(BF)
    body_part = total[:, :width].astype(BF)
    for i in range(out.shape[0]):
        out[i, :, :width] = body_part
        out[i, :, width:] = tail


def finish_kernel(where, own, other, mixed, d_tokens, route):
    core = where[0]
    width = own.shape[2] - LANES
    for source, side in ((own, core), (other, 1 - core)):
        cols = pl.ds(pl.multiple_of(side * width, LANES), width)
        for target, odd in ((mixed, 0), (d_tokens, 1)):
            for i in range(0, own.shape[0] // 2, 2):
                pair = [source[2 * (i + j) + odd, :, :width].astype(F32) for j in range(2)]
                target[8 * i : 8 * i + 16, cols] = jnp.concatenate(pair, axis=0).astype(BF)
    for i in range(own.shape[0] // 2):
        total = jnp.zeros((8, LANES), F32)
        for source in (own, other):
            for odd in range(2):
                total = total + source[2 * i + odd, :, width:].astype(F32)
        count = route.shape[1]
        route[8 * i : 8 * i + 8, :] = total[:, :count] + total[:, 8 : 8 + count]


def body(tokens, d_mixed, route_ids, route_weight, gate_weight, up_weight, down_weight):
    dp_count = lax.axis_size("dp")
    z_count = lax.axis_size("z")
    dp_index, z_index, core = lax.axis_index("dp"), lax.axis_index("z"), lax.axis_index("core")
    row_count, width = tokens.shape
    half = width // CORES
    hidden_count = gate_weight.shape[1]
    total = dp_count * row_count
    slot_rows = dp_count * SLOTS
    chip_expert = z_index * CORES * EXP_DEV
    column_expert = chip_expert + core * EXP_DEV
    expert = column_expert + dp_index // (dp_count // EXP_DEV)
    gate_piece, up_piece, down_piece = gate_weight[0], up_weight[0], down_weight[0]
    own_ids = lax.dynamic_slice_in_dim(route_ids, dp_index * row_count, row_count, 0)
    own_weight = lax.dynamic_slice_in_dim(route_weight, dp_index * row_count, row_count, 0)

    all_grad = lax.all_gather(d_mixed, "dp", axis=0, tiled=True)

    (sent,) = call(
        send_kernel, [((dp_count, SLOTS, width), BF)], [column_expert], own_ids, tokens
    )
    route_ids, route_weight, own_weight, sent = lax.optimization_barrier(
        (route_ids, route_weight, own_weight, sent)
    )
    rows_in = lax.all_to_all(sent, "dp", 0, 0, tiled=True).reshape(slot_rows, width)
    place, scale = call(
        table_kernel,
        [((total, SLOTS), BF), ((total, 1), F32)],
        [expert],
        route_ids,
        route_weight,
    )

    out, gate, up, hidden = call(
        forward_kernel,
        [
            ((CORES * dp_count, SLOTS, half), BF),
            ((slot_rows, hidden_count), F32),
            ((slot_rows, hidden_count), F32),
            ((slot_rows, hidden_count), BF),
        ],
        [expert],
        rows_in,
        gate_piece,
        up_piece,
        down_piece,
    )
    returned = lax.all_to_all(out, ("dp", "core"), 0, 0, tiled=True)

    out_in, d_gate, d_up = call(
        backward_kernel,
        [
            ((CORES * dp_count, SLOTS, half), BF),
            ((slot_rows, hidden_count), BF),
            ((slot_rows, hidden_count), BF),
        ],
        [expert],
        all_grad,
        place,
        scale,
        gate,
        up,
        gate_piece,
        up_piece,
        down_piece,
        scratch=[pltpu.VMEM((slot_rows, hidden_count), F32)],
    )
    out_in, d_gate, returned = lax.optimization_barrier((out_in, d_gate, returned))
    returned_in = lax.all_to_all(out_in, ("dp", "core"), 0, 0, tiled=True)
    grad_gate, grad_up, grad_down = call(
        grads_kernel,
        [((hidden_count, width), BF)] * 3,
        [expert],
        rows_in,
        all_grad,
        place,
        scale,
        hidden,
        d_gate,
        d_up,
        scratch=[pltpu.VMEM((total, hidden_count), BF)],
    )
    mixed_part, route_part, own_place = call(
        combine_kernel,
        [
            ((row_count, half), F32),
            ((row_count, LANES), F32),
            ((row_count, CORES * slot_rows), BF),
        ],
        [chip_expert, core],
        returned.reshape(CORES * slot_rows, half),
        own_ids,
        own_weight,
        d_mixed,
    )
    (packed,) = call(
        pack_kernel,
        [((z_count, 8, half + LANES), BF)],
        [core],
        returned_in.reshape(CORES * slot_rows, half),
        own_place,
        mixed_part,
        route_part,
    )
    parts = lax.all_to_all(packed, "z", 0, 0, tiled=True)
    (summed,) = call(total_kernel, [((z_count, 8, half + LANES), BF)], [core], parts)
    whole = lax.all_to_all(summed, "z", 0, 0, tiled=True)
    other = lax.ppermute(whole, "core", [(0, 1), (1, 0)])
    mixed, d_tokens, d_route = call(
        finish_kernel,
        [
            ((row_count, width), BF),
            ((row_count, width), BF),
            ((row_count, route_ids.shape[1]), F32),
        ],
        [core],
        whole,
        other,
    )
    return (mixed, d_route, d_tokens, grad_gate[None], grad_up[None], grad_down[None])


def solution(mesh):
    dp_count, expert_count = mesh.devices.shape
    fine = Mesh(
        mesh.devices.reshape(dp_count, expert_count // CORES, CORES), ("dp", "z", "core")
    )
    rows = P("dp", None)
    blocks = P(("z", "core", "dp"), None, None)
    in_specs = (rows, rows, P(), P(), blocks, blocks, blocks)
    out_specs = (rows, rows, rows, blocks, blocks, blocks)
    return jax.shard_map(body, mesh=fine, in_specs=in_specs, out_specs=out_specs, check_vma=False)
```

time: 351 us -> 242 us (0.69)
  blocking collectives: 106 us -> 53.9 us
  waiting for transfers between devices: 135 us -> 88.2 us
  other arithmetic: 35.2 us -> 0.08 us
  matrix products: 28.6 us -> 0 us
  Pallas kernels: 0 us -> 25.2 us
  starting transfers between devices: 9.72 us -> 33.1 us
  local copies, waits for them, and re-layouts: 18.1 us -> 25.8 us
    psum x1 -> x0, blocking collectives: 106 us -> none  [body(): mixed_sum, route_sum = lax.psum((mixed_part, route_part), 'expert')]
    all_gather x2 -> x1, waiting for transfers between devices: 99.6 us -> 34.6 us  [body(): all_grad = lax.all_gather(d_mixed, 'dp', axis=0, tiled=True)]
    all_to_all x0 -> x2, blocking collectives: none -> 53.9 us  [the longest x1 28.5 us: body(): parts = lax.all_to_all(packed, 'z', 0, 0, tiled=True)]
    dot_general x14 -> x0, matrix products: 28.6 us -> none  [the longest x3 7.31 us: contract_last(): lax.dot_general(left, right, (((1,), (1,)), ((), ())), preferred_element_...]
    another operation x4 -> x1, other arithmetic: 27.8 us -> 0.08 us  [call(): jnp.stack(scalars).astype(jnp.int32)]
    pallas_call x0 -> x9, Pallas kernels: none -> 25.2 us  [call(): pl.pallas_call(kernel, out_shape=[jax.ShapeDtypeStruct(shape, kind) for s...]
    all_to_all x2 -> x3, waiting for transfers between devices: 33.7 us -> 52.9 us  [the longest x1 27.2 us: body(): lax.all_to_all(sent, 'dp', 0, 0, tiled=True).reshape(slot_rows, width)]
    unnamed x18 -> x64, local copies, waits for them, and re-layouts: 2 us -> 20 us
  transfers between devices with their start and end apart: 4 -> 5, of which waited for: 4 -> 3; matrix products, arithmetic and copies ran while one was open for 18% -> 2% of each run, Pallas kernels for 0% -> 9%
where the time goes in v1:
time: 242 us; the launch traced here: 240 us
  waiting for transfers between devices  88.2 us (36%)
  blocking collectives  53.9 us (22%)
  starting transfers between devices  33.1 us (14%)
  local copies, waits for them, and re-layouts  25.8 us (11%)
  Pallas kernels  25.2 us (10%)
  between operations  14.2 us (6%)
    all_gather x1, waiting for transfers between devices, body(): all_grad = lax.all_gather(d_mixed, 'dp', axis=0, tiled=True)  34.6 us
    all_to_all x1, blocking collectives, body(): parts = lax.all_to_all(packed, 'z', 0, 0, tiled=True)  28.5 us
    all_to_all x1, waiting for transfers between devices, body(): lax.all_to_all(sent, 'dp', 0, 0, tiled=True).reshape(slot_rows, width)  27.2 us
    all_to_all x1, waiting for transfers between devices, body(): returned_in = lax.all_to_all(out_in, ('dp', 'core'), 0, 0, tiled=True)  25.7 us
    all_to_all x1, blocking collectives, body(): whole = lax.all_to_all(summed, 'z', 0, 0, tiled=True)  25.4 us
    pallas_call x9, Pallas kernels, call(): pl.pallas_call(kernel, out_shape=[jax.ShapeDtypeStruct(shape, kind) for s...  25.2 us
    unnamed x64, local copies, waits for them, and re-layouts  20 us
    all_to_all x1, starting transfers between devices, body(): returned = lax.all_to_all(out, ('dp', 'core'), 0, 0, tiled=True)  10.8 us
  transfers between devices with their start and end apart: 5, of which 3 were waited for; matrix products, arithmetic and copies ran while one was open for 2% of the time, Pallas kernels for 9%

profile of v1, /device:TPU:1, one launch (start us, length us, event | category | flops | bytes accessed | tf_op | source)
XLA Modules:
  0.0 240.5 jit_solution(16699353510539162729)
XLA Ops:
  10.2 0.9 copy-done.29
  11.8 1.4 copy-done.2
  13.8 7.7 %all-to-all-start = ((bf16[16,32,2048]{2,1,0:T(8,128)(2,1)}), bf16[16,32,2048]{2,1,0:T(8,128)(2,1)S(1)}, u32[]{:S(2)}, u32[]{:S(2)}) async-start(bf16[16,32,2048]{2,1,0:T(8,128)(2,1)} %copy-done.2), calls=%async_computation | async-start | bytes 4194304 | tf_op jit(solution)/shard_map/all_to_all | solution.py:239
  21.5 27.2 %all-to-all-done = bf16[16,32,2048]{2,1,0:T(8,128)(2,1)S(1)} async-done(((bf16[16,32,2048]{2,1,0:T(8,128)(2,1)}), bf16[16,32,2048]{2,1,0:T(8,128)(2,1)S(1)}, u32[]{:S(2)}, u32[]{:S(2)}) %all-to-all-start) | async-done | bytes 2097184 | tf_op jit(solution)/shard_map/all_to_all | solution.py:239
  48.7 1.4 copy-done
  50.1 1.1 copy-done.5
  51.2 3.4 %shard_map.120 = (bf16[32,32,1024]{2,1,0:T(8,128)(2,1)S(1)}, f32[512,176]{1,0:T(8,128)S(1)}, f32[512,176]{1,0:T(8,128)S(1)}, bf16[512,176]{1,0:T(8,128)(2,1)S(1)}) custom-call(s32[1]{0:T(128)} %bitcast.1.where, bf16[512,2048]{1,0:T(8,128)(2,1)} %bitcast.13, bf16[176,2048]{1,0:T(8,128)(2,1)S(1)} %bitcast.16, bf16[176,2048]{1,0:T(8,128)(2,1)S(1)} %bitcast.18, ...), custom_call_target="tpu_custom_call" | custom-call | tf_op jit(solution)/shard_map/pallas_call | solution.py:57
  54.6 1.3 copy-done.10
  55.9 0.8 copy-done.17
  56.7 0.8 copy-done.19
  58.2 10.8 %all-to-all-start.1 = ((bf16[32,32,1024]{2,1,0:T(8,128)(2,1)}), bf16[32,32,1024]{2,1,0:T(8,128)(2,1)S(1)}, u32[]{:S(2)}, u32[]{:S(2)}) async-start(bf16[32,32,1024]{2,1,0:T(8,128)(2,1)} %copy-done.10), calls=%async_computation.1 | async-start | bytes 4194304 | tf_op jit(solution)/shard_map/all_to_all | solution.py:262
  69.0 1.8 copy.15.ids
  70.8 1.8 copy.16.weight
  72.6 1.0 copy-done.11
  73.6 1.0 copy-done.12
  74.6 2.0 shard_map.119
  78.2 34.6 %all-gather.2.cloned.1.call-done.d_mixed = bf16[1024,2048]{1,0:T(8,128)(2,1)} async-done(((bf16[64,2048]{1,0:T(8,128)(2,1)}), bf16[1024,2048]{1,0:T(8,128)(2,1)}) %all-gather.2.cloned.1.call-update) | async-done | bytes 4194320 | tf_op jit(solution)/shard_map/all_gather | solution.py:231
  112.8 1.1 copy-done.6
  113.9 1.0 copy-done.8
  114.9 0.9 copy-done.14
  115.9 1.0 copy-done.18
  116.9 1.0 copy-done.20
  118.0 8.2 %shard_map.121 = (bf16[32,32,1024]{2,1,0:T(8,128)(2,1)}, bf16[512,176]{1,0:T(8,128)(2,1)S(1)}, bf16[512,176]{1,0:T(8,128)(2,1)S(1)}) custom-call(s32[1]{0:T(128)} %bitcast.1.where, bf16[1024,2048]{1,0:T(8,128)(2,1)} %all-gather.2.cloned.1.call-done.d_mixed, bf16[1024,32]{1,0:T(8,128)(2,1)S(1)} %copy-done.14, f32[1024,1]{1,0:T(8,128)S(1)} %copy-done.8, ...), custom_call_target="tpu_custom_call" | custom-call | tf_op jit(solution)/shard_map/pallas_call | solution.py:57
  127.6 6.1 %all-to-all-start.2 = ((bf16[32,32,1024]{2,1,0:T(8,128)(2,1)}), bf16[32,32,1024]{2,1,0:T(8,128)(2,1)}, u32[]{:S(2)}, u32[]{:S(2)}) async-start(bf16[32,32,1024]{2,1,0:T(8,128)(2,1)} %get-tuple-element.41), calls=%async_computation.2 | async-start | bytes 4194304 | tf_op jit(solution)/shard_map/all_to_all | solution.py:283
  133.8 2.5 %shard_map.122 = (f32[64,1024]{1,0:T(8,128)S(1)}, f32[64,128]{1,0:T(8,128)S(1)}, bf16[64,1024]{1,0:T(8,128)(2,1)S(1)}) custom-call(s32[2]{0:T(128)S(1)} %pad_add_fusion.where, bf16[1024,1024]{1,0:T(8,128)(2,1)S(1)} %bitcast.15, s32[64,6]{1,0:T(8,128)S(1)} %copy-done.22, f32[64,6]{1,0:T(8,128)S(1)} %copy-done.30, bf16[64,2048]{1,0:T(8,128)(2,1)S(1)} %copy-done.16), custom_call_target="tpu_custom_call" | custom-call | tf_op jit(solution)/shard_map/pallas_call | solution.py:57
  136.3 25.7 %all-to-all-done.2 = bf16[32,32,1024]{2,1,0:T(8,128)(2,1)} async-done(((bf16[32,32,1024]{2,1,0:T(8,128)(2,1)}), bf16[32,32,1024]{2,1,0:T(8,128)(2,1)}, u32[]{:S(2)}, u32[]{:S(2)}) %all-to-all-start.2) | async-done | bytes 2097184 | tf_op jit(solution)/shard_map/all_to_all | solution.py:283
  162.1 2.2 shard_map.123
  164.3 28.5 %all_to_all.25.parts = bf16[16,8,1152]{2,1,0:T(8,128)(2,1)S(1)} all-to-all(bf16[16,8,1152]{2,1,0:T(8,128)(2,1)S(1)} %shard_map.123), channel_id=1, replica_groups=mesh['dp'=16,'z'=16,'core'=2] {'z'}, dimensions={0} | all-to-all | bytes 589824 | tf_op jit(solution)/shard_map/all_to_all | solution.py:319
  192.8 25.4 %all_to_all.26.own = bf16[16,8,1152]{2,1,0:T(8,128)(2,1)S(1)} all-to-all(bf16[16,8,1152]{2,1,0:T(8,128)(2,1)S(1)} %shard_map.124), channel_id=1, replica_groups=mesh['dp'=16,'z'=16,'core'=2] {'z'}, dimensions={0} | all-to-all | bytes 589824 | tf_op jit(solution)/shard_map/all_to_all | solution.py:321
  218.3 8.4 %collective-permute-start = (bf16[16,8,1152]{2,1,0:T(8,128)(2,1)S(1)}, bf16[16,8,1152]{2,1,0:T(8,128)(2,1)S(1)}, u32[]{:S(2)}, u32[]{:S(2)}) collective-permute-start(bf16[16,8,1152]{2,1,0:T(8,128)(2,1)S(1)} %all_to_all.26.own), channel_id=1, source_target_pairs={{0,1},{1,0},{2,3},{3,2},{4,5},{5,4},{6,7},{7,6},{8,9},{9,8},{10,11... | collective-permute-start | bytes 884744 | tf_op jit(solution)/shard_map/ppermute | solution.py:322
  226.8 5.4 %shard_map.126 = (bf16[176,2048]{1,0:T(8,128)(2,1)}, bf16[176,2048]{1,0:T(8,128)(2,1)}, bf16[176,2048]{1,0:T(8,128)(2,1)}) custom-call(s32[1]{0:T(128)} %bitcast.1.where, bf16[512,2048]{1,0:T(8,128)(2,1)S(1)} %bitcast.14, bf16[1024,2048]{1,0:T(8,128)(2,1)} %all-gather.2.cloned.1.call-done.d_mixed, bf16[1024,32]{1,0:T(8,128)(2,1)S(1)} %copy-done.15, ...), custom_call_target="tpu_custom_call" | custom-call | tf_op jit(solution)/shard_map/pallas_call | solution.py:57
  232.1 0.8 shard_map.125
  (60 shorter events, 8.7 us)
Async XLA Ops:
  7.2 105.6 %all-gather.2.cloned.1.call-start = ((), (), s32[]{:S(2)}) async-start(), calls=%async_computation.5 | async-start | bytes 4456448 | tf_op jit(solution)/shard_map/all_gather | solution.py:231
  10.2 0.9 copy-start.29
  11.8 1.4 copy-start.2
  13.8 36.3 %copy-start.3 = (bf16[1,176,2048]{2,1,0:T(8,128)(2,1)S(1)}, bf16[1,176,2048]{2,1,0:T(8,128)(2,1)}, u32[]{:S(2)}) copy-start(bf16[1,176,2048]{2,1,0:T(8,128)(2,1)} %param.11) | copy-start | bytes 2162692
  13.8 36.3 %copy-start.4 = (bf16[1,176,2048]{2,1,0:T(8,128)(2,1)S(1)}, bf16[1,176,2048]{2,1,0:T(8,128)(2,1)}, u32[]{:S(2)}) copy-start(bf16[1,176,2048]{2,1,0:T(8,128)(2,1)} %param.12) | copy-start | bytes 2162692
  13.8 34.9 %all-to-all-start = ((bf16[16,32,2048]{2,1,0:T(8,128)(2,1)}), bf16[16,32,2048]{2,1,0:T(8,128)(2,1)S(1)}, u32[]{:S(2)}, u32[]{:S(2)}) async-start(bf16[16,32,2048]{2,1,0:T(8,128)(2,1)} %copy-done.2), calls=%async_computation | async-start | bytes 4194304 | tf_op jit(solution)/shard_map/all_to_all | solution.py:239
  48.7 1.4 copy-start
  50.1 1.1 copy-start.5
  54.6 1.3 copy-start.10
  55.9 0.8 copy-start.17
  56.7 0.8 copy-start.19
  57.5 0.7 copy-start.23
  58.2 69.4 %all-to-all-start.1 = ((bf16[32,32,1024]{2,1,0:T(8,128)(2,1)}), bf16[32,32,1024]{2,1,0:T(8,128)(2,1)S(1)}, u32[]{:S(2)}, u32[]{:S(2)}) async-start(bf16[32,32,1024]{2,1,0:T(8,128)(2,1)} %copy-done.10), calls=%async_computation.1 | async-start | bytes 4194304 | tf_op jit(solution)/shard_map/all_to_all | solution.py:262
  72.6 1.0 copy-start.11
  73.6 1.0 copy-start.12
  76.7 0.8 copy-start.7
  112.8 1.1 copy-start.6
  113.9 1.0 copy-start.8
  114.9 0.9 copy-start.14
  115.9 1.0 copy-start.18
  116.9 1.0 copy-start.20
  127.6 6.2 %copy-start.16 = (bf16[64,2048]{1,0:T(8,128)(2,1)S(1)}, bf16[64,2048]{1,0:T(8,128)(2,1)}, u32[]{:S(2)}) copy-start(bf16[64,2048]{1,0:T(8,128)(2,1)} %d_mixed.1) | copy-start | bytes 786436
  127.6 6.2 %copy-start.22 = (s32[64,6]{1,0:T(8,128)S(1)}, s32[64,6]{1,0:T(8,128)}, u32[]{:S(2)}) copy-start(s32[64,6]{1,0:T(8,128)} %copy-done.21) | copy-start | bytes 4612
  127.6 6.2 %copy-start.30 = (f32[64,6]{1,0:T(8,128)S(1)}, f32[64,6]{1,0:T(8,128)}, u32[]{:S(2)}) copy-start(f32[64,6]{1,0:T(8,128)} %copy.18.weight) | copy-start | bytes 4612
  127.6 34.4 %all-to-all-start.2 = ((bf16[32,32,1024]{2,1,0:T(8,128)(2,1)}), bf16[32,32,1024]{2,1,0:T(8,128)(2,1)}, u32[]{:S(2)}, u32[]{:S(2)}) async-start(bf16[32,32,1024]{2,1,0:T(8,128)(2,1)} %get-tuple-element.41), calls=%async_computation.2 | async-start | bytes 4194304 | tf_op jit(solution)/shard_map/all_to_all | solution.py:283
  162.0 64.7 %copy-start.1 = (bf16[16,32,2048]{2,1,0:T(8,128)(2,1)S(1)}, bf16[16,32,2048]{2,1,0:T(8,128)(2,1)}, u32[]{:S(2)}) copy-start(bf16[16,32,2048]{2,1,0:T(8,128)(2,1)} %copy-done) | copy-start | bytes 6291460
  162.0 64.7 %copy-start.9 = (f32[1024,1]{1,0:T(8,128)S(1)}, f32[1024,1]{1,0:T(8,128)}, u32[]{:S(2)}) copy-start(f32[1024,1]{1,0:T(8,128)} %copy-done.7) | copy-start | bytes 12292
  162.0 64.7 %copy-start.15 = (bf16[1024,32]{1,0:T(8,128)(2,1)S(1)}, bf16[1024,32]{1,0:T(8,128)(2,1)}, u32[]{:S(2)}) copy-start(bf16[1024,32]{1,0:T(8,128)(2,1)} %copy-done.13) | copy-start | bytes 196612
  162.0 64.7 %copy-start.24 = (bf16[512,176]{1,0:T(8,128)(2,1)S(1)}, bf16[512,176]{1,0:T(8,128)(2,1)}, u32[]{:S(2)}) copy-start(bf16[512,176]{1,0:T(8,128)(2,1)} %copy-done.23) | copy-start | bytes 540676
  162.0 64.7 %copy-start.26 = (bf16[512,176]{1,0:T(8,128)(2,1)S(1)}, bf16[512,176]{1,0:T(8,128)(2,1)}, u32[]{:S(2)}) copy-start(bf16[512,176]{1,0:T(8,128)(2,1)} %copy-done.25) | copy-start | bytes 540676
  162.1 64.7 %copy-start.28 = (bf16[512,176]{1,0:T(8,128)(2,1)S(1)}, bf16[512,176]{1,0:T(8,128)(2,1)}, u32[]{:S(2)}) copy-start(bf16[512,176]{1,0:T(8,128)(2,1)} %copy-done.27) | copy-start | bytes 540676
  218.3 13.9 %collective-permute-start = (bf16[16,8,1152]{2,1,0:T(8,128)(2,1)S(1)}, bf16[16,8,1152]{2,1,0:T(8,128)(2,1)S(1)}, u32[]{:S(2)}, u32[]{:S(2)}) collective-permute-start(bf16[16,8,1152]{2,1,0:T(8,128)(2,1)S(1)} %all_to_all.26.own), channel_id=1, source_target_pairs={{0,1},{1,0},{2,3},{3,2},{4,5},{5,4},{6,7},{7,6},{8,9},{9,8},{10,11... | collective-permute-start | bytes 884744 | tf_op jit(solution)/shard_map/ppermute | solution.py:322
  (4 other events, 2.7 us)
Sparse Core Ops, SparseCore 0:
  11.0 101.7 all-gather.1

commit v2 on v1

v2 whole, which is shorter than its diff:
```python
import jax
import jax.numpy as jnp
from jax import lax
from jax.experimental import pallas as pl
from jax.experimental.pallas import tpu as pltpu
from jax.sharding import Mesh, PartitionSpec as P

CORES = 2
EXP_DEV = 2
SLOTS = 32
LANES = 128
BF = jnp.bfloat16
F32 = jnp.float32


def dot(left, right, left_dim=1, right_dim=0):
    return lax.dot_general(
        left, right, (((left_dim,), (right_dim,)), ((), ())), preferred_element_type=F32
    )


def iota(shape, dim):
    return lax.broadcasted_iota(jnp.int32, shape, dim)


def split(value):
    high = value.astype(BF)
    return high, (value - high.astype(F32)).astype(BF)


def slot_rows_of(ids, expert, slot):
    count = ids.shape[1]
    hit = ids[0:1, :] == expert
    for k in range(1, ids.shape[0]):
        hit = jnp.logical_or(hit, ids[k : k + 1, :] == expert)
    flag = hit.astype(F32)
    earlier = (iota((count, count), 0) < iota((count, count), 1)).astype(BF)
    return jnp.where(dot(flag.astype(BF), earlier) == slot.astype(F32), flag, 0.0)


def rows_of_slots(ids, expert, slot):
    count = ids.shape[0]
    hit = ids[:, 0:1] == expert
    for k in range(1, ids.shape[1]):
        hit = jnp.logical_or(hit, ids[:, k : k + 1] == expert)
    flag = hit.astype(F32)
    earlier = (iota((count, count), 1) < iota((count, count), 0)).astype(BF)
    return jnp.where(dot(earlier, flag.astype(BF)) == slot.astype(F32), flag, 0.0)


VMEM = pl.BlockSpec(memory_space=pltpu.VMEM)
ANY = pl.BlockSpec(memory_space=pl.ANY)


def call(kernel, outs, scalars, arrays, scratch=()):
    return pl.pallas_call(
        kernel,
        out_shape=[jax.ShapeDtypeStruct(shape, kind) for shape, kind, _ in outs],
        in_specs=[pl.BlockSpec(memory_space=pltpu.SMEM)] + [space for _, space in arrays],
        out_specs=[space for _, _, space in outs],
        scratch_shapes=list(scratch),
        compiler_params=pltpu.CompilerParams(vmem_limit_bytes=48 << 20),
    )(jnp.stack(scalars).astype(jnp.int32), *[array for array, _ in arrays])


def begin(pairs, sems):
    copies = [pltpu.make_async_copy(a, b, sems.at[i]) for i, (a, b) in enumerate(pairs)]
    for copy in copies:
        copy.start()
    return copies


def send_kernel(where, ids, tokens, out, held, picked, in_sem, out_sem):
    (load,) = begin([(tokens, held)], in_sem)
    spot = iota((EXP_DEV * SLOTS, 1), 0)
    pick = slot_rows_of(ids[...], where[0] + spot // SLOTS, spot % SLOTS).astype(BF)
    load.wait()
    picked[...] = dot(pick, held[...]).astype(BF).reshape(picked.shape)
    per_expert = out.shape[0] // EXP_DEV
    for copy in begin([(picked.at[d // per_expert], out.at[d]) for d in range(out.shape[0])], out_sem):
        copy.wait()


def forward_kernel(
    where, rows_in, gate_w, up_w, down_w, out, x, gate_v, up_v, down_v, y, in_sem, out_sem
):
    parts = 2
    blocks = x.shape[0] // parts
    loads = begin(
        [(gate_w, gate_v), (rows_in.at[:blocks], x.at[:blocks]), (up_w, up_v), (down_w, down_v)]
        + [(rows_in.at[blocks:], x.at[blocks:])],
        in_sem,
    )
    stores = []
    half = y.shape[3]
    for p in range(parts):
        span = slice(p * blocks, (p + 1) * blocks)
        if p == 0:
            loads[0].wait()
            loads[1].wait()
        else:
            loads[4].wait()
        rows = x[span].reshape(blocks * SLOTS, x.shape[2])
        g = dot(rows, gate_v[...], 1, 1)
        if p == 0:
            loads[2].wait()
        u = dot(rows, up_v[...], 1, 1)
        h = (g * jax.nn.sigmoid(g) * u).astype(BF)
        if p == 0:
            loads[3].wait()
        for c in range(CORES):
            piece = dot(h, down_v[:, c * half : (c + 1) * half]).astype(BF)
            y[c, span] = piece.reshape(blocks, SLOTS, half)
            i = CORES * p + c
            store = pltpu.make_async_copy(y.at[c, span], out.at[span, c], out_sem.at[i])
            store.start()
            stores.append(store)
    for store in stores:
        store.wait()


def factors_kernel(
    where, rows_in, gate_w, up_w, ids, weight, place, gate_factor, up_factor, hidden
):
    expert = where[0]
    block = 64
    x = rows_in[...]
    g = dot(x, gate_w[...], 1, 1)
    u = dot(x, up_w[...], 1, 1)
    sig = jax.nn.sigmoid(g)
    act = g * sig
    gate_factor[...] = u * sig * (1.0 + g * (1.0 - sig))
    up_factor[...] = act
    hidden[...] = (act * u).astype(BF)
    slot = iota((SLOTS, 1), 0)
    for b in range(ids.shape[1] // block):
        cols, rows = slice(b * block, (b + 1) * block), slice(b * SLOTS, (b + 1) * SLOTS)
        part = ids[:, cols]
        pick = slot_rows_of(part, jnp.full((SLOTS, 1), expert, jnp.int32), slot)
        place[rows, :] = pick.astype(BF)
        scale = jnp.zeros((1, block), F32)
        for k in range(part.shape[0]):
            scale = scale + jnp.where(part[k : k + 1, :] == expert, weight[k : k + 1, cols], 0.0)
        scale = jnp.sum(pick * scale, axis=1, keepdims=True)
        gate_factor[rows, :] = gate_factor[rows, :] * scale
        up_factor[rows, :] = up_factor[rows, :] * scale
        hidden[rows, :] = (hidden[rows, :].astype(F32) * scale).astype(BF)


def backward_kernel(
    where, d_mixed, place, gate_factor, up_factor, gate_w, up_w, down_w, out, d_gate, d_up,
    grad_v, place_v, gate_f, up_f, gate_v, up_v, down_v, tall, y, in_sem, out_sem
):
    parts = 2
    block = 64
    half = y.shape[3]
    blocks = y.shape[1] // parts
    near, far = slice(0, blocks), slice(blocks, 2 * blocks)
    loads = begin(
        [
            (down_w, down_v),
            (d_mixed.at[near], grad_v.at[near]),
            (place, place_v),
            (d_mixed.at[far], grad_v.at[far]),
            (gate_factor, gate_f),
            (up_factor, up_f),
            (gate_w, gate_v),
            (up_w, up_v),
        ],
        in_sem,
    )
    stores = []
    for p, span in enumerate((near, far)):
        if p == 0:
            loads[0].wait()
            loads[1].wait()
        else:
            loads[3].wait()
        high = jnp.zeros((blocks * block, down_v.shape[0]), F32)
        for c in range(CORES):
            part = grad_v[span, c].reshape(blocks * block, half)
            high = high + dot(part, down_v[:, c * half : (c + 1) * half], 1, 1)
        high, low = split(high)
        if p == 0:
            loads[2].wait()
        for i in range(blocks):
            b = p * blocks + i
            pick = place_v[b * SLOTS : (b + 1) * SLOTS, :]
            rows = slice(i * block, (i + 1) * block)
            tall[b * SLOTS : (b + 1) * SLOTS, :] = dot(pick, high[rows]) + dot(pick, low[rows])
        if p == 0:
            for load in loads[4:]:
                load.wait()
        rows = slice(p * blocks * SLOTS, (p + 1) * blocks * SLOTS)
        dg = (tall[rows, :] * gate_f[rows, :]).astype(BF)
        du = (tall[rows, :] * up_f[rows, :]).astype(BF)
        d_gate[rows, :] = dg
        d_up[rows, :] = du
        for c in range(CORES):
            cols = slice(c * half, (c + 1) * half)
            piece = (dot(dg, gate_v[:, cols]) + dot(du, up_v[:, cols])).astype(BF)
            y[c, span] = piece.reshape(blocks, SLOTS, half)
            i = CORES * p + c
            store = pltpu.make_async_copy(y.at[c, span], out.at[span, c], out_sem.at[i])
            store.start()
            stores.append(store)
    for store in stores:
        store.wait()


def grads_kernel(
    where, rows_in, d_mixed, place, hidden, d_gate, d_up, g_gate, g_up, g_down, spread
):
    block = 64
    half = d_mixed.shape[3]
    for b in range(d_mixed.shape[0]):
        rows = slice(b * SLOTS, (b + 1) * SLOTS)
        part = dot(place[rows, :], hidden[rows, :], 0, 0)
        spread[b * block : (b + 1) * block, :] = part.astype(BF)
    for c in range(CORES):
        part = d_mixed[:, c].reshape(spread.shape[0], half)
        g_down[:, c * half : (c + 1) * half] = dot(spread[...], part, 0, 0).astype(BF)
    g_gate[...] = dot(d_gate[...], rows_in[...], 0, 0).astype(BF)
    g_up[...] = dot(d_up[...], rows_in[...], 0, 0).astype(BF)


def combine_kernel(where, returned, ids, weight, d_mixed, mixed, route, place):
    first_expert, core = where[0], where[1]
    rows = ids.shape[0]
    count, half = returned.shape
    lane = iota((rows, count), 1)
    source = lane // SLOTS
    sources_per_expert = count // SLOTS // EXP_DEV
    expert = first_expert + (source % CORES) * EXP_DEV + source // sources_per_expert
    all_ids = ids[...]
    pick = rows_of_slots(all_ids, expert, lane % SLOTS)
    place[...] = pick.astype(BF)
    scale = jnp.zeros((rows, count), F32)
    for k in range(ids.shape[1]):
        scale = scale + jnp.where(all_ids[:, k : k + 1] == expert, weight[:, k : k + 1], 0.0)
    high, low = split(pick * scale)
    back = returned[...]
    mixed[...] = dot(high, back) + dot(low, back)
    own_grad = d_mixed[:, pl.ds(pl.multiple_of(core * half, LANES), half)]
    paired = dot(own_grad, back, 1, 1) * pick
    spot = iota((rows, LANES), 1)
    result = jnp.zeros((rows, LANES), F32)
    for k in range(ids.shape[1]):
        mine = jnp.where(all_ids[:, k : k + 1] == expert, paired, 0.0)
        result = jnp.where(spot % 8 == k, jnp.sum(mine, axis=1, keepdims=True), result)
    route[...] = result


def pack_kernel(where, returned, place, mixed, route, out, back, in_sem):
    half = returned.shape[1]
    step = back.shape[0] // in_sem.shape[0]
    spans = [slice(i * step, (i + 1) * step) for i in range(in_sem.shape[0])]
    loads = begin([(returned.at[span], back.at[span]) for span in spans], in_sem)
    high, low = split(route[...])
    for i in range(out.shape[0] // 2):
        rows = slice(8 * i, 8 * i + 8)
        out[2 * i, :, :half] = mixed[rows, :].astype(BF)
        out[2 * i, :, half:] = high.astype(F32)[rows].astype(BF)
        out[2 * i + 1, :, half:] = low.astype(F32)[rows].astype(BF)
    total = jnp.zeros((place.shape[0], half), F32)
    for span, load in zip(spans, loads):
        load.wait()
        total = total + dot(place[:, span], back[span])
    for i in range(out.shape[0] // 2):
        out[2 * i + 1, :, :half] = total[8 * i : 8 * i + 8].astype(BF)


def total_kernel(where, parts, out):
    total = parts[0].astype(F32)
    for i in range(1, parts.shape[0]):
        total = total + parts[i].astype(F32)
    width = total.shape[1] - LANES
    tail = total[:, width:]
    high, low = split(tail)
    spot = iota(tail.shape, 1)
    tail = jnp.where(spot < 8, high.astype(F32), low.astype(F32)).astype(BF)
    body_part = total[:, :width].astype(BF)
    for i in range(out.shape[0]):
        out[i, :, :width] = body_part
        out[i, :, width:] = tail


def finish_kernel(where, own, other, mixed, d_tokens, route):
    core = where[0]
    width = own.shape[2] - LANES
    for source, side in ((own, core), (other, 1 - core)):
        cols = pl.ds(pl.multiple_of(side * width, LANES), width)
        for target, odd in ((mixed, 0), (d_tokens, 1)):
            for i in range(0, own.shape[0] // 2, 2):
                pair = [source[2 * (i + j) + odd, :, :width].astype(F32) for j in range(2)]
                target[8 * i : 8 * i + 16, cols] = jnp.concatenate(pair, axis=0).astype(BF)
    parts = []
    for i in range(own.shape[0] // 2):
        total = jnp.zeros((8, LANES), F32)
        for source in (own, other):
            for odd in range(2):
                total = total + source[2 * i + odd, :, width:].astype(F32)
        parts.append(total)
    total = jnp.concatenate(parts, axis=0).T
    count = route.shape[0]
    route[...] = total[:count] + total[8 : 8 + count]


def body(tokens, d_mixed, route_ids, route_weight, gate_weight, up_weight, down_weight):
    dp_count = lax.axis_size("dp")
    z_count = lax.axis_size("z")
    dp_index, z_index, core = lax.axis_index("dp"), lax.axis_index("z"), lax.axis_index("core")
    row_count, width = tokens.shape
    half = width // CORES
    hidden_count = gate_weight.shape[1]
    total = dp_count * row_count
    slot_rows = dp_count * SLOTS
    dma = pltpu.SemaphoreType.DMA
    chip_expert = z_index * CORES * EXP_DEV
    column_expert = chip_expert + core * EXP_DEV
    expert = column_expert + dp_index // (dp_count // EXP_DEV)
    gate_piece, up_piece, down_piece = gate_weight[0], up_weight[0], down_weight[0]
    weight_v = pltpu.VMEM((hidden_count, width), BF)
    sent_shape = (dp_count, CORES, SLOTS, half)

    own_half = lax.dynamic_slice_in_dim(d_mixed, core * half, half, 1)
    all_grad = lax.all_gather(own_half, ("dp", "core"), axis=0, tiled=True)
    all_grad = all_grad.reshape(dp_count, CORES, row_count, half)

    own_ids = lax.dynamic_slice_in_dim(route_ids, dp_index * row_count, row_count, 0)
    (sent,) = call(
        send_kernel,
        [((dp_count, SLOTS, width), BF, ANY)],
        [column_expert],
        [(own_ids.T, VMEM), (tokens, ANY)],
        [
            pltpu.VMEM((row_count, width), BF),
            pltpu.VMEM((EXP_DEV, SLOTS, width), BF),
            dma((1,)),
            dma((dp_count,)),
        ],
    )
    route_ids, route_weight, own_ids, sent = lax.optimization_barrier(
        (route_ids, route_weight, own_ids, sent)
    )
    own_weight = lax.dynamic_slice_in_dim(route_weight, dp_index * row_count, row_count, 0)
    rows_in = lax.all_to_all(sent, "dp", 0, 0, tiled=True)

    (out,) = call(
        forward_kernel,
        [(sent_shape, BF, ANY)],
        [expert],
        [(rows_in, ANY), (gate_piece, ANY), (up_piece, ANY), (down_piece, ANY)],
        [
            pltpu.VMEM((dp_count, SLOTS, width), BF),
            weight_v,
            weight_v,
            weight_v,
            pltpu.VMEM((CORES, dp_count, SLOTS, half), BF),
            dma((5,)),
            dma((4,)),
        ],
    )
    out, rows_in = lax.optimization_barrier((out, rows_in))
    rows_in = rows_in.reshape(slot_rows, width)
    returned = lax.all_to_all(
        out.reshape(CORES * dp_count, SLOTS, half), ("dp", "core"), 0, 0, tiled=True
    )
    place, gate_factor, up_factor, hidden = call(
        factors_kernel,
        [
            ((slot_rows, row_count), BF, VMEM),
            ((slot_rows, hidden_count), F32, VMEM),
            ((slot_rows, hidden_count), F32, VMEM),
            ((slot_rows, hidden_count), BF, VMEM),
        ],
        [expert],
        [
            (rows_in, VMEM),
            (gate_piece, VMEM),
            (up_piece, VMEM),
            (route_ids.T, VMEM),
            (route_weight.T, VMEM),
        ],
    )

    out_in, d_gate, d_up = call(
        backward_kernel,
        [
            (sent_shape, BF, ANY),
            ((slot_rows, hidden_count), BF, VMEM),
            ((slot_rows, hidden_count), BF, VMEM),
        ],
        [expert],
        [
            (all_grad, ANY),
            (place, ANY),
            (gate_factor, ANY),
            (up_factor, ANY),
            (gate_piece, ANY),
            (up_piece, ANY),
            (down_piece, ANY),
        ],
        [
            pltpu.VMEM((dp_count, CORES, row_count, half), BF),
            pltpu.VMEM((slot_rows, row_count), BF),
            pltpu.VMEM((slot_rows, hidden_count), F32),
            pltpu.VMEM((slot_rows, hidden_count), F32),
            weight_v,
            weight_v,
            weight_v,
            pltpu.VMEM((slot_rows, hidden_count), F32),
            pltpu.VMEM((CORES, dp_count, SLOTS, half), BF),
            dma((8,)),
            dma((4,)),
        ],
    )
    out_in, d_gate, returned = lax.optimization_barrier((out_in, d_gate, returned))
    returned_in = lax.all_to_all(
        out_in.reshape(CORES * dp_count, SLOTS, half), ("dp", "core"), 0, 0, tiled=True
    )
    grads = call(
        grads_kernel,
        [((hidden_count, width), BF, VMEM)] * 3,
        [expert],
        [
            (rows_in, VMEM),
            (all_grad, VMEM),
            (place, VMEM),
            (hidden, VMEM),
            (d_gate, VMEM),
            (d_up, VMEM),
        ],
        [pltpu.VMEM((total, hidden_count), BF)],
    )
    mixed_part, route_part, own_place = call(
        combine_kernel,
        [
            ((row_count, half), F32, VMEM),
            ((row_count, LANES), F32, VMEM),
            ((row_count, CORES * slot_rows), BF, VMEM),
        ],
        [chip_expert, core],
        [
            (returned.reshape(CORES * slot_rows, half), VMEM),
            (own_ids, VMEM),
            (own_weight, VMEM),
            (d_mixed, VMEM),
        ],
    )
    grad_gate, grad_up, grad_down, own_place = lax.optimization_barrier((*grads, own_place))
    (packed,) = call(
        pack_kernel,
        [((z_count, 8, half + LANES), BF, VMEM)],
        [core],
        [
            (returned_in.reshape(CORES * slot_rows, half), ANY),
            (own_place, VMEM),
            (mixed_part, VMEM),
            (route_part, VMEM),
        ],
        [pltpu.VMEM((CORES * slot_rows, half), BF), dma((4,))],
    )
    parts = lax.all_to_all(packed, "z", 0, 0, tiled=True)
    (summed,) = call(
        total_kernel, [((z_count, 8, half + LANES), BF, VMEM)], [core], [(parts, VMEM)]
    )
    whole = lax.all_to_all(summed, "z", 0, 0, tiled=True)
    other = lax.ppermute(whole, "core", [(0, 1), (1, 0)])
    mixed, d_tokens, d_route = call(
        finish_kernel,
        [
            ((row_count, width), BF, VMEM),
            ((row_count, width), BF, VMEM),
            ((route_ids.shape[1], row_count), F32, VMEM),
        ],
        [core],
        [(whole, VMEM), (other, VMEM)],
    )
    return (mixed, d_route.T, d_tokens, grad_gate[None], grad_up[None], grad_down[None])


def solution(mesh):
    dp_count, expert_count = mesh.devices.shape
    fine = Mesh(
        mesh.devices.reshape(dp_count, expert_count // CORES, CORES), ("dp", "z", "core")
    )
    rows = P("dp", None)
    blocks = P(("z", "core", "dp"), None, None)
    in_specs = (rows, rows, P(), P(), blocks, blocks, blocks)
    out_specs = (rows, rows, rows, blocks, blocks, blocks)
    return jax.shard_map(body, mesh=fine, in_specs=in_specs, out_specs=out_specs, check_vma=False)
```

time: 242 us -> 230 us (0.950)
  waiting for transfers between devices: 88.2 us -> 76.5 us
  Pallas kernels: 25.2 us -> 28.8 us
  local copies, waits for them, and re-layouts: 25.8 us -> 23.2 us
    all_to_all x3, waiting for transfers between devices: 52.9 us -> 44.1 us  [the longest x1 26.6 us: body(): rows_in = lax.all_to_all(sent, 'dp', 0, 0, tiled=True)]
    pallas_call x9, Pallas kernels: 25.2 us -> 28.8 us  [call(): pl.pallas_call(kernel, out_shape=[jax.ShapeDtypeStruct(shape, kind) for s...]
    all_gather x1, waiting for transfers between devices: 34.6 us -> 31.2 us  [body(): all_grad = lax.all_gather(own_half, ('dp', 'core'), axis=0, tiled=True)]
    optimization_barrier x3 -> x2, local copies, waits for them, and re-layouts: 4.26 us -> 1.74 us  [body(): lax.optimization_barrier((route_ids, route_weight, own_ids, sent))]
    unnamed x64 -> x56, local copies, waits for them, and re-layouts: 20 us -> 17.6 us
  transfers between devices with their start and end apart: 5 -> 5, of which waited for: 3 -> 4; matrix products, arithmetic and copies ran while one was open for 2% -> 2% of each run, Pallas kernels for 9% -> 11%
where the time goes in v2:
time: 230 us; the launch traced here: 229 us
  waiting for transfers between devices  76.5 us (33%)
  blocking collectives  54.5 us (24%)
  starting transfers between devices  32 us (14%)
  Pallas kernels  28.8 us (13%)
  local copies, waits for them, and re-layouts  23.2 us (10%)
  between operations  14.3 us (6%)
    all_gather x1, waiting for transfers between devices, body(): all_grad = lax.all_gather(own_half, ('dp', 'core'), axis=0, tiled=True)  31.2 us
    all_to_all x1, blocking collectives, body(): parts = lax.all_to_all(packed, 'z', 0, 0, tiled=True)  29 us
    pallas_call x9, Pallas kernels, call(): pl.pallas_call(kernel, out_shape=[jax.ShapeDtypeStruct(shape, kind) for s...  28.8 us
    all_to_all x1, waiting for transfers between devices, body(): rows_in = lax.all_to_all(sent, 'dp', 0, 0, tiled=True)  26.6 us
    all_to_all x1, blocking collectives, body(): whole = lax.all_to_all(summed, 'z', 0, 0, tiled=True)  25.4 us
    unnamed x56, local copies, waits for them, and re-layouts  17.6 us
    all_to_all x1, waiting for transfers between devices, body(): lax.all_to_all(out_in.reshape(CORES * dp_count, SLOTS, half), ('dp', 'cor...  17.5 us
    all_to_all x1, starting transfers between devices, body(): lax.all_to_all(out.reshape(CORES * dp_count, SLOTS, half), ('dp', 'core')...  10.4 us
  transfers between devices with their start and end apart: 5, of which 4 were waited for; matrix products, arithmetic and copies ran while one was open for 2% of the time, Pallas kernels for 11%

profile of v2, /device:TPU:1, one launch (start us, length us, event | category | flops | bytes accessed | tf_op | source)
XLA Modules:
  0.0 229.2 jit_solution(14428628730807773529)
XLA Ops:
  7.2 1.6 constant_dynamic-slice_fusion.2
  11.1 0.9 copy-done.23
  12.0 3.2 %shard_map.118 = bf16[16,32,2048]{2,1,0:T(8,128)(2,1)S(1)} custom-call(s32[1]{0:T(128)} %bitcast.3.where, s32[6,64]{1,0:T(8,128)S(1)} %fusion.ids, bf16[64,2048]{1,0:T(8,128)(2,1)S(1)} %copy-done.23), custom_call_target="tpu_custom_call" | custom-call | tf_op jit(solution)/shard_map/pallas_call | solution.py:56
  15.3 1.4 copy-done.3
  16.6 7.7 %all-to-all-start = ((bf16[16,32,2048]{2,1,0:T(8,128)(2,1)}), bf16[16,32,2048]{2,1,0:T(8,128)(2,1)S(1)}, u32[]{:S(2)}, u32[]{:S(2)}) async-start(bf16[16,32,2048]{2,1,0:T(8,128)(2,1)} %copy-done.3), calls=%async_computation | async-start | bytes 4194304 | tf_op jit(solution)/shard_map/all_to_all | solution.py:347
  24.4 26.6 %all-to-all-done.rows_in = bf16[16,32,2048]{2,1,0:T(8,128)(2,1)S(1)} async-done(((bf16[16,32,2048]{2,1,0:T(8,128)(2,1)}), bf16[16,32,2048]{2,1,0:T(8,128)(2,1)S(1)}, u32[]{:S(2)}, u32[]{:S(2)}) %all-to-all-start) | async-done | bytes 2097184 | tf_op jit(solution)/shard_map/all_to_all | solution.py:347
  51.0 1.4 copy-done
  52.4 1.1 copy-done.6
  53.5 4.9 %shard_map.119 = bf16[16,2,32,1024]{3,2,1,0:T(8,128)(2,1)S(1)} custom-call(s32[1]{0:T(128)} %bitcast.1.where, bf16[16,32,2048]{2,1,0:T(8,128)(2,1)} %copy-done, bf16[176,2048]{1,0:T(8,128)(2,1)S(1)} %bitcast.25, bf16[176,2048]{1,0:T(8,128)(2,1)S(1)} %bitcast.28, bf16[176,2048]{1,0:T(8,128)(2,1)S(1)} %bitcast.31), custom_call_target="tpu_custom_call" | custom-call | tf_op jit(solution)/shard_map/pallas_call | solution.py:56
  58.5 1.3 copy-done.2
  59.9 10.4 %all-to-all-start.1 = ((bf16[32,32,1024]{2,1,0:T(8,128)(2,1)}), bf16[32,32,1024]{2,1,0:T(8,128)(2,1)}, u32[]{:S(2)}, u32[]{:S(2)}) async-start(bf16[32,32,1024]{2,1,0:T(8,128)(2,1)} %bitcast.24), calls=%async_computation.1 | async-start | bytes 4194304 | tf_op jit(solution)/shard_map/all_to_all | solution.py:366
  71.8 1.5 shard_map.120
  74.0 0.8 copy-done.13
  74.8 0.8 copy-done.15
  76.3 31.2 %all-gather.2.cloned.1.call-done = bf16[2048,1024]{1,0:T(8,128)(2,1)} async-done(((bf16[64,1024]{1,0:T(8,128)(2,1)}), bf16[2048,1024]{1,0:T(8,128)(2,1)}) %all-gather.2.cloned.1.call-update) | async-done | bytes 4194320 | tf_op jit(solution)/shard_map/all_gather | solution.py:327
  107.4 1.1 copy-done.7
  108.5 0.9 copy-done.11
  109.4 1.0 copy-done.14
  110.5 1.0 copy-done.16
  111.5 7.5 %shard_map.121 = (bf16[16,2,32,1024]{3,2,1,0:T(8,128)(2,1)S(1)}, bf16[512,176]{1,0:T(8,128)(2,1)S(1)}, bf16[512,176]{1,0:T(8,128)(2,1)S(1)}) custom-call(s32[1]{0:T(128)} %bitcast.1.where, bf16[16,2,64,1024]{3,2,1,0:T(8,128)(2,1)} %bitcast.36, bf16[512,64]{1,0:T(8,128)(2,1)S(1)} %copy-done.11, f32[512,176]{1,0:T(8,128)S(1)} %copy-done.14, ...), custom_call_target="tpu_custom_call" | custom-call | tf_op jit(solution)/shard_map/pallas_call | solution.py:56
  119.1 1.4 copy-done.8
  121.9 5.4 %all-to-all-start.2 = ((bf16[32,32,1024]{2,1,0:T(8,128)(2,1)}), bf16[32,32,1024]{2,1,0:T(8,128)(2,1)}, u32[]{:S(2)}, u32[]{:S(2)}) async-start(bf16[32,32,1024]{2,1,0:T(8,128)(2,1)} %bitcast.33), calls=%async_computation.2 | async-start | bytes 4194304 | tf_op jit(solution)/shard_map/all_to_all | solution.py:419
  127.3 1.0 copy.15
  129.2 5.3 %shard_map.122 = (bf16[176,2048]{1,0:T(8,128)(2,1)}, bf16[176,2048]{1,0:T(8,128)(2,1)}, bf16[176,2048]{1,0:T(8,128)(2,1)}) custom-call(s32[1]{0:T(128)} %bitcast.1.where, bf16[512,2048]{1,0:T(8,128)(2,1)S(1)} %bitcast.23, bf16[16,2,64,1024]{3,2,1,0:T(8,128)(2,1)} %bitcast.37, bf16[512,64]{1,0:T(8,128)(2,1)S(1)} %copy-done.12, ...), custom_call_target="tpu_custom_call" | custom-call | tf_op jit(solution)/shard_map/pallas_call | solution.py:56
  134.6 3.6 %shard_map.123 = (f32[64,1024]{1,0:T(8,128)S(1)}, f32[64,128]{1,0:T(8,128)S(1)}, bf16[64,1024]{1,0:T(8,128)(2,1)S(1)}) custom-call(s32[2]{0:T(128)S(1)} %pad_add_fusion.where, bf16[1024,1024]{1,0:T(8,128)(2,1)} %bitcast.15.returned, s32[64,6]{1,0:T(8,128)S(1)} %copy-done.26, f32[64,6]{1,0:T(8,128)S(1)} %constant_dynamic-slice_fusion.weight, ...), custom_call_target="tpu_custom_call" | custom-call | tf_op jit(solution)/shard_map/pallas_call | solution.py:56
  138.2 17.5 %all-to-all-done.2 = bf16[32,32,1024]{2,1,0:T(8,128)(2,1)} async-done(((bf16[32,32,1024]{2,1,0:T(8,128)(2,1)}), bf16[32,32,1024]{2,1,0:T(8,128)(2,1)}, u32[]{:S(2)}, u32[]{:S(2)}) %all-to-all-start.2) | async-done | bytes 2097184 | tf_op jit(solution)/shard_map/all_to_all | solution.py:419
  155.6 1.8 shard_map.124
  157.4 29.0 %all_to_all.25.parts = bf16[16,8,1152]{2,1,0:T(8,128)(2,1)S(1)} all-to-all(bf16[16,8,1152]{2,1,0:T(8,128)(2,1)S(1)} %shard_map.124), channel_id=1, replica_groups=mesh['dp'=16,'z'=16,'core'=2] {'z'}, dimensions={0} | all-to-all | bytes 589824 | tf_op jit(solution)/shard_map/all_to_all | solution.py:464
  186.5 25.4 %all_to_all.26.own = bf16[16,8,1152]{2,1,0:T(8,128)(2,1)S(1)} all-to-all(bf16[16,8,1152]{2,1,0:T(8,128)(2,1)S(1)} %shard_map.125), channel_id=1, replica_groups=mesh['dp'=16,'z'=16,'core'=2] {'z'}, dimensions={0} | all-to-all | bytes 589824 | tf_op jit(solution)/shard_map/all_to_all | solution.py:468
  211.9 8.4 %collective-permute-start = (bf16[16,8,1152]{2,1,0:T(8,128)(2,1)S(1)}, bf16[16,8,1152]{2,1,0:T(8,128)(2,1)S(1)}, u32[]{:S(2)}, u32[]{:S(2)}) collective-permute-start(bf16[16,8,1152]{2,1,0:T(8,128)(2,1)S(1)} %all_to_all.26.own), channel_id=1, source_target_pairs={{0,1},{1,0},{2,3},{3,2},{4,5},{5,4},{6,7},{7,6},{8,9},{9,8},{10,11... | collective-permute-start | bytes 884744 | tf_op jit(solution)/shard_map/ppermute | solution.py:469
  220.4 1.2 collective-permute-done.other
  221.6 0.8 shard_map.126
  (53 shorter events, 7.5 us)
Async XLA Ops:
  7.2 100.2 %all-gather.2.cloned.1.call-start = ((), (), s32[]{:S(2)}) async-start(), calls=%async_computation.5 | async-start | bytes 4325376 | tf_op jit(solution)/shard_map/all_gather | solution.py:327
  11.1 0.9 copy-start.23
  15.3 1.4 copy-start.3
  16.6 35.8 %copy-start.4 = (bf16[1,176,2048]{2,1,0:T(8,128)(2,1)S(1)}, bf16[1,176,2048]{2,1,0:T(8,128)(2,1)}, u32[]{:S(2)}) copy-start(bf16[1,176,2048]{2,1,0:T(8,128)(2,1)} %param.11) | copy-start | bytes 2162692
  16.6 35.8 %copy-start.5 = (bf16[1,176,2048]{2,1,0:T(8,128)(2,1)S(1)}, bf16[1,176,2048]{2,1,0:T(8,128)(2,1)}, u32[]{:S(2)}) copy-start(bf16[1,176,2048]{2,1,0:T(8,128)(2,1)} %param.12) | copy-start | bytes 2162692
  16.6 34.4 %all-to-all-start = ((bf16[16,32,2048]{2,1,0:T(8,128)(2,1)}), bf16[16,32,2048]{2,1,0:T(8,128)(2,1)S(1)}, u32[]{:S(2)}, u32[]{:S(2)}) async-start(bf16[16,32,2048]{2,1,0:T(8,128)(2,1)} %copy-done.3), calls=%async_computation | async-start | bytes 4194304 | tf_op jit(solution)/shard_map/all_to_all | solution.py:347
  51.0 1.4 copy-start
  52.4 1.1 copy-start.6
  58.5 1.4 copy-start.2
  59.9 10.4 %copy-start.1 = (bf16[16,32,2048]{2,1,0:T(8,128)(2,1)S(1)}, bf16[16,32,2048]{2,1,0:T(8,128)(2,1)}, u32[]{:S(2)}) copy-start(bf16[16,32,2048]{2,1,0:T(8,128)(2,1)} %copy-done) | copy-start | bytes 6291460
  59.9 62.0 %all-to-all-start.1 = ((bf16[32,32,1024]{2,1,0:T(8,128)(2,1)}), bf16[32,32,1024]{2,1,0:T(8,128)(2,1)}, u32[]{:S(2)}, u32[]{:S(2)}) async-start(bf16[32,32,1024]{2,1,0:T(8,128)(2,1)} %bitcast.24), calls=%async_computation.1 | async-start | bytes 4194304 | tf_op jit(solution)/shard_map/all_to_all | solution.py:366
  70.3 0.8 copy-start.24
  71.0 0.8 copy-start.27
  74.0 0.8 copy-start.13
  74.8 0.8 copy-start.15
  75.6 0.7 copy-start.17
  107.4 1.1 copy-start.7
  108.5 0.9 copy-start.11
  109.4 1.0 copy-start.14
  110.5 1.0 copy-start.16
  119.1 1.4 copy-start.8
  120.5 0.7 copy-start.19
  121.2 0.7 copy-start.21
  121.9 5.4 %copy-start.25 = (f32[1024,6]{0,1:T(8,128)S(1)}, f32[1024,6]{0,1:T(8,128)}, u32[]{:S(2)}) copy-start(f32[1024,6]{0,1:T(8,128)} %param.10) | copy-start | bytes 73732
  121.9 7.3 %copy-start.12 = (bf16[512,64]{1,0:T(8,128)(2,1)S(1)}, bf16[512,64]{1,0:T(8,128)(2,1)}, u32[]{:S(2)}) copy-start(bf16[512,64]{1,0:T(8,128)(2,1)} %copy-done.10) | copy-start | bytes 196612
  121.9 7.3 %copy-start.18 = (bf16[512,176]{1,0:T(8,128)(2,1)S(1)}, bf16[512,176]{1,0:T(8,128)(2,1)}, u32[]{:S(2)}) copy-start(bf16[512,176]{1,0:T(8,128)(2,1)} %copy-done.17) | copy-start | bytes 540676
  121.9 7.3 %copy-start.20 = (bf16[512,176]{1,0:T(8,128)(2,1)S(1)}, bf16[512,176]{1,0:T(8,128)(2,1)}, u32[]{:S(2)}) copy-start(bf16[512,176]{1,0:T(8,128)(2,1)} %copy-done.19) | copy-start | bytes 540676
  121.9 7.3 %copy-start.22 = (bf16[512,176]{1,0:T(8,128)(2,1)S(1)}, bf16[512,176]{1,0:T(8,128)(2,1)}, u32[]{:S(2)}) copy-start(bf16[512,176]{1,0:T(8,128)(2,1)} %copy-done.21) | copy-start | bytes 540676
  121.9 33.7 %all-to-all-start.2 = ((bf16[32,32,1024]{2,1,0:T(8,128)(2,1)}), bf16[32,32,1024]{2,1,0:T(8,128)(2,1)}, u32[]{:S(2)}, u32[]{:S(2)}) async-start(bf16[32,32,1024]{2,1,0:T(8,128)(2,1)} %bitcast.33), calls=%async_computation.2 | async-start | bytes 4194304 | tf_op jit(solution)/shard_map/all_to_all | solution.py:419
  129.2 5.4 %copy-start.9 = (bf16[64,2048]{1,0:T(8,128)(2,1)S(1)}, bf16[64,2048]{1,0:T(8,128)(2,1)}, u32[]{:S(2)}) copy-start(bf16[64,2048]{1,0:T(8,128)(2,1)} %d_mixed.1) | copy-start | bytes 786436
  129.2 5.3 %copy-start.26 = (s32[64,6]{1,0:T(8,128)S(1)}, s32[64,6]{1,0:T(8,128)}, u32[]{:S(2)}) copy-start(s32[64,6]{1,0:T(8,128)} %copy.16.ids) | copy-start | bytes 4612
  211.9 9.6 %collective-permute-start = (bf16[16,8,1152]{2,1,0:T(8,128)(2,1)S(1)}, bf16[16,8,1152]{2,1,0:T(8,128)(2,1)S(1)}, u32[]{:S(2)}, u32[]{:S(2)}) collective-permute-start(bf16[16,8,1152]{2,1,0:T(8,128)(2,1)S(1)} %all_to_all.26.own), channel_id=1, source_target_pairs={{0,1},{1,0},{2,3},{3,2},{4,5},{5,4},{6,7},{7,6},{8,9},{9,8},{10,11... | collective-permute-start | bytes 884744 | tf_op jit(solution)/shard_map/ppermute | solution.py:469
  (1 other events, 0.7 us)
Sparse Core Ops, SparseCore 0:
  11.7 95.6 all-gather.1

commit v3 on v1

v3 whole, which is shorter than its diff:
```python
import math

import jax
import jax.numpy as jnp
from jax import lax
from jax.experimental import pallas as pl
from jax.experimental.pallas import tpu as pltpu
from jax.sharding import Mesh, PartitionSpec as P

CORES = 2
EXP_DEV = 2
SLOTS = 30
ROWS = 32
LANES = 128
BF = jnp.bfloat16
F32 = jnp.float32


def dot(left, right, left_dim=1, right_dim=0):
    return lax.dot_general(
        left, right, (((left_dim,), (right_dim,)), ((), ())), preferred_element_type=F32
    )


def iota(shape, dim):
    return lax.broadcasted_iota(jnp.int32, shape, dim)


def split(value):
    high = value.astype(BF)
    return high, (value - high.astype(F32)).astype(BF)


def slot_rows_of(ids, expert, slot):
    count = ids.shape[1]
    hit = ids[0:1, :] == expert
    for k in range(1, ids.shape[0]):
        hit = jnp.logical_or(hit, ids[k : k + 1, :] == expert)
    flag = hit.astype(F32)
    earlier = (iota((count, count), 0) < iota((count, count), 1)).astype(BF)
    return jnp.where(dot(flag.astype(BF), earlier) == slot.astype(F32), flag, 0.0)


def rows_of_slots(ids, expert, slot):
    count = ids.shape[0]
    hit = ids[:, 0:1] == expert
    for k in range(1, ids.shape[1]):
        hit = jnp.logical_or(hit, ids[:, k : k + 1] == expert)
    flag = hit.astype(F32)
    earlier = (iota((count, count), 1) < iota((count, count), 0)).astype(BF)
    return jnp.where(dot(earlier, flag.astype(BF)) == slot.astype(F32), flag, 0.0)


VMEM = pl.BlockSpec(memory_space=pltpu.VMEM)
HBM = pl.BlockSpec(memory_space=pltpu.HBM)


def call(kernel, outs, scalars, arrays, scratch=(), vmem=8):
    ins = [i for i, (_, space) in enumerate(arrays) if space is HBM]
    kept = [i for i, (_, _, space) in enumerate(outs) if space is HBM]
    count, total = len(arrays), len(arrays) + len(outs)

    def wrapped(where, *refs):
        given, results, rest = list(refs[:count]), list(refs[count:total]), list(refs[total:])
        in_sem, out_sem = rest.pop(), rest.pop()
        loads = {}
        for n, i in enumerate(ins):
            loads[i] = pltpu.make_async_copy(given[i], rest[n], in_sem.at[n])
            loads[i].start()
            given[i] = rest[n]
        rest = rest[len(ins) :]
        targets = {}
        for n, i in enumerate(kept):
            targets[i] = (results[i], out_sem.at[n])
            results[i] = rest[n]
        rest = rest[len(kept) :]
        stores = []

        def ready(*names):
            for i in names:
                if i in loads:
                    loads.pop(i).wait()

        def done(i):
            target, sem = targets.pop(i)
            stores.append(pltpu.make_async_copy(results[i], target, sem))
            stores[-1].start()

        kernel(where, ready, done, *given, *results, *rest)
        ready(*list(loads))
        for i in list(targets):
            done(i)
        for store in stores:
            store.wait()

    def held(array, space):
        return pltpu.with_memory_space_constraint(array, pltpu.HBM) if space is HBM else array

    def result(shape, kind, space):
        return pltpu.HBM(shape, kind) if space is HBM else jax.ShapeDtypeStruct(shape, kind)

    dma = pltpu.SemaphoreType.DMA
    return pl.pallas_call(
        wrapped,
        out_shape=[result(*out) for out in outs],
        in_specs=[pl.BlockSpec(memory_space=pltpu.SMEM)] + [space for _, space in arrays],
        out_specs=[space for _, _, space in outs],
        scratch_shapes=[pltpu.VMEM(arrays[i][0].shape, arrays[i][0].dtype) for i in ins]
        + [pltpu.VMEM(outs[i][0], outs[i][1]) for i in kept]
        + list(scratch)
        + [dma((max(1, len(kept)),)), dma((max(1, len(ins)),))],
        compiler_params=pltpu.CompilerParams(vmem_limit_bytes=vmem << 20),
    )(jnp.stack(scalars).astype(jnp.int32), *[held(*array) for array in arrays])


def padded(block):
    extra = jnp.zeros((ROWS - block.shape[0], block.shape[1]), F32)
    return jnp.concatenate([block.astype(F32), extra], axis=0)


def send_kernel(where, ready, done, ids, tokens, out):
    spot = iota((EXP_DEV * ROWS, 1), 0)
    pick = slot_rows_of(ids[...], where[0] + spot // ROWS, spot % ROWS).astype(BF)
    ready(1)
    picked = dot(pick, tokens[...]).astype(BF)
    per_expert = out.shape[0] // EXP_DEV
    for d in range(out.shape[0]):
        first = d // per_expert * ROWS
        out[d] = picked[first : first + SLOTS]


def weights_of_slots(expert, ids, weight):
    slot = iota((ROWS, 1), 0)
    pick = slot_rows_of(ids, jnp.full((ROWS, 1), expert, jnp.int32), slot)
    scale = jnp.zeros((1, ids.shape[1]), F32)
    for k in range(ids.shape[0]):
        scale = scale + jnp.where(ids[k : k + 1, :] == expert, weight[k : k + 1, :], 0.0)
    return jnp.sum(pick * scale, axis=1, keepdims=True)


def forward_kernel(
    where, ready, done, ids, weight, rows_in, gate_w, up_w, down_w,
    out, x, gate_factor, up_factor, hidden
):
    blocks = rows_in.shape[0]
    block = ids.shape[1] // blocks
    half = out.shape[2]
    for b in range(blocks):
        x[b * ROWS : (b + 1) * ROWS, :] = padded(rows_in[b]).astype(BF)
    done(1)
    ready(3, 4)
    g = dot(x[...], gate_w[...], 1, 1)
    u = dot(x[...], up_w[...], 1, 1)
    sig = jax.nn.sigmoid(g)
    act = g * sig
    h = (act * u).astype(BF)
    ready(5)
    for c in range(CORES):
        piece = dot(h, down_w[:, c * half : (c + 1) * half]).astype(BF)
        for d in range(blocks):
            out[CORES * d + c] = piece[d * ROWS : d * ROWS + SLOTS]
    done(0)
    gate_factor[...] = u * sig * (1.0 + g * (1.0 - sig))
    up_factor[...] = act
    hidden[...] = h
    for b in range(blocks):
        cols, rows = slice(b * block, (b + 1) * block), slice(b * ROWS, (b + 1) * ROWS)
        scale = weights_of_slots(where[0], ids[:, cols], weight[:, cols])
        gate_factor[rows, :] = gate_factor[rows, :] * scale
        up_factor[rows, :] = up_factor[rows, :] * scale
        hidden[rows, :] = (hidden[rows, :].astype(F32) * scale).astype(BF)


def backward_kernel(
    where, ready, done, rows_grad, down_w, gate_factor, up_factor, gate_w, up_w,
    out, rows, d_gate, d_up
):
    blocks = rows_grad.shape[0]
    half = out.shape[2]
    ready(0)
    for b in range(blocks):
        rows[b * ROWS : (b + 1) * ROWS, :] = padded(rows_grad[b]).astype(BF)
    ready(1)
    d_hidden = dot(rows[...], down_w[...], 1, 1)
    ready(2, 3)
    dg = (d_hidden * gate_factor[...]).astype(BF)
    du = (d_hidden * up_factor[...]).astype(BF)
    ready(4, 5)
    for c in range(CORES):
        cols = slice(c * half, (c + 1) * half)
        piece = (dot(dg, gate_w[:, cols]) + dot(du, up_w[:, cols])).astype(BF)
        for d in range(blocks):
            out[CORES * d + c] = piece[d * ROWS : d * ROWS + SLOTS]
    done(0)
    d_gate[...] = dg
    d_up[...] = du


def grads_kernel(
    where, ready, done, x, rows_grad, hidden, d_gate, d_up, g_gate, g_up, g_down
):
    ready(1, 2)
    g_down[...] = dot(hidden[...], rows_grad[...], 0, 0).astype(BF)
    done(2)
    ready(0, 3)
    g_gate[...] = dot(d_gate[...], x[...], 0, 0).astype(BF)
    done(0)
    ready(4)
    g_up[...] = dot(d_up[...], x[...], 0, 0).astype(BF)


def gathered(returned, total):
    sources = returned.shape[0]
    pieces = sources // CORES // EXP_DEV
    for j in range(EXP_DEV):
        for c in range(CORES):
            part = None
            for d in range(j * pieces, (j + 1) * pieces):
                block = returned[CORES * d + c].astype(F32)
                part = block if part is None else part + block
            first = (CORES * j + c) * ROWS
            total[first : first + ROWS, :] = padded(part)
    return split(total[...])


def combine_kernel(
    where, ready, done, returned, ids, weight, d_mixed, mixed, route, place, total
):
    first_expert, core = where[0], where[1]
    rows = ids.shape[0]
    half = returned.shape[2]
    count = total.shape[0]
    lane = iota((rows, count), 1)
    source = lane // ROWS
    expert = first_expert + (source % CORES) * EXP_DEV + source // CORES
    all_ids = ids[...]
    pick = rows_of_slots(all_ids, expert, lane % ROWS)
    place[...] = pick.astype(BF)
    scale = jnp.zeros((rows, count), F32)
    for k in range(ids.shape[1]):
        scale = scale + jnp.where(all_ids[:, k : k + 1] == expert, weight[:, k : k + 1], 0.0)
    high, low = split(pick * scale)
    ready(0)
    back, rest = gathered(returned, total)
    mixed[...] = dot(high, back) + (dot(low, back) + dot(high, rest))
    ready(3)
    own_grad = d_mixed[:, pl.ds(pl.multiple_of(core * half, LANES), half)]
    paired = (dot(own_grad, back, 1, 1) + dot(own_grad, rest, 1, 1)) * pick
    spot = iota((rows, LANES), 1)
    result = jnp.zeros((rows, LANES), F32)
    for k in range(ids.shape[1]):
        mine = jnp.where(all_ids[:, k : k + 1] == expert, paired, 0.0)
        result = jnp.where(spot % 8 == k, jnp.sum(mine, axis=1, keepdims=True), result)
    route[...] = result


def pack_kernel(where, ready, done, returned, place, mixed, route, out, total):
    half = returned.shape[2]
    high, low = split(route[...])
    for i in range(out.shape[0] // 2):
        rows = slice(8 * i, 8 * i + 8)
        out[2 * i, :, :half] = mixed[rows, :].astype(BF)
        out[2 * i, :, half:] = high.astype(F32)[rows].astype(BF)
        out[2 * i + 1, :, half:] = low.astype(F32)[rows].astype(BF)
    ready(0)
    back, rest = gathered(returned, total)
    sums = dot(place[...], back) + dot(place[...], rest)
    for i in range(out.shape[0] // 2):
        out[2 * i + 1, :, :half] = sums[8 * i : 8 * i + 8].astype(BF)


def total_kernel(where, ready, done, parts, out):
    total = parts[0].astype(F32)
    for i in range(1, parts.shape[0]):
        total = total + parts[i].astype(F32)
    width = total.shape[1] - LANES
    tail = total[:, width:]
    high, low = split(tail)
    spot = iota(tail.shape, 1)
    tail = jnp.where(spot < 8, high.astype(F32), low.astype(F32)).astype(BF)
    body_part = total[:, :width].astype(BF)
    for i in range(out.shape[0]):
        out[i, :, :width] = body_part
        out[i, :, width:] = tail


def finish_kernel(where, ready, done, own, other, mixed, d_tokens, route):
    core = where[0]
    width = own.shape[2] - LANES
    for source, side in ((own, core), (other, 1 - core)):
        cols = pl.ds(pl.multiple_of(side * width, LANES), width)
        for target, odd in ((mixed, 0), (d_tokens, 1)):
            for i in range(0, own.shape[0] // 2, 2):
                pair = [source[2 * (i + j) + odd, :, :width].astype(F32) for j in range(2)]
                target[8 * i : 8 * i + 16, cols] = jnp.concatenate(pair, axis=0).astype(BF)
    parts = []
    for i in range(own.shape[0] // 2):
        total = jnp.zeros((8, LANES), F32)
        for source in (own, other):
            for odd in range(2):
                total = total + source[2 * i + odd, :, width:].astype(F32)
        parts.append(total)
    total = jnp.concatenate(parts, axis=0).T
    count = route.shape[0]
    route[...] = total[:count] + total[8 : 8 + count]


def body(tokens, d_mixed, route_ids, route_weight, gate_weight, up_weight, down_weight):
    side = lax.axis_size("y")
    dp_count = lax.axis_size("x") * side
    z_count = lax.axis_size("z")
    z_index, core = lax.axis_index("z"), lax.axis_index("core")
    dp_index = lax.axis_index("x") * side + lax.axis_index("y")
    row_count, width = tokens.shape
    half = width // CORES
    hidden_count = gate_weight.shape[1]
    rows = dp_count * ROWS
    chip_expert = z_index * CORES * EXP_DEV
    column_expert = chip_expert + core * EXP_DEV
    expert = column_expert + dp_index // (dp_count // EXP_DEV)
    gate_piece, up_piece, down_piece = gate_weight[0], up_weight[0], down_weight[0]
    out_shape = (CORES * dp_count, SLOTS, half)
    gathered_v = pltpu.VMEM((CORES * EXP_DEV * ROWS, half), F32)

    def own_rows(array):
        return lax.dynamic_slice_in_dim(array, dp_index * row_count, row_count, 0)

    def send(array, ids):
        (sent,) = call(
            send_kernel,
            [((dp_count, SLOTS, width), BF, HBM)],
            [column_expert],
            [(ids, VMEM), (array, HBM)],
        )
        return sent

    sent = send(tokens, own_rows(route_ids).T)
    sent, route_ids, route_weight = lax.optimization_barrier((sent, route_ids, route_weight))
    rows_in = lax.all_to_all(sent, ("x", "y"), 0, 0, tiled=True)
    sent_grad = send(d_mixed, own_rows(route_ids).T)
    rows_grad = lax.all_to_all(sent_grad, ("x", "y"), 0, 0, tiled=True)

    out, x, gate_factor, up_factor, hidden = call(
        forward_kernel,
        [
            (out_shape, BF, HBM),
            ((rows, width), BF, HBM),
            ((rows, hidden_count), F32, HBM),
            ((rows, hidden_count), F32, HBM),
            ((rows, hidden_count), BF, HBM),
        ],
        [expert],
        [
            (route_ids.T, VMEM),
            (route_weight.T, VMEM),
            (rows_in, VMEM),
            (gate_piece, HBM),
            (up_piece, HBM),
            (down_piece, HBM),
        ],
        vmem=24,
    )
    out, rows_grad = lax.optimization_barrier((out, rows_grad))
    returned = lax.all_to_all(out, ("x", "y", "core"), 0, 0, tiled=True)

    out_in, padded_grad, d_gate, d_up = call(
        backward_kernel,
        [
            (out_shape, BF, HBM),
            ((rows, width), BF, HBM),
            ((rows, hidden_count), BF, HBM),
            ((rows, hidden_count), BF, HBM),
        ],
        [expert],
        [
            (rows_grad, HBM),
            (down_piece, HBM),
            (gate_factor, HBM),
            (up_factor, HBM),
            (gate_piece, HBM),
            (up_piece, HBM),
        ],
        vmem=24,
    )
    grads = call(
        grads_kernel,
        [((hidden_count, width), BF, HBM)] * 3,
        [expert],
        [(x, HBM), (padded_grad, HBM), (hidden, HBM), (d_gate, HBM), (d_up, HBM)],
        vmem=24,
    )
    grad_gate, grad_up, grad_down, out_in, route_ids, route_weight = lax.optimization_barrier(
        (*grads, out_in, route_ids, route_weight)
    )
    returned_in = lax.all_to_all(out_in, ("x", "y", "core"), 0, 0, tiled=True)
    mixed_part, route_part, own_place = call(
        combine_kernel,
        [
            ((row_count, half), F32, VMEM),
            ((row_count, LANES), F32, VMEM),
            ((row_count, CORES * EXP_DEV * ROWS), BF, VMEM),
        ],
        [chip_expert, core],
        [
            (returned, VMEM),
            (own_rows(route_ids), VMEM),
            (own_rows(route_weight), VMEM),
            (d_mixed, HBM),
        ],
        [gathered_v],
        vmem=16,
    )
    (packed,) = call(
        pack_kernel,
        [((z_count, 8, half + LANES), BF, VMEM)],
        [core],
        [(returned_in, VMEM), (own_place, VMEM), (mixed_part, VMEM), (route_part, VMEM)],
        [gathered_v],
    )
    parts = lax.all_to_all(packed, "z", 0, 0, tiled=True)
    (summed,) = call(
        total_kernel, [((z_count, 8, half + LANES), BF, VMEM)], [core], [(parts, VMEM)]
    )
    whole = lax.all_to_all(summed, "z", 0, 0, tiled=True)
    other = lax.ppermute(whole, "core", [(0, 1), (1, 0)])
    mixed, d_tokens, d_route = call(
        finish_kernel,
        [
            ((row_count, width), BF, VMEM),
            ((row_count, width), BF, VMEM),
            ((route_ids.shape[1], row_count), F32, VMEM),
        ],
        [core],
        [(whole, VMEM), (other, VMEM)],
    )
    return (mixed, d_route.T, d_tokens, grad_gate[None], grad_up[None], grad_down[None])


def solution(mesh):
    dp_count, expert_count = mesh.devices.shape
    side = math.isqrt(dp_count)
    fine = Mesh(
        mesh.devices.reshape(side, side, expert_count // CORES, CORES), ("x", "y", "z", "core")
    )
    rows = P(("x", "y"), None)
    blocks = P(("z", "core", "x", "y"), None, None)
    in_specs = (rows, rows, P(), P(), blocks, blocks, blocks)
    out_specs = (rows, rows, rows, blocks, blocks, blocks)
    return jax.shard_map(body, mesh=fine, in_specs=in_specs, out_specs=out_specs, check_vma=False)
```

time: 242 us -> 208 us (0.86)
  local copies, waits for them, and re-layouts: 25.8 us -> 1.32 us
  between operations: 14.2 us -> 0.84 us
  starting transfers between devices: 33.1 us -> 38.1 us
  waiting for transfers between devices: 88.2 us -> 84.7 us
  Pallas kernels: 25.2 us -> 28.6 us
    all_gather x1 -> x0, waiting for transfers between devices: 34.6 us -> none  [body(): all_grad = lax.all_gather(d_mixed, 'dp', axis=0, tiled=True)]
    all_to_all x3 -> x4, waiting for transfers between devices: 52.9 us -> 83.5 us  [the longest x1 25.4 us: body(): returned_in = lax.all_to_all(out_in, ('x', 'y', 'core'), 0, 0, tiled=True)]
    unnamed x64 -> x4, local copies, waits for them, and re-layouts: 20 us -> 0.01 us
    all_to_all x3 -> x4, starting transfers between devices: 24.6 us -> 29.6 us  [the longest x1 10.3 us: body(): returned = lax.all_to_all(out, ('x', 'y', 'core'), 0, 0, tiled=True)]
    optimization_barrier x3 -> x2, local copies, waits for them, and re-layouts: 4.26 us -> 0.45 us  [body(): lax.optimization_barrier((*grads, out_in, route_ids, route_weight))]
    pallas_call x9, Pallas kernels: 25.2 us -> 28.6 us  [call(): pl.pallas_call(wrapped, out_shape=[result(*out) for out in outs], in_spec...]
  transfers between devices with their start and end apart: 5 -> 5, of which waited for: 3 -> 5; matrix products, arithmetic and copies ran while one was open for 2% -> 0% of each run, Pallas kernels for 9% -> 11%
where the time goes in v3:
time: 208 us
  waiting for transfers between devices  84.7 us (41%)
  blocking collectives  54.1 us (26%)
  starting transfers between devices  38.1 us (18%)
  Pallas kernels  28.6 us (14%)
    pallas_call x9, Pallas kernels, call(): pl.pallas_call(wrapped, out_shape=[result(*out) for out in outs], in_spec...  28.6 us
    all_to_all x1, blocking collectives, body(): parts = lax.all_to_all(packed, 'z', 0, 0, tiled=True)  28.6 us
    all_to_all x1, blocking collectives, body(): whole = lax.all_to_all(summed, 'z', 0, 0, tiled=True)  25.4 us
    all_to_all x1, waiting for transfers between devices, body(): returned_in = lax.all_to_all(out_in, ('x', 'y', 'core'), 0, 0, tiled=True)  25.4 us
    all_to_all x1, waiting for transfers between devices, body(): rows_in = lax.all_to_all(sent, ('x', 'y'), 0, 0, tiled=True)  22.6 us
    all_to_all x1, waiting for transfers between devices, body(): rows_grad = lax.all_to_all(sent_grad, ('x', 'y'), 0, 0, tiled=True)  19.3 us
    all_to_all x1, waiting for transfers between devices, body(): returned = lax.all_to_all(out, ('x', 'y', 'core'), 0, 0, tiled=True)  16.2 us
    all_to_all x1, starting transfers between devices, body(): returned = lax.all_to_all(out, ('x', 'y', 'core'), 0, 0, tiled=True)  10.3 us
  transfers between devices with their start and end apart: 5, of which 5 were waited for; matrix products, arithmetic and copies ran while one was open for 0% of the time, Pallas kernels for 11%

profile of v3, /device:TPU:1, one launch (start us, length us, event | category | flops | bytes accessed | tf_op | source)
XLA Modules:
  0.0 207.7 jit_solution(1411845160747498006)
XLA Ops:
  0.6 0.8 dynamic-slice_bitcast_fusion.1.refs_0_
  1.4 2.6 %shard_map.118 = bf16[16,30,2048]{2,1,0:T(8,128)(2,1)} custom-call(s32[1]{0:T(128)} %bitcast.2.where, s32[6,64]{1,0:T(8,128)S(1)} %dynamic-slice_bitcast_fusion.1.refs_0_, bf16[64,2048]{1,0:T(8,128)(2,1)} %refs_1_.2), custom_call_target="tpu_custom_call" | custom-call | tf_op jit(solution)/shard_map/pallas_call | solution.py:103
  4.1 0.0 copy-start
  4.1 7.6 %all-to-all-start = ((bf16[16,30,2048]{2,1,0:T(8,128)(2,1)}), bf16[16,30,2048]{2,1,0:T(8,128)(2,1)S(1)}, u32[]{:S(2)}, u32[]{:S(2)}) async-start(bf16[16,30,2048]{2,1,0:T(8,128)(2,1)} %shard_map.118), calls=%async_computation | async-start | bytes 4194304 | tf_op jit(solution)/shard_map/all_to_all | solution.py:339
  11.7 0.0 copy-done
  11.7 0.1 dynamic-slice_bitcast_fusion.refs_0_
  11.8 2.6 %shard_map.120 = bf16[16,30,2048]{2,1,0:T(8,128)(2,1)} custom-call(s32[1]{0:T(128)} %bitcast.2.where, s32[6,64]{1,0:T(8,128)S(1)} %dynamic-slice_bitcast_fusion.refs_0_, bf16[64,2048]{1,0:T(8,128)(2,1)} %refs_3_.1), custom_call_target="tpu_custom_call" | custom-call | tf_op jit(solution)/shard_map/pallas_call | solution.py:103
  14.4 0.0 copy-start.1
  14.4 22.6 %all-to-all-done.refs_2_ = bf16[16,30,2048]{2,1,0:T(8,128)(2,1)S(1)} async-done(((bf16[16,30,2048]{2,1,0:T(8,128)(2,1)}), bf16[16,30,2048]{2,1,0:T(8,128)(2,1)S(1)}, u32[]{:S(2)}, u32[]{:S(2)}) %all-to-all-start) | async-done | bytes 1966112 | tf_op jit(solution)/shard_map/all_to_all | solution.py:339
  37.0 6.5 %all-to-all-start.1 = ((bf16[16,30,2048]{2,1,0:T(8,128)(2,1)}), bf16[16,30,2048]{2,1,0:T(8,128)(2,1)}, u32[]{:S(2)}, u32[]{:S(2)}) async-start(bf16[16,30,2048]{2,1,0:T(8,128)(2,1)} %shard_map.120), calls=%async_computation.1 | async-start | bytes 4194304 | tf_op jit(solution)/shard_map/all_to_all | solution.py:341
  43.6 0.0 copy-done.1
  43.6 5.9 %shard_map.119 = (bf16[32,30,1024]{2,1,0:T(8,128)(2,1)}, bf16[512,2048]{1,0:T(8,128)(2,1)}, f32[512,176]{1,0:T(8,128)}, f32[512,176]{1,0:T(8,128)}, bf16[512,176]{1,0:T(8,128)(2,1)}) custom-call(s32[1]{0:T(128)} %bitcast.1.where, s32[6,1024]{1,0:T(8,128)S(1)} %bitcast.17, f32[6,1024]{1,0:T(8,128)S(1)} %bitcast.18, ...), custom_call_target="tpu_custom_call" | custom-call | tf_op jit(solution)/shard_map/pallas_call | solution.py:103
  49.4 19.3 %all-to-all-done.1.refs_0_ = bf16[16,30,2048]{2,1,0:T(8,128)(2,1)} async-done(((bf16[16,30,2048]{2,1,0:T(8,128)(2,1)}), bf16[16,30,2048]{2,1,0:T(8,128)(2,1)}, u32[]{:S(2)}, u32[]{:S(2)}) %all-to-all-start.1) | async-done | bytes 1966112 | tf_op jit(solution)/shard_map/all_to_all | solution.py:341
  68.7 10.3 %all-to-all-start.3 = ((bf16[32,30,1024]{2,1,0:T(8,128)(2,1)}), bf16[32,30,1024]{2,1,0:T(8,128)(2,1)S(1)}, u32[]{:S(2)}, u32[]{:S(2)}) async-start(bf16[32,30,1024]{2,1,0:T(8,128)(2,1)} %get-tuple-element.52), calls=%async_computation.3 | async-start | bytes 4194304 | tf_op jit(solution)/shard_map/all_to_all | solution.py:364
  79.0 7.2 %shard_map.121 = (bf16[32,30,1024]{2,1,0:T(8,128)(2,1)}, bf16[512,2048]{1,0:T(8,128)(2,1)}, bf16[512,176]{1,0:T(8,128)(2,1)}, bf16[512,176]{1,0:T(8,128)(2,1)}) custom-call(s32[1]{0:T(128)} %bitcast.1.where, bf16[16,30,2048]{2,1,0:T(8,128)(2,1)} %all-to-all-done.1.refs_0_, bf16[176,2048]{1,0:T(8,128)(2,1)} %bitcast.20, ...), custom_call_target="tpu_custom_call" | custom-call | tf_op jit(solution)/shard_map/pallas_call | solution.py:103
  86.2 4.9 %shard_map.122 = (bf16[176,2048]{1,0:T(8,128)(2,1)}, bf16[176,2048]{1,0:T(8,128)(2,1)}, bf16[176,2048]{1,0:T(8,128)(2,1)}) custom-call(s32[1]{0:T(128)} %bitcast.1.where, bf16[512,2048]{1,0:T(8,128)(2,1)} %get-tuple-element.38.refs_0_, bf16[512,2048]{1,0:T(8,128)(2,1)} %get-tuple-element.43.refs_1_, bf16[512,176]{1,0:T(8,128)(2,1)} %get-tuple-element.44.refs_2_, ...), custom_call_target="tpu_custom_call" | custom-call | tf_op jit(solution)/shard_map/pallas_call | solution.py:103
  91.1 16.2 %all-to-all-done.3.refs_0_ = bf16[32,30,1024]{2,1,0:T(8,128)(2,1)S(1)} async-done(((bf16[32,30,1024]{2,1,0:T(8,128)(2,1)}), bf16[32,30,1024]{2,1,0:T(8,128)(2,1)S(1)}, u32[]{:S(2)}, u32[]{:S(2)}) %all-to-all-start.3) | async-done | bytes 1966112 | tf_op jit(solution)/shard_map/all_to_all | solution.py:364
  107.3 5.2 %all-to-all-start.2 = ((bf16[32,30,1024]{2,1,0:T(8,128)(2,1)}), bf16[32,30,1024]{2,1,0:T(8,128)(2,1)}, u32[]{:S(2)}, u32[]{:S(2)}) async-start(bf16[32,30,1024]{2,1,0:T(8,128)(2,1)} %get-tuple-element.51), calls=%async_computation.2 | async-start | bytes 4194304 | tf_op jit(solution)/shard_map/all_to_all | solution.py:395
  112.5 0.1 pad_add_fusion.where
  112.6 0.2 copy.13
  112.8 0.2 copy.14
  113.1 2.4 %shard_map.123 = (f32[64,1024]{1,0:T(8,128)S(1)}, f32[64,128]{1,0:T(8,128)S(1)}, bf16[64,128]{1,0:T(8,128)(2,1)S(1)}) custom-call(s32[2]{0:T(128)S(1)} %pad_add_fusion.where, bf16[32,30,1024]{2,1,0:T(8,128)(2,1)S(1)} %all-to-all-done.3.refs_0_, s32[64,6]{1,0:T(8,128)S(1)} %constant_dynamic-slice_fusion.1.refs_1_, ...), custom_call_target="tpu_custom_call" | custom-call | tf_op jit(solution)/shard_map/pallas_call | solution.py:103
  115.5 25.4 %all-to-all-done.2.refs_0_ = bf16[32,30,1024]{2,1,0:T(8,128)(2,1)} async-done(((bf16[32,30,1024]{2,1,0:T(8,128)(2,1)}), bf16[32,30,1024]{2,1,0:T(8,128)(2,1)}, u32[]{:S(2)}, u32[]{:S(2)}) %all-to-all-start.2) | async-done | bytes 1966112 | tf_op jit(solution)/shard_map/all_to_all | solution.py:395
  140.9 2.1 %shard_map.124 = bf16[16,8,1152]{2,1,0:T(8,128)(2,1)S(1)} custom-call(s32[1]{0:T(128)} %bitcast.where, bf16[32,30,1024]{2,1,0:T(8,128)(2,1)} %all-to-all-done.2.refs_0_, bf16[64,128]{1,0:T(8,128)(2,1)S(1)} %get-tuple-element.55.refs_1_, f32[64,1024]{1,0:T(8,128)S(1)} %get-tuple-element.56.refs_2_, f32[64,128]{1,0:T(8,128)S(1)} %get-tuple-element.57.refs_3_), custom_call_target="tpu_custom_call" | custom-call | tf_op jit(solution)/shard_map/pallas_call | solution.py:103
  143.1 28.6 %all_to_all.30.refs_0_ = bf16[16,8,1152]{2,1,0:T(8,128)(2,1)S(1)} all-to-all(bf16[16,8,1152]{2,1,0:T(8,128)(2,1)S(1)} %shard_map.124), channel_id=1, replica_groups=mesh['x'=4,'y'=4,'z'=16,'core'=2] {'z'}, dimensions={0} | all-to-all | bytes 589824 | tf_op jit(solution)/shard_map/all_to_all | solution.py:420
  171.7 0.1 shard_map.125
  171.8 25.4 %all_to_all.31.refs_0_ = bf16[16,8,1152]{2,1,0:T(8,128)(2,1)S(1)} all-to-all(bf16[16,8,1152]{2,1,0:T(8,128)(2,1)S(1)} %shard_map.125), channel_id=1, replica_groups=mesh['x'=4,'y'=4,'z'=16,'core'=2] {'z'}, dimensions={0} | all-to-all | bytes 589824 | tf_op jit(solution)/shard_map/all_to_all | solution.py:424
  197.2 8.4 %collective-permute-start = (bf16[16,8,1152]{2,1,0:T(8,128)(2,1)S(1)}, bf16[16,8,1152]{2,1,0:T(8,128)(2,1)S(1)}, u32[]{:S(2)}, u32[]{:S(2)}) collective-permute-start(bf16[16,8,1152]{2,1,0:T(8,128)(2,1)S(1)} %all_to_all.31.refs_0_), channel_id=1, source_target_pairs={{0,1},{1,0},{2,3},{3,2},{4,5},{5,4},{6,7},{7,6},{8,9},{9,8},{10,11... | collective-permute-start | bytes 884744 | tf_op jit(solution)/shard_map/ppermute | solution.py:425
  205.7 1.2 collective-permute-done.refs_1_
  206.9 0.8 shard_map.126
  (2 shorter events, 0.0 us)
Async XLA Ops:
  4.1 7.6 %copy-start = (s32[1024,6]{0,1:T(8,128)S(1)}, s32[1024,6]{0,1:T(8,128)}, u32[]{:S(2)}) copy-start(s32[1024,6]{0,1:T(8,128)} %param.9) | copy-start | bytes 73732
  4.1 32.9 %all-to-all-start = ((bf16[16,30,2048]{2,1,0:T(8,128)(2,1)}), bf16[16,30,2048]{2,1,0:T(8,128)(2,1)S(1)}, u32[]{:S(2)}, u32[]{:S(2)}) async-start(bf16[16,30,2048]{2,1,0:T(8,128)(2,1)} %shard_map.118), calls=%async_computation | async-start | bytes 4194304 | tf_op jit(solution)/shard_map/all_to_all | solution.py:339
  14.4 29.1 %copy-start.1 = (f32[1024,6]{0,1:T(8,128)S(1)}, f32[1024,6]{0,1:T(8,128)}, u32[]{:S(2)}) copy-start(f32[1024,6]{0,1:T(8,128)} %param.10) | copy-start | bytes 73732
  37.0 31.7 %all-to-all-start.1 = ((bf16[16,30,2048]{2,1,0:T(8,128)(2,1)}), bf16[16,30,2048]{2,1,0:T(8,128)(2,1)}, u32[]{:S(2)}, u32[]{:S(2)}) async-start(bf16[16,30,2048]{2,1,0:T(8,128)(2,1)} %shard_map.120), calls=%async_computation.1 | async-start | bytes 4194304 | tf_op jit(solution)/shard_map/all_to_all | solution.py:341
  68.7 38.6 %all-to-all-start.3 = ((bf16[32,30,1024]{2,1,0:T(8,128)(2,1)}), bf16[32,30,1024]{2,1,0:T(8,128)(2,1)S(1)}, u32[]{:S(2)}, u32[]{:S(2)}) async-start(bf16[32,30,1024]{2,1,0:T(8,128)(2,1)} %get-tuple-element.52), calls=%async_computation.3 | async-start | bytes 4194304 | tf_op jit(solution)/shard_map/all_to_all | solution.py:364
  107.3 33.6 %all-to-all-start.2 = ((bf16[32,30,1024]{2,1,0:T(8,128)(2,1)}), bf16[32,30,1024]{2,1,0:T(8,128)(2,1)}, u32[]{:S(2)}, u32[]{:S(2)}) async-start(bf16[32,30,1024]{2,1,0:T(8,128)(2,1)} %get-tuple-element.51), calls=%async_computation.2 | async-start | bytes 4194304 | tf_op jit(solution)/shard_map/all_to_all | solution.py:395
  197.2 9.6 %collective-permute-start = (bf16[16,8,1152]{2,1,0:T(8,128)(2,1)S(1)}, bf16[16,8,1152]{2,1,0:T(8,128)(2,1)S(1)}, u32[]{:S(2)}, u32[]{:S(2)}) collective-permute-start(bf16[16,8,1152]{2,1,0:T(8,128)(2,1)S(1)} %all_to_all.31.refs_0_), channel_id=1, source_target_pairs={{0,1},{1,0},{2,3},{3,2},{4,5},{5,4},{6,7},{7,6},{8,9},{9,8},{10,11... | collective-permute-start | bytes 884744 | tf_op jit(solution)/shard_map/ppermute | solution.py:425

commit v4 on v3

--- a/solution.py
+++ b/solution.py
@@ -31,13 +31,14 @@
     return high, (value - high.astype(F32)).astype(BF)
 
 
-def slot_rows_of(ids, expert, slot):
+def slot_rows_of(ids, expert, slot, block):
     count = ids.shape[1]
     hit = ids[0:1, :] == expert
     for k in range(1, ids.shape[0]):
         hit = jnp.logical_or(hit, ids[k : k + 1, :] == expert)
     flag = hit.astype(F32)
-    earlier = (iota((count, count), 0) < iota((count, count), 1)).astype(BF)
+    before, after = iota((count, count), 0), iota((count, count), 1)
+    earlier = jnp.logical_and(before < after, before // block == after // block).astype(BF)
     return jnp.where(dot(flag.astype(BF), earlier) == slot.astype(F32), flag, 0.0)
 
 
@@ -53,6 +54,13 @@
 
 VMEM = pl.BlockSpec(memory_space=pltpu.VMEM)
 HBM = pl.BlockSpec(memory_space=pltpu.HBM)
+
+
+def begin(pairs, sems):
+    copies = [pltpu.make_async_copy(a, b, sems.at[i]) for i, (a, b) in enumerate(pairs)]
+    for copy in copies:
+        copy.start()
+    return copies
 
 
 def call(kernel, outs, scalars, arrays, scratch=(), vmem=8):
@@ -120,7 +128,7 @@
 
 def send_kernel(where, ready, done, ids, tokens, out):
     spot = iota((EXP_DEV * ROWS, 1), 0)
-    pick = slot_rows_of(ids[...], where[0] + spot // ROWS, spot % ROWS).astype(BF)
+    pick = slot_rows_of(ids[...], where[0] + spot // ROWS, spot % ROWS, ids.shape[1]).astype(BF)
     ready(1)
     picked = dot(pick, tokens[...]).astype(BF)
     per_expert = out.shape[0] // EXP_DEV
@@ -129,46 +137,94 @@
         out[d] = picked[first : first + SLOTS]
 
 
-def weights_of_slots(expert, ids, weight):
+def weights_of_slots(expert, ids, weight, block):
     slot = iota((ROWS, 1), 0)
-    pick = slot_rows_of(ids, jnp.full((ROWS, 1), expert, jnp.int32), slot)
+    pick = slot_rows_of(ids, jnp.full((ROWS, 1), expert, jnp.int32), slot, block)
     scale = jnp.zeros((1, ids.shape[1]), F32)
     for k in range(ids.shape[0]):
         scale = scale + jnp.where(ids[k : k + 1, :] == expert, weight[k : k + 1, :], 0.0)
-    return jnp.sum(pick * scale, axis=1, keepdims=True)
+    scale = pick * scale
+    owner = iota(scale.shape, 1) // block
+    return [
+        jnp.sum(jnp.where(owner == j, scale, 0.0), axis=1, keepdims=True)
+        for j in range(ids.shape[1] // block)
+    ]
+
+
+def prepare_kernel(where, ids, rows, all_ids, all_weight, *refs):
+    out, scale, rows_v, ids_v, weight_v, picked, scale_v = refs[-7:]
+
+    @pl.when(where[1] == where[2])
+    def _():
+        pltpu.sync_copy(rows, rows_v)
+        send_kernel(where, lambda _: None, None, ids, rows_v, picked)
+        pltpu.sync_copy(picked, out)
+        pltpu.sync_copy(all_ids, ids_v)
+        pltpu.sync_copy(all_weight, weight_v)
+        block = ids.shape[1]
+        per_step = LANES // block
+
+        def some_blocks(i, carry):
+            cols = pl.ds(pl.multiple_of(i * LANES, LANES), LANES)
+            parts = weights_of_slots(where[3], ids_v[:, cols], weight_v[:, cols], block)
+            for j, part in enumerate(parts):
+                first = pl.multiple_of((i * per_step + j) * ROWS, ROWS)
+                scale_v[pl.ds(first, ROWS), :] = part
+            return carry
+
+        lax.fori_loop(0, all_ids.shape[1] // LANES, some_blocks, 0)
+        pltpu.sync_copy(scale_v, scale)
+
+
+def prepare(turn, core, experts, ids, rows, all_ids, all_weight, shapes, before=()):
+    arrays = [
+        pltpu.with_memory_space_constraint(array, pltpu.HBM)
+        for array in (rows, all_ids, all_weight, *before)
+    ]
+    (out, out_kind), (scale, scale_kind) = shapes
+    return pl.pallas_call(
+        prepare_kernel,
+        out_shape=[pltpu.HBM(out, out_kind), pltpu.HBM(scale, scale_kind)],
+        in_specs=[pl.BlockSpec(memory_space=pltpu.SMEM), VMEM] + [HBM] * len(arrays),
+        out_specs=[HBM, HBM],
+        input_output_aliases={5: 0, 6: 1} if before else {},
+        scratch_shapes=[
+            pltpu.VMEM(rows.shape, rows.dtype),
+            pltpu.VMEM(all_ids.shape, all_ids.dtype),
+            pltpu.VMEM(all_weight.shape, all_weight.dtype),
+            pltpu.VMEM(out, out_kind),
+            pltpu.VMEM(scale, scale_kind),
+        ],
+        compiler_params=pltpu.CompilerParams(vmem_limit_bytes=8 << 20),
+    )(jnp.stack([experts[0], core, jnp.int32(turn), experts[1]]).astype(jnp.int32), ids, *arrays)
 
 
 def forward_kernel(
-    where, ready, done, ids, weight, rows_in, gate_w, up_w, down_w,
+    where, ready, done, scale, rows_in, gate_w, up_w, down_w,
     out, x, gate_factor, up_factor, hidden
 ):
     blocks = rows_in.shape[0]
-    block = ids.shape[1] // blocks
-    half = out.shape[2]
+    half = out.shape[2] // CORES
     for b in range(blocks):
         x[b * ROWS : (b + 1) * ROWS, :] = padded(rows_in[b]).astype(BF)
     done(1)
-    ready(3, 4)
+    ready(2, 3)
     g = dot(x[...], gate_w[...], 1, 1)
     u = dot(x[...], up_w[...], 1, 1)
     sig = jax.nn.sigmoid(g)
     act = g * sig
     h = (act * u).astype(BF)
-    ready(5)
+    ready(4)
     for c in range(CORES):
-        piece = dot(h, down_w[:, c * half : (c + 1) * half]).astype(BF)
+        cols = slice(c * half, (c + 1) * half)
+        piece = dot(h, down_w[:, cols]).astype(BF)
         for d in range(blocks):
-            out[CORES * d + c] = piece[d * ROWS : d * ROWS + SLOTS]
+            out[d, :, cols] = piece[d * ROWS : d * ROWS + SLOTS]
     done(0)
-    gate_factor[...] = u * sig * (1.0 + g * (1.0 - sig))
-    up_factor[...] = act
-    hidden[...] = h
-    for b in range(blocks):
-        cols, rows = slice(b * block, (b + 1) * block), slice(b * ROWS, (b + 1) * ROWS)
-        scale = weights_of_slots(where[0], ids[:, cols], weight[:, cols])
-        gate_factor[rows, :] = gate_factor[rows, :] * scale
-        up_factor[rows, :] = up_factor[rows, :] * scale
-        hidden[rows, :] = (hidden[rows, :].astype(F32) * scale).astype(BF)
+    ready(0)
+    gate_factor[...] = u * sig * (1.0 + g * (1.0 - sig)) * scale[...]
+    up_factor[...] = act * scale[...]
+    hidden[...] = (h.astype(F32) * scale[...]).astype(BF)
 
 
 def backward_kernel(
@@ -176,7 +232,7 @@
     out, rows, d_gate, d_up
 ):
     blocks = rows_grad.shape[0]
-    half = out.shape[2]
+    half = out.shape[2] // CORES
     ready(0)
     for b in range(blocks):
         rows[b * ROWS : (b + 1) * ROWS, :] = padded(rows_grad[b]).astype(BF)
@@ -190,7 +246,7 @@
         cols = slice(c * half, (c + 1) * half)
         piece = (dot(dg, gate_w[:, cols]) + dot(du, up_w[:, cols])).astype(BF)
         for d in range(blocks):
-            out[CORES * d + c] = piece[d * ROWS : d * ROWS + SLOTS]
+            out[d, :, cols] = piece[d * ROWS : d * ROWS + SLOTS]
     done(0)
     d_gate[...] = dg
     d_up[...] = du
@@ -211,28 +267,30 @@
 
 def gathered(returned, total):
     sources = returned.shape[0]
-    pieces = sources // CORES // EXP_DEV
+    pieces = sources // EXP_DEV
     for j in range(EXP_DEV):
-        for c in range(CORES):
-            part = None
-            for d in range(j * pieces, (j + 1) * pieces):
-                block = returned[CORES * d + c].astype(F32)
-                part = block if part is None else part + block
-            first = (CORES * j + c) * ROWS
-            total[first : first + ROWS, :] = padded(part)
+        part = None
+        for d in range(j * pieces, (j + 1) * pieces):
+            block = returned[d].astype(F32)
+            part = block if part is None else part + block
+        total[j * ROWS : (j + 1) * ROWS, :] = padded(part)
     return split(total[...])
 
 
+def shared(core, full, keep, give):
+    half = keep.shape[1]
+    keep[...] = full[:, pl.ds(pl.multiple_of(core * half, LANES), half)]
+    give[...] = full[:, pl.ds(pl.multiple_of((1 - core) * half, LANES), half)].astype(BF)
+
+
 def combine_kernel(
-    where, ready, done, returned, ids, weight, d_mixed, mixed, route, place, total
+    where, ready, done, returned, ids, weight, d_mixed, keep, give, route, place, total, full
 ):
     first_expert, core = where[0], where[1]
     rows = ids.shape[0]
-    half = returned.shape[2]
     count = total.shape[0]
     lane = iota((rows, count), 1)
-    source = lane // ROWS
-    expert = first_expert + (source % CORES) * EXP_DEV + source // CORES
+    expert = first_expert + lane // ROWS
     all_ids = ids[...]
     pick = rows_of_slots(all_ids, expert, lane % ROWS)
     place[...] = pick.astype(BF)
@@ -242,10 +300,11 @@
     high, low = split(pick * scale)
     ready(0)
     back, rest = gathered(returned, total)
-    mixed[...] = dot(high, back) + (dot(low, back) + dot(high, rest))
+    full[...] = dot(high, back) + (dot(low, back) + dot(high, rest))
+    shared(core, full, keep, give)
     ready(3)
-    own_grad = d_mixed[:, pl.ds(pl.multiple_of(core * half, LANES), half)]
-    paired = (dot(own_grad, back, 1, 1) + dot(own_grad, rest, 1, 1)) * pick
+    grad = d_mixed[...]
+    paired = (dot(grad, back, 1, 1) + dot(grad, rest, 1, 1)) * pick
     spot = iota((rows, LANES), 1)
     result = jnp.zeros((rows, LANES), F32)
     for k in range(ids.shape[1]):
@@ -254,19 +313,24 @@
     route[...] = result
 
 
-def pack_kernel(where, ready, done, returned, place, mixed, route, out, total):
-    half = returned.shape[2]
-    high, low = split(route[...])
+def tokens_kernel(where, ready, done, returned, place, keep, give, total, full):
+    back, rest = gathered(returned, total)
+    full[...] = dot(place[...], back) + dot(place[...], rest)
+    shared(where[0], full, keep, give)
+
+
+def pack_kernel(
+    where, ready, done, mixed, mixed_other, route, d_tokens, d_tokens_other, out
+):
+    half = mixed.shape[1]
+    high, low = [part.astype(F32) for part in split(route[...])]
+    sums = [mixed[...] + mixed_other[...].astype(F32)]
+    sums.append(d_tokens[...] + d_tokens_other[...].astype(F32))
     for i in range(out.shape[0] // 2):
         rows = slice(8 * i, 8 * i + 8)
-        out[2 * i, :, :half] = mixed[rows, :].astype(BF)
-        out[2 * i, :, half:] = high.astype(F32)[rows].astype(BF)
-        out[2 * i + 1, :, half:] = low.astype(F32)[rows].astype(BF)
-    ready(0)
-    back, rest = gathered(returned, total)
-    sums = dot(place[...], back) + dot(place[...], rest)
-    for i in range(out.shape[0] // 2):
-        out[2 * i + 1, :, :half] = sums[8 * i : 8 * i + 8].astype(BF)
+        for j, tail in enumerate((high, low)):
+            out[2 * i + j, :, :half] = sums[j][rows].astype(BF)
+            out[2 * i + j, :, half:] = tail[rows].astype(BF)
 
 
 def total_kernel(where, ready, done, parts, out):
@@ -315,12 +379,12 @@
     half = width // CORES
     hidden_count = gate_weight.shape[1]
     rows = dp_count * ROWS
-    chip_expert = z_index * CORES * EXP_DEV
-    column_expert = chip_expert + core * EXP_DEV
+    column_expert = (z_index * CORES + core) * EXP_DEV
     expert = column_expert + dp_index // (dp_count // EXP_DEV)
     gate_piece, up_piece, down_piece = gate_weight[0], up_weight[0], down_weight[0]
-    out_shape = (CORES * dp_count, SLOTS, half)
-    gathered_v = pltpu.VMEM((CORES * EXP_DEV * ROWS, half), F32)
+    out_shape = (dp_count, SLOTS, width)
+    gathered_v = pltpu.VMEM((EXP_DEV * ROWS, width), F32)
+    full_v = pltpu.VMEM((row_count, width), F32)
 
     def own_rows(array):
         return lax.dynamic_slice_in_dim(array, dp_index * row_count, row_count, 0)
@@ -334,10 +398,19 @@
         )
         return sent
 
-    sent = send(tokens, own_rows(route_ids).T)
-    sent, route_ids, route_weight = lax.optimization_barrier((sent, route_ids, route_weight))
+    ids, all_ids, all_weight = own_rows(route_ids).T, route_ids.T, route_weight.T
+    shapes = [((dp_count, SLOTS, width), BF), ((rows, 1), F32)]
+    experts = (column_expert, expert)
+    prepared = prepare(0, core, experts, ids, d_mixed, all_ids, all_weight, shapes)
+    *prepared, first_ids = lax.optimization_barrier((*prepared, ids))
+    sent = send(tokens, first_ids)
+    sent, ids, route_ids, route_weight = lax.optimization_barrier(
+        (sent, ids, route_ids, route_weight)
+    )
     rows_in = lax.all_to_all(sent, ("x", "y"), 0, 0, tiled=True)
-    sent_grad = send(d_mixed, own_rows(route_ids).T)
+    sent_grad, scale = prepare(
+        1, core, experts, ids, d_mixed, all_ids, all_weight, shapes, prepared
+    )
     rows_grad = lax.all_to_all(sent_grad, ("x", "y"), 0, 0, tiled=True)
 
     out, x, gate_factor, up_factor, hidden = call(
@@ -351,8 +424,7 @@
         ],
         [expert],
         [
-            (route_ids.T, VMEM),
-            (route_weight.T, VMEM),
+            (scale, HBM),
             (rows_in, VMEM),
             (gate_piece, HBM),
             (up_piece, HBM),
@@ -361,7 +433,7 @@
         vmem=24,
     )
     out, rows_grad = lax.optimization_barrier((out, rows_grad))
-    returned = lax.all_to_all(out, ("x", "y", "core"), 0, 0, tiled=True)
+    returned = lax.all_to_all(out, ("x", "y"), 0, 0, tiled=True)
 
     out_in, padded_grad, d_gate, d_up = call(
         backward_kernel,
@@ -392,37 +464,53 @@
     grad_gate, grad_up, grad_down, out_in, route_ids, route_weight = lax.optimization_barrier(
         (*grads, out_in, route_ids, route_weight)
     )
-    returned_in = lax.all_to_all(out_in, ("x", "y", "core"), 0, 0, tiled=True)
-    mixed_part, route_part, own_place = call(
+    returned_in = lax.all_to_all(out_in, ("x", "y"), 0, 0, tiled=True)
+    swap = [(0, 1), (1, 0)]
+    shares = [((row_count, half), F32, VMEM), ((row_count, half), BF, VMEM)]
+    mixed_part, mixed_give, route_part, own_place = call(
         combine_kernel,
         [
-            ((row_count, half), F32, VMEM),
+            *shares,
             ((row_count, LANES), F32, VMEM),
-            ((row_count, CORES * EXP_DEV * ROWS), BF, VMEM),
-        ],
-        [chip_expert, core],
+            ((row_count, EXP_DEV * ROWS), BF, VMEM),
+        ],
+        [column_expert, core],
         [
             (returned, VMEM),
             (own_rows(route_ids), VMEM),
             (own_rows(route_weight), VMEM),
             (d_mixed, HBM),
         ],
-        [gathered_v],
+        [gathered_v, full_v],
         vmem=16,
     )
+    mixed_other = lax.ppermute(mixed_give, "core", swap)
+    tokens_part, tokens_give = call(
+        tokens_kernel,
+        shares,
+        [core],
+        [(returned_in, VMEM), (own_place, VMEM)],
+        [gathered_v, full_v],
+    )
+    tokens_other = lax.ppermute(tokens_give, "core", swap)
     (packed,) = call(
         pack_kernel,
         [((z_count, 8, half + LANES), BF, VMEM)],
         [core],
-        [(returned_in, VMEM), (own_place, VMEM), (mixed_part, VMEM), (route_part, VMEM)],
-        [gathered_v],
+        [
+            (mixed_part, VMEM),
+            (mixed_other, VMEM),
+            (route_part, VMEM),
+            (tokens_part, VMEM),
+            (tokens_other, VMEM),
+        ],
     )
     parts = lax.all_to_all(packed, "z", 0, 0, tiled=True)
     (summed,) = call(
         total_kernel, [((z_count, 8, half + LANES), BF, VMEM)], [core], [(parts, VMEM)]
     )
     whole = lax.all_to_all(summed, "z", 0, 0, tiled=True)
-    other = lax.ppermute(whole, "core", [(0, 1), (1, 0)])
+    other = lax.ppermute(whole, "core", swap)
     mixed, d_tokens, d_route = call(
         finish_kernel,
         [

time: 208 us -> 189 us (0.909)
  waiting for transfers between devices: 84.7 us -> 34.1 us
  starting transfers between devices: 38.1 us -> 61.1 us
  Pallas kernels: 28.6 us -> 34.1 us
    all_to_all x2, waiting for transfers between devices: 41.7 us -> 8.41 us  [the longest x1 5.49 us: body(): returned = lax.all_to_all(out, ('x', 'y'), 0, 0, tiled=True)]
    ppermute x1 -> x3, starting transfers between devices: 8.45 us -> 31.8 us  [the longest x1 12.7 us: body(): tokens_other = lax.ppermute(tokens_give, 'core', swap)]
    all_to_all x1, waiting for transfers between devices: 22.6 us -> 11.3 us  [body(): rows_in = lax.all_to_all(sent, ('x', 'y'), 0, 0, tiled=True)]
    pallas_call x0 -> x2, Pallas kernels: none -> 7.72 us  [prepare(): pl.pallas_call(prepare_kernel, out_shape=[pltpu.HBM(out, out_kind), pltpu...]
    all_to_all x1, waiting for transfers between devices: 19.3 us -> 12.3 us  [body(): rows_grad = lax.all_to_all(sent_grad, ('x', 'y'), 0, 0, tiled=True)]
    pallas_call x9, Pallas kernels: 28.6 us -> 26.4 us  [call(): pl.pallas_call(wrapped, out_shape=[result(*out) for out in outs], in_spec...]
  transfers between devices with their start and end apart: 5 -> 7, of which waited for: 5 -> 6; matrix products, arithmetic and copies ran while one was open for 0% -> 1% of each run, Pallas kernels for 11% -> 16%
where the time goes in v4:
time: 189 us; the launch traced here: 188 us
  starting transfers between devices  61.1 us (32%)
  blocking collectives  54.6 us (29%)
  Pallas kernels  34.1 us (18%)
  waiting for transfers between devices  34.1 us (18%)
  local copies, waits for them, and re-layouts  2.8 us (1%)
    all_to_all x1, blocking collectives, body(): parts = lax.all_to_all(packed, 'z', 0, 0, tiled=True)  29.4 us
    pallas_call x9, Pallas kernels, call(): pl.pallas_call(wrapped, out_shape=[result(*out) for out in outs], in_spec...  26.4 us
    all_to_all x1, blocking collectives, body(): whole = lax.all_to_all(summed, 'z', 0, 0, tiled=True)  25.2 us
    ppermute x1, starting transfers between devices, body(): tokens_other = lax.ppermute(tokens_give, 'core', swap)  12.7 us
    all_to_all x1, waiting for transfers between devices, body(): rows_grad = lax.all_to_all(sent_grad, ('x', 'y'), 0, 0, tiled=True)  12.3 us
    all_to_all x1, waiting for transfers between devices, body(): rows_in = lax.all_to_all(sent, ('x', 'y'), 0, 0, tiled=True)  11.3 us
    ppermute x1, starting transfers between devices, body(): mixed_other = lax.ppermute(mixed_give, 'core', swap)  11 us
    all_to_all x1, starting transfers between devices, body(): returned_in = lax.all_to_all(out_in, ('x', 'y'), 0, 0, tiled=True)  8.42 us
  transfers between devices with their start and end apart: 7, of which 6 were waited for; matrix products, arithmetic and copies ran while one was open for 1% of the time, Pallas kernels for 16%

profile of v4, /device:TPU:1, one launch (start us, length us, event | category | flops | bytes accessed | tf_op | source)
XLA Modules:
  0.0 187.7 jit_solution(9232350268538892024)
XLA Ops:
  0.7 0.8 dynamic-slice_bitcast_fusion.ids.refs_0_
  1.4 0.1 add_add_fusion
  1.5 0.5 shard_map.118
  2.1 2.6 %shard_map.119 = bf16[16,30,2048]{2,1,0:T(8,128)(2,1)} custom-call(s32[1]{0:T(128)} %bitcast.1.where, s32[6,64]{1,0:T(8,128)S(1)} %dynamic-slice_bitcast_fusion.ids.refs_0_, bf16[64,2048]{1,0:T(8,128)(2,1)} %refs_1_.1), custom_call_target="tpu_custom_call" | custom-call | tf_op jit(solution)/shard_map/pallas_call | solution.py:111
  4.7 7.6 %all-to-all-start = ((bf16[16,30,2048]{2,1,0:T(8,128)(2,1)}), bf16[16,30,2048]{2,1,0:T(8,128)(2,1)S(1)}, u32[]{:S(2)}, u32[]{:S(2)}) async-start(bf16[16,30,2048]{2,1,0:T(8,128)(2,1)} %shard_map.119), calls=%async_computation | async-start | bytes 4194304 | tf_op jit(solution)/shard_map/all_to_all | solution.py:410
  12.3 7.2 %shard_map.120 = (bf16[16,30,2048]{2,1,0:T(8,128)(2,1)}, f32[512,1]{1,0:T(8,128)}) custom-call(s32[4]{0:T(128)S(1)} %get-tuple-element.86.where, s32[6,64]{1,0:T(8,128)S(1)} %dynamic-slice_bitcast_fusion.ids.refs_0_, bf16[64,2048]{1,0:T(8,128)(2,1)} %refs_3_.1, s32[6,1024]{1,0:T(8,128)} %bitcast.21, ...), custom_call_target="tpu_custom_call", output_to_operand_aliasing={{0}: (5, {}), {1}: (6, {})} | custom-call | tf_op jit(solution)/shard_map/pallas_call | solution.py:185
  19.5 11.3 %all-to-all-done.refs_1_ = bf16[16,30,2048]{2,1,0:T(8,128)(2,1)S(1)} async-done(((bf16[16,30,2048]{2,1,0:T(8,128)(2,1)}), bf16[16,30,2048]{2,1,0:T(8,128)(2,1)S(1)}, u32[]{:S(2)}, u32[]{:S(2)}) %all-to-all-start) | async-done | bytes 1966112 | tf_op jit(solution)/shard_map/all_to_all | solution.py:410
  30.7 6.9 %all-to-all-start.1 = ((bf16[16,30,2048]{2,1,0:T(8,128)(2,1)}), bf16[16,30,2048]{2,1,0:T(8,128)(2,1)}, u32[]{:S(2)}, u32[]{:S(2)}) async-start(bf16[16,30,2048]{2,1,0:T(8,128)(2,1)} %get-tuple-element.55), calls=%async_computation.1 | async-start | bytes 4194304 | tf_op jit(solution)/shard_map/all_to_all | solution.py:414
  37.7 6.0 %shard_map.121 = (bf16[16,30,2048]{2,1,0:T(8,128)(2,1)}, bf16[512,2048]{1,0:T(8,128)(2,1)}, f32[512,176]{1,0:T(8,128)}, f32[512,176]{1,0:T(8,128)}, bf16[512,176]{1,0:T(8,128)(2,1)}) custom-call(s32[1]{0:T(128)} %bitcast.2.where, f32[512,1]{1,0:T(8,128)} %get-tuple-element.52.refs_0_, bf16[16,30,2048]{2,1,0:T(8,128)(2,1)S(1)} %all-to-all-done.refs_1_, ...), custom_call_target="tpu_custom_call" | custom-call | tf_op jit(solution)/shard_map/pallas_call | solution.py:111
  43.6 12.3 %all-to-all-done.1.refs_0_ = bf16[16,30,2048]{2,1,0:T(8,128)(2,1)} async-done(((bf16[16,30,2048]{2,1,0:T(8,128)(2,1)}), bf16[16,30,2048]{2,1,0:T(8,128)(2,1)}, u32[]{:S(2)}, u32[]{:S(2)}) %all-to-all-start.1) | async-done | bytes 1966112 | tf_op jit(solution)/shard_map/all_to_all | solution.py:414
  56.0 6.4 %all-to-all-start.2 = ((bf16[16,30,2048]{2,1,0:T(8,128)(2,1)}), bf16[16,30,2048]{2,1,0:T(8,128)(2,1)S(1)}, u32[]{:S(2)}, u32[]{:S(2)}) async-start(bf16[16,30,2048]{2,1,0:T(8,128)(2,1)} %get-tuple-element.56), calls=%async_computation.2 | async-start | bytes 4194304 | tf_op jit(solution)/shard_map/all_to_all | solution.py:436
  62.3 7.1 %shard_map.122 = (bf16[16,30,2048]{2,1,0:T(8,128)(2,1)}, bf16[512,2048]{1,0:T(8,128)(2,1)}, bf16[512,176]{1,0:T(8,128)(2,1)}, bf16[512,176]{1,0:T(8,128)(2,1)}) custom-call(s32[1]{0:T(128)} %bitcast.2.where, bf16[16,30,2048]{2,1,0:T(8,128)(2,1)} %all-to-all-done.1.refs_0_, bf16[176,2048]{1,0:T(8,128)(2,1)} %bitcast.19, ...), custom_call_target="tpu_custom_call" | custom-call | tf_op jit(solution)/shard_map/pallas_call | solution.py:111
  69.5 4.9 %shard_map.123 = (bf16[176,2048]{1,0:T(8,128)(2,1)}, bf16[176,2048]{1,0:T(8,128)(2,1)}, bf16[176,2048]{1,0:T(8,128)(2,1)}) custom-call(s32[1]{0:T(128)} %bitcast.2.where, bf16[512,2048]{1,0:T(8,128)(2,1)} %get-tuple-element.57.refs_0_, bf16[512,2048]{1,0:T(8,128)(2,1)} %get-tuple-element.61.refs_1_, bf16[512,176]{1,0:T(8,128)(2,1)} %get-tuple-element.62.refs_2_, ...), custom_call_target="tpu_custom_call" | custom-call | tf_op jit(solution)/shard_map/pallas_call | solution.py:111
  74.5 5.5 %all-to-all-done.2.refs_0_ = bf16[16,30,2048]{2,1,0:T(8,128)(2,1)S(1)} async-done(((bf16[16,30,2048]{2,1,0:T(8,128)(2,1)}), bf16[16,30,2048]{2,1,0:T(8,128)(2,1)S(1)}, u32[]{:S(2)}, u32[]{:S(2)}) %all-to-all-start.2) | async-done | bytes 1966112 | tf_op jit(solution)/shard_map/all_to_all | solution.py:436
  79.9 8.4 %all-to-all-start.3 = ((bf16[16,30,2048]{2,1,0:T(8,128)(2,1)}), bf16[16,30,2048]{2,1,0:T(8,128)(2,1)}, u32[]{:S(2)}, u32[]{:S(2)}) async-start(bf16[16,30,2048]{2,1,0:T(8,128)(2,1)} %get-tuple-element.76), calls=%async_computation.3 | async-start | bytes 4194304 | tf_op jit(solution)/shard_map/all_to_all | solution.py:467
  88.4 0.1 pad_add_fusion.where
  88.5 1.0 copy.15
  89.5 0.2 copy.16
  89.7 0.8 constant_dynamic-slice_fusion.1.refs_1_
  90.5 2.5 %shard_map.124 = (f32[64,1024]{1,0:T(8,128)S(1)}, bf16[64,1024]{1,0:T(8,128)(2,1)S(1)}, f32[64,128]{1,0:T(8,128)S(1)}, bf16[64,64]{1,0:T(8,128)(2,1)S(1)}) custom-call(s32[2]{0:T(128)S(1)} %pad_add_fusion.where, bf16[16,30,2048]{2,1,0:T(8,128)(2,1)S(1)} %all-to-all-done.2.refs_0_, s32[64,6]{1,0:T(8,128)S(1)} %constant_dynamic-slice_fusion.1.refs_1_, ...), custom_call_target="tpu_custom_call" | custom-call | tf_op jit(solution)/shard_map/pallas_call | solution.py:111
  93.0 11.0 %collective-permute-start = (bf16[64,1024]{1,0:T(8,128)(2,1)S(1)}, bf16[64,1024]{1,0:T(8,128)(2,1)S(1)}, u32[]{:S(2)}, u32[]{:S(2)}) collective-permute-start(bf16[64,1024]{1,0:T(8,128)(2,1)S(1)} %get-tuple-element.74), channel_id=1, source_target_pairs={{0,1},{1,0},{2,3},{3,2},{4,5},{5,4},{6,7},{7,6},{8,9},{9,8},{10,11... | collective-permute-start | bytes 393224 | tf_op jit(solution)/shard_map/ppermute | solution.py:487
  104.1 2.9 %all-to-all-done.3.refs_0_ = bf16[16,30,2048]{2,1,0:T(8,128)(2,1)} async-done(((bf16[16,30,2048]{2,1,0:T(8,128)(2,1)}), bf16[16,30,2048]{2,1,0:T(8,128)(2,1)}, u32[]{:S(2)}, u32[]{:S(2)}) %all-to-all-start.3) | async-done | bytes 1966112 | tf_op jit(solution)/shard_map/all_to_all | solution.py:467
  107.0 2.2 %shard_map.125 = (f32[64,1024]{1,0:T(8,128)S(1)}, bf16[64,1024]{1,0:T(8,128)(2,1)S(1)}) custom-call(s32[1]{0:T(128)} %bitcast.where, bf16[16,30,2048]{2,1,0:T(8,128)(2,1)} %all-to-all-done.3.refs_0_, bf16[64,64]{1,0:T(8,128)(2,1)S(1)} %get-tuple-element.77.refs_1_), custom_call_target="tpu_custom_call" | custom-call | tf_op jit(solution)/shard_map/pallas_call | solution.py:111
  109.2 12.7 %collective-permute-start.1 = (bf16[64,1024]{1,0:T(8,128)(2,1)S(1)}, bf16[64,1024]{1,0:T(8,128)(2,1)S(1)}, u32[]{:S(2)}, u32[]{:S(2)}) collective-permute-start(bf16[64,1024]{1,0:T(8,128)(2,1)S(1)} %get-tuple-element.79), channel_id=1, source_target_pairs={{0,1},{1,0},{2,3},{3,2},{4,5},{5,4},{6,7},{7,6},{8,9},{9,8},{10,11... | collective-permute-start | bytes 393224 | tf_op jit(solution)/shard_map/ppermute | solution.py:495
  122.0 1.0 collective-permute-done.1.refs_4_
  122.9 0.1 shard_map.126
  123.0 29.4 %all_to_all.30.refs_0_ = bf16[16,8,1152]{2,1,0:T(8,128)(2,1)S(1)} all-to-all(bf16[16,8,1152]{2,1,0:T(8,128)(2,1)S(1)} %shard_map.126), channel_id=1, replica_groups=mesh['x'=4,'y'=4,'z'=16,'core'=2] {'z'}, dimensions={0} | all-to-all | bytes 589824 | tf_op jit(solution)/shard_map/all_to_all | solution.py:508
  152.4 0.1 shard_map.127
  152.4 25.2 %all_to_all.31.refs_0_ = bf16[16,8,1152]{2,1,0:T(8,128)(2,1)S(1)} all-to-all(bf16[16,8,1152]{2,1,0:T(8,128)(2,1)S(1)} %shard_map.127), channel_id=1, replica_groups=mesh['x'=4,'y'=4,'z'=16,'core'=2] {'z'}, dimensions={0} | all-to-all | bytes 589824 | tf_op jit(solution)/shard_map/all_to_all | solution.py:512
  177.7 8.0 %collective-permute-start.2 = (bf16[16,8,1152]{2,1,0:T(8,128)(2,1)S(1)}, bf16[16,8,1152]{2,1,0:T(8,128)(2,1)S(1)}, u32[]{:S(2)}, u32[]{:S(2)}) collective-permute-start(bf16[16,8,1152]{2,1,0:T(8,128)(2,1)S(1)} %all_to_all.31.refs_0_), channel_id=1, source_target_pairs={{0,1},{1,0},{2,3},{3,2},{4,5},{5,4},{6,7},{7,6},{8,9},{9,8},{10,11... | collective-permute-start | bytes 884744 | tf_op jit(solution)/shard_map/ppermute | solution.py:513
  185.7 1.2 collective-permute-done.2.refs_1_
  186.9 0.8 shard_map.128
  (6 shorter events, 0.0 us)
Async XLA Ops:
  4.7 26.0 %all-to-all-start = ((bf16[16,30,2048]{2,1,0:T(8,128)(2,1)}), bf16[16,30,2048]{2,1,0:T(8,128)(2,1)S(1)}, u32[]{:S(2)}, u32[]{:S(2)}) async-start(bf16[16,30,2048]{2,1,0:T(8,128)(2,1)} %shard_map.119), calls=%async_computation | async-start | bytes 4194304 | tf_op jit(solution)/shard_map/all_to_all | solution.py:410
  30.7 25.2 %all-to-all-start.1 = ((bf16[16,30,2048]{2,1,0:T(8,128)(2,1)}), bf16[16,30,2048]{2,1,0:T(8,128)(2,1)}, u32[]{:S(2)}, u32[]{:S(2)}) async-start(bf16[16,30,2048]{2,1,0:T(8,128)(2,1)} %get-tuple-element.55), calls=%async_computation.1 | async-start | bytes 4194304 | tf_op jit(solution)/shard_map/all_to_all | solution.py:414
  56.0 24.0 %all-to-all-start.2 = ((bf16[16,30,2048]{2,1,0:T(8,128)(2,1)}), bf16[16,30,2048]{2,1,0:T(8,128)(2,1)S(1)}, u32[]{:S(2)}, u32[]{:S(2)}) async-start(bf16[16,30,2048]{2,1,0:T(8,128)(2,1)} %get-tuple-element.56), calls=%async_computation.2 | async-start | bytes 4194304 | tf_op jit(solution)/shard_map/all_to_all | solution.py:436
  74.4 14.0 %copy-start = (s32[1024,6]{0,1:T(8,128)S(1)}, s32[1024,6]{0,1:T(8,128)}, u32[]{:S(2)}) copy-start(s32[1024,6]{0,1:T(8,128)} %param.9) | copy-start | bytes 73732
  74.4 15.0 %copy-start.1 = (f32[1024,6]{0,1:T(8,128)S(1)}, f32[1024,6]{0,1:T(8,128)}, u32[]{:S(2)}) copy-start(f32[1024,6]{0,1:T(8,128)} %param.10) | copy-start | bytes 73732
  79.9 27.1 %all-to-all-start.3 = ((bf16[16,30,2048]{2,1,0:T(8,128)(2,1)}), bf16[16,30,2048]{2,1,0:T(8,128)(2,1)}, u32[]{:S(2)}, u32[]{:S(2)}) async-start(bf16[16,30,2048]{2,1,0:T(8,128)(2,1)} %get-tuple-element.76), calls=%async_computation.3 | async-start | bytes 4194304 | tf_op jit(solution)/shard_map/all_to_all | solution.py:467
  93.0 28.9 %collective-permute-start = (bf16[64,1024]{1,0:T(8,128)(2,1)S(1)}, bf16[64,1024]{1,0:T(8,128)(2,1)S(1)}, u32[]{:S(2)}, u32[]{:S(2)}) collective-permute-start(bf16[64,1024]{1,0:T(8,128)(2,1)S(1)} %get-tuple-element.74), channel_id=1, source_target_pairs={{0,1},{1,0},{2,3},{3,2},{4,5},{5,4},{6,7},{7,6},{8,9},{9,8},{10,11... | collective-permute-start | bytes 393224 | tf_op jit(solution)/shard_map/ppermute | solution.py:487
  109.2 13.7 %collective-permute-start.1 = (bf16[64,1024]{1,0:T(8,128)(2,1)S(1)}, bf16[64,1024]{1,0:T(8,128)(2,1)S(1)}, u32[]{:S(2)}, u32[]{:S(2)}) collective-permute-start(bf16[64,1024]{1,0:T(8,128)(2,1)S(1)} %get-tuple-element.79), channel_id=1, source_target_pairs={{0,1},{1,0},{2,3},{3,2},{4,5},{5,4},{6,7},{7,6},{8,9},{9,8},{10,11... | collective-permute-start | bytes 393224 | tf_op jit(solution)/shard_map/ppermute | solution.py:495
  177.7 9.2 %collective-permute-start.2 = (bf16[16,8,1152]{2,1,0:T(8,128)(2,1)S(1)}, bf16[16,8,1152]{2,1,0:T(8,128)(2,1)S(1)}, u32[]{:S(2)}, u32[]{:S(2)}) collective-permute-start(bf16[16,8,1152]{2,1,0:T(8,128)(2,1)S(1)} %all_to_all.31.refs_0_), channel_id=1, source_target_pairs={{0,1},{1,0},{2,3},{3,2},{4,5},{5,4},{6,7},{7,6},{8,9},{9,8},{10,11... | collective-permute-start | bytes 884744 | tf_op jit(solution)/shard_map/ppermute | solution.py:513

commit v5 on v4

--- a/solution.py
+++ b/solution.py
@@ -126,9 +126,20 @@
     return jnp.concatenate([block.astype(F32), extra], axis=0)
 
 
-def send_kernel(where, ready, done, ids, tokens, out):
+def own_block(array, index, block):
+    total = None
+    for b in range(array.shape[1] // block):
+        part = jnp.where(index == b, array[:, b * block : (b + 1) * block], 0)
+        total = part if total is None else total + part
+    return total
+
+
+def send_kernel(where, ready, done, all_ids, tokens, out):
+    block = tokens.shape[0]
+    ready(0)
+    ids = own_block(all_ids[...], where[1], block)
     spot = iota((EXP_DEV * ROWS, 1), 0)
-    pick = slot_rows_of(ids[...], where[0] + spot // ROWS, spot % ROWS, ids.shape[1]).astype(BF)
+    pick = slot_rows_of(ids, where[0] + spot // ROWS, spot % ROWS, block).astype(BF)
     ready(1)
     picked = dot(pick, tokens[...]).astype(BF)
     per_expert = out.shape[0] // EXP_DEV
@@ -151,22 +162,22 @@
     ]
 
 
-def prepare_kernel(where, ids, rows, all_ids, all_weight, *refs):
+def prepare_kernel(where, rows, all_ids, all_weight, *refs):
     out, scale, rows_v, ids_v, weight_v, picked, scale_v = refs[-7:]
 
-    @pl.when(where[1] == where[2])
+    @pl.when(where[2] == where[3])
     def _():
         pltpu.sync_copy(rows, rows_v)
-        send_kernel(where, lambda _: None, None, ids, rows_v, picked)
+        pltpu.sync_copy(all_ids, ids_v)
+        send_kernel(where, lambda _: None, None, ids_v, rows_v, picked)
         pltpu.sync_copy(picked, out)
-        pltpu.sync_copy(all_ids, ids_v)
         pltpu.sync_copy(all_weight, weight_v)
-        block = ids.shape[1]
+        block = rows.shape[0]
         per_step = LANES // block
 
         def some_blocks(i, carry):
             cols = pl.ds(pl.multiple_of(i * LANES, LANES), LANES)
-            parts = weights_of_slots(where[3], ids_v[:, cols], weight_v[:, cols], block)
+            parts = weights_of_slots(where[4], ids_v[:, cols], weight_v[:, cols], block)
             for j, part in enumerate(parts):
                 first = pl.multiple_of((i * per_step + j) * ROWS, ROWS)
                 scale_v[pl.ds(first, ROWS), :] = part
@@ -176,7 +187,7 @@
         pltpu.sync_copy(scale_v, scale)
 
 
-def prepare(turn, core, experts, ids, rows, all_ids, all_weight, shapes, before=()):
+def prepare(turn, core, column_expert, dp_index, expert, rows, all_ids, all_weight, shapes, before=()):
     arrays = [
         pltpu.with_memory_space_constraint(array, pltpu.HBM)
         for array in (rows, all_ids, all_weight, *before)
@@ -185,9 +196,9 @@
     return pl.pallas_call(
         prepare_kernel,
         out_shape=[pltpu.HBM(out, out_kind), pltpu.HBM(scale, scale_kind)],
-        in_specs=[pl.BlockSpec(memory_space=pltpu.SMEM), VMEM] + [HBM] * len(arrays),
+        in_specs=[pl.BlockSpec(memory_space=pltpu.SMEM)] + [HBM] * len(arrays),
         out_specs=[HBM, HBM],
-        input_output_aliases={5: 0, 6: 1} if before else {},
+        input_output_aliases={4: 0, 5: 1} if before else {},
         scratch_shapes=[
             pltpu.VMEM(rows.shape, rows.dtype),
             pltpu.VMEM(all_ids.shape, all_ids.dtype),
@@ -196,7 +207,10 @@
             pltpu.VMEM(scale, scale_kind),
         ],
         compiler_params=pltpu.CompilerParams(vmem_limit_bytes=8 << 20),
-    )(jnp.stack([experts[0], core, jnp.int32(turn), experts[1]]).astype(jnp.int32), ids, *arrays)
+    )(
+        jnp.stack([column_expert, dp_index, core, jnp.int32(turn), expert]).astype(jnp.int32),
+        *arrays,
+    )
 
 
 def forward_kernel(
@@ -313,10 +327,37 @@
     route[...] = result
 
 
-def tokens_kernel(where, ready, done, returned, place, keep, give, total, full):
-    back, rest = gathered(returned, total)
-    full[...] = dot(place[...], back) + dot(place[...], rest)
-    shared(where[0], full, keep, give)
+def tokens_kernel(where, returned, place, out, held, total, sems):
+    width = out.shape[1]
+    cols = pl.ds(pl.multiple_of(where[0] * width, LANES), width)
+    pieces = held.shape[0] // EXP_DEV
+    spans = [slice(j * pieces, (j + 1) * pieces) for j in range(EXP_DEV)]
+    loads = begin([(returned.at[span, :, cols], held.at[span]) for span in spans], sems)
+    for j, span in enumerate(spans):
+        loads[j].wait()
+        part = held[span.start].astype(F32)
+        for d in range(span.start + 1, span.stop):
+            part = part + held[d].astype(F32)
+        total[j * ROWS : (j + 1) * ROWS, :] = padded(part)
+    back, rest = split(total[...])
+    out[...] = (dot(place[...], back) + dot(place[...], rest)).astype(out.dtype)
+
+
+def tokens_half(side, returned, place, kind):
+    sources, slots, width = returned.shape
+    half = width // CORES
+    return pl.pallas_call(
+        tokens_kernel,
+        out_shape=jax.ShapeDtypeStruct((place.shape[0], half), kind),
+        in_specs=[pl.BlockSpec(memory_space=pltpu.SMEM), HBM, VMEM],
+        out_specs=VMEM,
+        scratch_shapes=[
+            pltpu.VMEM((sources, slots, half), BF),
+            pltpu.VMEM((EXP_DEV * ROWS, half), F32),
+            pltpu.SemaphoreType.DMA((EXP_DEV,)),
+        ],
+        compiler_params=pltpu.CompilerParams(vmem_limit_bytes=8 << 20),
+    )(side.reshape(1), pltpu.with_memory_space_constraint(returned, pltpu.HBM), place)
 
 
 def pack_kernel(
@@ -389,28 +430,22 @@
     def own_rows(array):
         return lax.dynamic_slice_in_dim(array, dp_index * row_count, row_count, 0)
 
-    def send(array, ids):
-        (sent,) = call(
-            send_kernel,
-            [((dp_count, SLOTS, width), BF, HBM)],
-            [column_expert],
-            [(ids, VMEM), (array, HBM)],
-        )
-        return sent
-
-    ids, all_ids, all_weight = own_rows(route_ids).T, route_ids.T, route_weight.T
+    all_ids, all_weight = route_ids.T, route_weight.T
     shapes = [((dp_count, SLOTS, width), BF), ((rows, 1), F32)]
-    experts = (column_expert, expert)
-    prepared = prepare(0, core, experts, ids, d_mixed, all_ids, all_weight, shapes)
-    *prepared, first_ids = lax.optimization_barrier((*prepared, ids))
-    sent = send(tokens, first_ids)
-    sent, ids, route_ids, route_weight = lax.optimization_barrier(
-        (sent, ids, route_ids, route_weight)
+    prepare_in = (core, column_expert, dp_index, expert, d_mixed, all_ids, all_weight, shapes)
+    prepared = prepare(0, *prepare_in)
+    *prepared, first_ids = lax.optimization_barrier((*prepared, all_ids))
+    (sent,) = call(
+        send_kernel,
+        [((dp_count, SLOTS, width), BF, HBM)],
+        [column_expert, dp_index],
+        [(first_ids, HBM), (tokens, HBM)],
+    )
+    sent, route_ids, route_weight, *prepared = lax.optimization_barrier(
+        (sent, route_ids, route_weight, *prepared)
     )
     rows_in = lax.all_to_all(sent, ("x", "y"), 0, 0, tiled=True)
-    sent_grad, scale = prepare(
-        1, core, experts, ids, d_mixed, all_ids, all_weight, shapes, prepared
-    )
+    sent_grad, scale = prepare(1, *prepare_in, prepared)
     rows_grad = lax.all_to_all(sent_grad, ("x", "y"), 0, 0, tiled=True)
 
     out, x, gate_factor, up_factor, hidden = call(
@@ -482,17 +517,12 @@
             (d_mixed, HBM),
         ],
         [gathered_v, full_v],
-        vmem=16,
     )
     mixed_other = lax.ppermute(mixed_give, "core", swap)
-    tokens_part, tokens_give = call(
-        tokens_kernel,
-        shares,
-        [core],
-        [(returned_in, VMEM), (own_place, VMEM)],
-        [gathered_v, full_v],
-    )
+    tokens_give = tokens_half(1 - core, returned_in, own_place, BF)
     tokens_other = lax.ppermute(tokens_give, "core", swap)
+    returned_in, tokens_give = lax.optimization_barrier((returned_in, tokens_give))
+    tokens_part = tokens_half(core, returned_in, own_place, F32)
     (packed,) = call(
         pack_kernel,
         [((z_count, 8, half + LANES), BF, VMEM)],

time: 189 us -> 188 us (level)
    pallas_call x0 -> x2, Pallas kernels: none -> 3 us  [tokens_half(): pl.pallas_call(tokens_kernel, out_shape=jax.ShapeDtypeStruct((place.shape...]
    pallas_call x9 -> x8, Pallas kernels: 26.4 us -> 24.7 us  [call(): pl.pallas_call(wrapped, out_shape=[result(*out) for out in outs], in_spec...]
  transfers between devices with their start and end apart: 7 -> 7, of which waited for: 6 -> 5; matrix products, arithmetic and copies ran while one was open for 1% -> 1% of each run, Pallas kernels for 16% -> 16%
where the time goes in v5:
time: 188 us
  starting transfers between devices  60.9 us (32%)
  blocking collectives  55 us (29%)
  Pallas kernels  35.6 us (19%)
  waiting for transfers between devices  33 us (18%)
  local copies, waits for them, and re-layouts  2.2 us (1%)
    all_to_all x1, blocking collectives, body(): parts = lax.all_to_all(packed, 'z', 0, 0, tiled=True)  29.9 us
    all_to_all x1, blocking collectives, body(): whole = lax.all_to_all(summed, 'z', 0, 0, tiled=True)  25.1 us
    pallas_call x8, Pallas kernels, call(): pl.pallas_call(wrapped, out_shape=[result(*out) for out in outs], in_spec...  24.7 us
    ppermute x1, starting transfers between devices, body(): tokens_other = lax.ppermute(tokens_give, 'core', swap)  12.9 us
    all_to_all x1, waiting for transfers between devices, body(): rows_grad = lax.all_to_all(sent_grad, ('x', 'y'), 0, 0, tiled=True)  12.5 us
    ppermute x1, starting transfers between devices, body(): mixed_other = lax.ppermute(mixed_give, 'core', swap)  11.9 us
    all_to_all x1, waiting for transfers between devices, body(): rows_in = lax.all_to_all(sent, ('x', 'y'), 0, 0, tiled=True)  11 us
    ppermute x1, starting transfers between devices, body(): other = lax.ppermute(whole, 'core', swap)  7.9 us
  transfers between devices with their start and end apart: 7, of which 5 were waited for; matrix products, arithmetic and copies ran while one was open for 1% of the time, Pallas kernels for 16%

profile of v5, /device:TPU:1, one launch (start us, length us, event | category | flops | bytes accessed | tf_op | source)
XLA Modules:
  0.0 187.6 jit_solution(2475362628721496201)
XLA Ops:
  0.7 0.1 pad_add_fusion.1.where
  0.7 0.1 stack.45.where
  0.8 0.5 shard_map.118
  1.4 3.2 %shard_map.119 = bf16[16,30,2048]{2,1,0:T(8,128)(2,1)} custom-call(s32[2]{0:T(128)S(1)} %pad_add_fusion.1.where, s32[6,1024]{1,0:T(8,128)} %bitcast.21, bf16[64,2048]{1,0:T(8,128)(2,1)} %refs_1_.1), custom_call_target="tpu_custom_call" | custom-call | tf_op jit(solution)/shard_map/pallas_call | solution.py:111
  4.6 7.6 %all-to-all-start = ((bf16[16,30,2048]{2,1,0:T(8,128)(2,1)}), bf16[16,30,2048]{2,1,0:T(8,128)(2,1)S(1)}, u32[]{:S(2)}, u32[]{:S(2)}) async-start(bf16[16,30,2048]{2,1,0:T(8,128)(2,1)} %shard_map.119), calls=%async_computation | async-start | bytes 4194304 | tf_op jit(solution)/shard_map/all_to_all | solution.py:447
  12.2 0.1 stack.21.where
  12.3 7.3 %shard_map.120 = (bf16[16,30,2048]{2,1,0:T(8,128)(2,1)}, f32[512,1]{1,0:T(8,128)}) custom-call(s32[5]{0:T(128)S(1)} %stack.21.where, bf16[64,2048]{1,0:T(8,128)(2,1)} %refs_3_.1, s32[6,1024]{1,0:T(8,128)} %bitcast.22, f32[6,1024]{1,0:T(8,128)} %bitcast.24, ...), custom_call_target="tpu_custom_call", output_to_operand_aliasing={{0}: (4, {}), {1}: (5, {})} | custom-call | tf_op jit(solution)/shard_map/pallas_call | solution.py:196
  19.6 11.0 %all-to-all-done.refs_1_ = bf16[16,30,2048]{2,1,0:T(8,128)(2,1)S(1)} async-done(((bf16[16,30,2048]{2,1,0:T(8,128)(2,1)}), bf16[16,30,2048]{2,1,0:T(8,128)(2,1)S(1)}, u32[]{:S(2)}, u32[]{:S(2)}) %all-to-all-start) | async-done | bytes 1966112 | tf_op jit(solution)/shard_map/all_to_all | solution.py:447
  30.6 7.0 %all-to-all-start.1 = ((bf16[16,30,2048]{2,1,0:T(8,128)(2,1)}), bf16[16,30,2048]{2,1,0:T(8,128)(2,1)}, u32[]{:S(2)}, u32[]{:S(2)}) async-start(bf16[16,30,2048]{2,1,0:T(8,128)(2,1)} %get-tuple-element.56), calls=%async_computation.1 | async-start | bytes 4194304 | tf_op jit(solution)/shard_map/all_to_all | solution.py:449
  37.7 6.0 %shard_map.121 = (bf16[16,30,2048]{2,1,0:T(8,128)(2,1)}, bf16[512,2048]{1,0:T(8,128)(2,1)}, f32[512,176]{1,0:T(8,128)}, f32[512,176]{1,0:T(8,128)}, bf16[512,176]{1,0:T(8,128)(2,1)}) custom-call(s32[1]{0:T(128)} %bitcast.2.where, f32[512,1]{1,0:T(8,128)} %get-tuple-element.53.refs_0_, bf16[16,30,2048]{2,1,0:T(8,128)(2,1)S(1)} %all-to-all-done.refs_1_, ...), custom_call_target="tpu_custom_call" | custom-call | tf_op jit(solution)/shard_map/pallas_call | solution.py:111
  43.6 12.5 %all-to-all-done.1.refs_0_ = bf16[16,30,2048]{2,1,0:T(8,128)(2,1)} async-done(((bf16[16,30,2048]{2,1,0:T(8,128)(2,1)}), bf16[16,30,2048]{2,1,0:T(8,128)(2,1)}, u32[]{:S(2)}, u32[]{:S(2)}) %all-to-all-start.1) | async-done | bytes 1966112 | tf_op jit(solution)/shard_map/all_to_all | solution.py:449
  56.2 6.7 %all-to-all-start.2 = ((bf16[16,30,2048]{2,1,0:T(8,128)(2,1)}), bf16[16,30,2048]{2,1,0:T(8,128)(2,1)S(1)}, u32[]{:S(2)}, u32[]{:S(2)}) async-start(bf16[16,30,2048]{2,1,0:T(8,128)(2,1)} %get-tuple-element.57), calls=%async_computation.2 | async-start | bytes 4194304 | tf_op jit(solution)/shard_map/all_to_all | solution.py:471
  62.9 7.1 %shard_map.122 = (bf16[16,30,2048]{2,1,0:T(8,128)(2,1)}, bf16[512,2048]{1,0:T(8,128)(2,1)}, bf16[512,176]{1,0:T(8,128)(2,1)}, bf16[512,176]{1,0:T(8,128)(2,1)}) custom-call(s32[1]{0:T(128)} %bitcast.2.where, bf16[16,30,2048]{2,1,0:T(8,128)(2,1)} %all-to-all-done.1.refs_0_, bf16[176,2048]{1,0:T(8,128)(2,1)} %bitcast.19, ...), custom_call_target="tpu_custom_call" | custom-call | tf_op jit(solution)/shard_map/pallas_call | solution.py:111
  70.1 4.9 %shard_map.123 = (bf16[176,2048]{1,0:T(8,128)(2,1)}, bf16[176,2048]{1,0:T(8,128)(2,1)}, bf16[176,2048]{1,0:T(8,128)(2,1)}) custom-call(s32[1]{0:T(128)} %bitcast.2.where, bf16[512,2048]{1,0:T(8,128)(2,1)} %get-tuple-element.58.refs_0_, bf16[512,2048]{1,0:T(8,128)(2,1)} %get-tuple-element.62.refs_1_, bf16[512,176]{1,0:T(8,128)(2,1)} %get-tuple-element.63.refs_2_, ...), custom_call_target="tpu_custom_call" | custom-call | tf_op jit(solution)/shard_map/pallas_call | solution.py:111
  75.0 6.3 %all-to-all-done.2.refs_0_ = bf16[16,30,2048]{2,1,0:T(8,128)(2,1)S(1)} async-done(((bf16[16,30,2048]{2,1,0:T(8,128)(2,1)}), bf16[16,30,2048]{2,1,0:T(8,128)(2,1)S(1)}, u32[]{:S(2)}, u32[]{:S(2)}) %all-to-all-start.2) | async-done | bytes 1966112 | tf_op jit(solution)/shard_map/all_to_all | solution.py:471
  81.3 6.8 %all-to-all-start.3 = ((bf16[16,30,2048]{2,1,0:T(8,128)(2,1)}), bf16[16,30,2048]{2,1,0:T(8,128)(2,1)}, u32[]{:S(2)}, u32[]{:S(2)}) async-start(bf16[16,30,2048]{2,1,0:T(8,128)(2,1)} %get-tuple-element.77), calls=%async_computation.3 | async-start | bytes 4194304 | tf_op jit(solution)/shard_map/all_to_all | solution.py:502
  88.1 0.1 pad_add_fusion.where
  88.2 1.0 copy.15
  89.2 0.2 copy.16
  89.4 0.8 constant_dynamic-slice_fusion.1.refs_1_
  90.2 2.5 %shard_map.124 = (f32[64,1024]{1,0:T(8,128)S(1)}, bf16[64,1024]{1,0:T(8,128)(2,1)S(1)}, f32[64,128]{1,0:T(8,128)S(1)}, bf16[64,64]{1,0:T(8,128)(2,1)S(1)}) custom-call(s32[2]{0:T(128)S(1)} %pad_add_fusion.where, bf16[16,30,2048]{2,1,0:T(8,128)(2,1)S(1)} %all-to-all-done.2.refs_0_, s32[64,6]{1,0:T(8,128)S(1)} %constant_dynamic-slice_fusion.1.refs_1_, ...), custom_call_target="tpu_custom_call" | custom-call | tf_op jit(solution)/shard_map/pallas_call | solution.py:111
  92.7 11.9 %collective-permute-start = (bf16[64,1024]{1,0:T(8,128)(2,1)S(1)}, bf16[64,1024]{1,0:T(8,128)(2,1)S(1)}, u32[]{:S(2)}, u32[]{:S(2)}) collective-permute-start(bf16[64,1024]{1,0:T(8,128)(2,1)S(1)} %get-tuple-element.75), channel_id=1, source_target_pairs={{0,1},{1,0},{2,3},{3,2},{4,5},{5,4},{6,7},{7,6},{8,9},{9,8},{10,11... | collective-permute-start | bytes 393224 | tf_op jit(solution)/shard_map/ppermute | solution.py:521
  104.6 1.9 %all-to-all-done.3.returned = bf16[16,30,2048]{2,1,0:T(8,128)(2,1)} async-done(((bf16[16,30,2048]{2,1,0:T(8,128)(2,1)}), bf16[16,30,2048]{2,1,0:T(8,128)(2,1)}, u32[]{:S(2)}, u32[]{:S(2)}) %all-to-all-start.3) | async-done | bytes 1966112 | tf_op jit(solution)/shard_map/all_to_all | solution.py:502
  106.6 1.5 shard_map.125
  108.1 12.9 %collective-permute-start.1 = (bf16[64,1024]{1,0:T(8,128)(2,1)S(1)}, bf16[64,1024]{1,0:T(8,128)(2,1)S(1)}, u32[]{:S(2)}, u32[]{:S(2)}) collective-permute-start(bf16[64,1024]{1,0:T(8,128)(2,1)S(1)} %shard_map.125), channel_id=1, source_target_pairs={{0,1},{1,0},{2,3},{3,2},{4,5},{5,4},{6,7},{7,6},{8,9},{9,8},{10,11... | collective-permute-start | bytes 393224 | tf_op jit(solution)/shard_map/ppermute | solution.py:523
  121.0 1.5 shard_map.126.refs_3_
  122.6 29.9 %all_to_all.30.refs_0_ = bf16[16,8,1152]{2,1,0:T(8,128)(2,1)S(1)} all-to-all(bf16[16,8,1152]{2,1,0:T(8,128)(2,1)S(1)} %shard_map.127), channel_id=1, replica_groups=mesh['x'=4,'y'=4,'z'=16,'core'=2] {'z'}, dimensions={0} | all-to-all | bytes 589824 | tf_op jit(solution)/shard_map/all_to_all | solution.py:538
  152.5 0.1 shard_map.128
  152.6 25.1 %all_to_all.31.refs_0_ = bf16[16,8,1152]{2,1,0:T(8,128)(2,1)S(1)} all-to-all(bf16[16,8,1152]{2,1,0:T(8,128)(2,1)S(1)} %shard_map.128), channel_id=1, replica_groups=mesh['x'=4,'y'=4,'z'=16,'core'=2] {'z'}, dimensions={0} | all-to-all | bytes 589824 | tf_op jit(solution)/shard_map/all_to_all | solution.py:542
  177.7 7.9 %collective-permute-start.2 = (bf16[16,8,1152]{2,1,0:T(8,128)(2,1)S(1)}, bf16[16,8,1152]{2,1,0:T(8,128)(2,1)S(1)}, u32[]{:S(2)}, u32[]{:S(2)}) collective-permute-start(bf16[16,8,1152]{2,1,0:T(8,128)(2,1)S(1)} %all_to_all.31.refs_0_), channel_id=1, source_target_pairs={{0,1},{1,0},{2,3},{3,2},{4,5},{5,4},{6,7},{7,6},{8,9},{9,8},{10,11... | collective-permute-start | bytes 884744 | tf_op jit(solution)/shard_map/ppermute | solution.py:543
  185.6 1.2 collective-permute-done.2.refs_1_
  186.8 0.8 shard_map.129
  (8 shorter events, 0.1 us)
Async XLA Ops:
  4.6 26.0 %all-to-all-start = ((bf16[16,30,2048]{2,1,0:T(8,128)(2,1)}), bf16[16,30,2048]{2,1,0:T(8,128)(2,1)S(1)}, u32[]{:S(2)}, u32[]{:S(2)}) async-start(bf16[16,30,2048]{2,1,0:T(8,128)(2,1)} %shard_map.119), calls=%async_computation | async-start | bytes 4194304 | tf_op jit(solution)/shard_map/all_to_all | solution.py:447
  30.6 25.5 %all-to-all-start.1 = ((bf16[16,30,2048]{2,1,0:T(8,128)(2,1)}), bf16[16,30,2048]{2,1,0:T(8,128)(2,1)}, u32[]{:S(2)}, u32[]{:S(2)}) async-start(bf16[16,30,2048]{2,1,0:T(8,128)(2,1)} %get-tuple-element.56), calls=%async_computation.1 | async-start | bytes 4194304 | tf_op jit(solution)/shard_map/all_to_all | solution.py:449
  56.2 25.1 %all-to-all-start.2 = ((bf16[16,30,2048]{2,1,0:T(8,128)(2,1)}), bf16[16,30,2048]{2,1,0:T(8,128)(2,1)S(1)}, u32[]{:S(2)}, u32[]{:S(2)}) async-start(bf16[16,30,2048]{2,1,0:T(8,128)(2,1)} %get-tuple-element.57), calls=%async_computation.2 | async-start | bytes 4194304 | tf_op jit(solution)/shard_map/all_to_all | solution.py:471
  75.0 13.2 %copy-start = (s32[1024,6]{0,1:T(8,128)S(1)}, s32[1024,6]{0,1:T(8,128)}, u32[]{:S(2)}) copy-start(s32[1024,6]{0,1:T(8,128)} %param.9) | copy-start | bytes 73732
  75.0 14.2 %copy-start.1 = (f32[1024,6]{0,1:T(8,128)S(1)}, f32[1024,6]{0,1:T(8,128)}, u32[]{:S(2)}) copy-start(f32[1024,6]{0,1:T(8,128)} %param.10) | copy-start | bytes 73732
  81.3 25.3 %all-to-all-start.3 = ((bf16[16,30,2048]{2,1,0:T(8,128)(2,1)}), bf16[16,30,2048]{2,1,0:T(8,128)(2,1)}, u32[]{:S(2)}, u32[]{:S(2)}) async-start(bf16[16,30,2048]{2,1,0:T(8,128)(2,1)} %get-tuple-element.77), calls=%async_computation.3 | async-start | bytes 4194304 | tf_op jit(solution)/shard_map/all_to_all | solution.py:502
  92.7 29.7 %collective-permute-start = (bf16[64,1024]{1,0:T(8,128)(2,1)S(1)}, bf16[64,1024]{1,0:T(8,128)(2,1)S(1)}, u32[]{:S(2)}, u32[]{:S(2)}) collective-permute-start(bf16[64,1024]{1,0:T(8,128)(2,1)S(1)} %get-tuple-element.75), channel_id=1, source_target_pairs={{0,1},{1,0},{2,3},{3,2},{4,5},{5,4},{6,7},{7,6},{8,9},{9,8},{10,11... | collective-permute-start | bytes 393224 | tf_op jit(solution)/shard_map/ppermute | solution.py:521
  108.1 14.4 %collective-permute-start.1 = (bf16[64,1024]{1,0:T(8,128)(2,1)S(1)}, bf16[64,1024]{1,0:T(8,128)(2,1)S(1)}, u32[]{:S(2)}, u32[]{:S(2)}) collective-permute-start(bf16[64,1024]{1,0:T(8,128)(2,1)S(1)} %shard_map.125), channel_id=1, source_target_pairs={{0,1},{1,0},{2,3},{3,2},{4,5},{5,4},{6,7},{7,6},{8,9},{9,8},{10,11... | collective-permute-start | bytes 393224 | tf_op jit(solution)/shard_map/ppermute | solution.py:523
  177.7 9.1 %collective-permute-start.2 = (bf16[16,8,1152]{2,1,0:T(8,128)(2,1)S(1)}, bf16[16,8,1152]{2,1,0:T(8,128)(2,1)S(1)}, u32[]{:S(2)}, u32[]{:S(2)}) collective-permute-start(bf16[16,8,1152]{2,1,0:T(8,128)(2,1)S(1)} %all_to_all.31.refs_0_), channel_id=1, source_target_pairs={{0,1},{1,0},{2,3},{3,2},{4,5},{5,4},{6,7},{7,6},{8,9},{9,8},{10,11... | collective-permute-start | bytes 884744 | tf_op jit(solution)/shard_map/ppermute | solution.py:543

commit v6 on v4

--- a/solution.py
+++ b/solution.py
@@ -277,16 +277,10 @@
     return split(total[...])
 
 
-def shared(core, full, keep, give):
-    half = keep.shape[1]
-    keep[...] = full[:, pl.ds(pl.multiple_of(core * half, LANES), half)]
-    give[...] = full[:, pl.ds(pl.multiple_of((1 - core) * half, LANES), half)].astype(BF)
-
-
 def combine_kernel(
-    where, ready, done, returned, ids, weight, d_mixed, keep, give, route, place, total, full
+    where, ready, done, returned, ids, weight, d_mixed, keep, give, route, place, total
 ):
-    first_expert, core = where[0], where[1]
+    first_expert = where[0]
     rows = ids.shape[0]
     count = total.shape[0]
     lane = iota((rows, count), 1)
@@ -300,8 +294,8 @@
     high, low = split(pick * scale)
     ready(0)
     back, rest = gathered(returned, total)
-    full[...] = dot(high, back) + (dot(low, back) + dot(high, rest))
-    shared(core, full, keep, give)
+    keep[...] = dot(high, back) + (dot(low, back) + dot(high, rest))
+    give[...] = keep[...].astype(BF)
     ready(3)
     grad = d_mixed[...]
     paired = (dot(grad, back, 1, 1) + dot(grad, rest, 1, 1)) * pick
@@ -313,23 +307,26 @@
     route[...] = result
 
 
-def tokens_kernel(where, ready, done, returned, place, keep, give, total, full):
+def tokens_kernel(where, ready, done, returned, place, keep, give, total):
     back, rest = gathered(returned, total)
-    full[...] = dot(place[...], back) + dot(place[...], rest)
-    shared(where[0], full, keep, give)
+    keep[...] = dot(place[...], back) + dot(place[...], rest)
+    give[...] = keep[...].astype(BF)
 
 
 def pack_kernel(
     where, ready, done, mixed, mixed_other, route, d_tokens, d_tokens_other, out
 ):
-    half = mixed.shape[1]
+    half = mixed.shape[1] // 2
     high, low = [part.astype(F32) for part in split(route[...])]
-    sums = [mixed[...] + mixed_other[...].astype(F32)]
-    sums.append(d_tokens[...] + d_tokens_other[...].astype(F32))
+    sums = jnp.where(
+        where[0] == 1,
+        mixed[...] + mixed_other[...].astype(F32),
+        d_tokens[...] + d_tokens_other[...].astype(F32),
+    )
     for i in range(out.shape[0] // 2):
         rows = slice(8 * i, 8 * i + 8)
         for j, tail in enumerate((high, low)):
-            out[2 * i + j, :, :half] = sums[j][rows].astype(BF)
+            out[2 * i + j, :, :half] = sums[rows, j * half : (j + 1) * half].astype(BF)
             out[2 * i + j, :, half:] = tail[rows].astype(BF)
 
 
@@ -349,20 +346,25 @@
 
 
 def finish_kernel(where, ready, done, own, other, mixed, d_tokens, route):
-    core = where[0]
     width = own.shape[2] - LANES
-    for source, side in ((own, core), (other, 1 - core)):
-        cols = pl.ds(pl.multiple_of(side * width, LANES), width)
-        for target, odd in ((mixed, 0), (d_tokens, 1)):
-            for i in range(0, own.shape[0] // 2, 2):
-                pair = [source[2 * (i + j) + odd, :, :width].astype(F32) for j in range(2)]
-                target[8 * i : 8 * i + 16, cols] = jnp.concatenate(pair, axis=0).astype(BF)
+    mine = where[0] == 1
+    for i in range(0, own.shape[0] // 2, 2):
+        for j in range(2):
+            cols = slice(j * width, (j + 1) * width)
+            pairs = [
+                jnp.concatenate(
+                    [source[2 * (i + k) + j, :, :width].astype(F32) for k in range(2)], axis=0
+                )
+                for source in (own, other)
+            ]
+            mixed[8 * i : 8 * i + 16, cols] = jnp.where(mine, pairs[0], pairs[1]).astype(BF)
+            d_tokens[8 * i : 8 * i + 16, cols] = jnp.where(mine, pairs[1], pairs[0]).astype(BF)
     parts = []
     for i in range(own.shape[0] // 2):
         total = jnp.zeros((8, LANES), F32)
         for source in (own, other):
-            for odd in range(2):
-                total = total + source[2 * i + odd, :, width:].astype(F32)
+            for j in range(2):
+                total = total + source[2 * i + j, :, width:].astype(F32)
         parts.append(total)
     total = jnp.concatenate(parts, axis=0).T
     count = route.shape[0]
@@ -384,7 +386,6 @@
     gate_piece, up_piece, down_piece = gate_weight[0], up_weight[0], down_weight[0]
     out_shape = (dp_count, SLOTS, width)
     gathered_v = pltpu.VMEM((EXP_DEV * ROWS, width), F32)
-    full_v = pltpu.VMEM((row_count, width), F32)
 
     def own_rows(array):
         return lax.dynamic_slice_in_dim(array, dp_index * row_count, row_count, 0)
@@ -465,8 +466,7 @@
         (*grads, out_in, route_ids, route_weight)
     )
     returned_in = lax.all_to_all(out_in, ("x", "y"), 0, 0, tiled=True)
-    swap = [(0, 1), (1, 0)]
-    shares = [((row_count, half), F32, VMEM), ((row_count, half), BF, VMEM)]
+    shares = [((row_count, width), F32, VMEM), ((row_count, width), BF, VMEM)]
     mixed_part, mixed_give, route_part, own_place = call(
         combine_kernel,
         [
@@ -481,18 +481,17 @@
             (own_rows(route_weight), VMEM),
             (d_mixed, HBM),
         ],
-        [gathered_v, full_v],
-        vmem=16,
-    )
-    mixed_other = lax.ppermute(mixed_give, "core", swap)
+        [gathered_v],
+    )
+    mixed_other = lax.ppermute(mixed_give, "core", [(0, 1)])
     tokens_part, tokens_give = call(
         tokens_kernel,
         shares,
         [core],
         [(returned_in, VMEM), (own_place, VMEM)],
-        [gathered_v, full_v],
-    )
-    tokens_other = lax.ppermute(tokens_give, "core", swap)
+        [gathered_v],
+    )
+    tokens_other = lax.ppermute(tokens_give, "core", [(1, 0)])
     (packed,) = call(
         pack_kernel,
         [((z_count, 8, half + LANES), BF, VMEM)],
@@ -510,7 +509,7 @@
         total_kernel, [((z_count, 8, half + LANES), BF, VMEM)], [core], [(parts, VMEM)]
     )
     whole = lax.all_to_all(summed, "z", 0, 0, tiled=True)
-    other = lax.ppermute(whole, "core", swap)
+    other = lax.ppermute(whole, "core", [(0, 1), (1, 0)])
     mixed, d_tokens, d_route = call(
         finish_kernel,
         [

time: 189 us -> 189 us (level)
  waiting for transfers between devices: 34.1 us -> 45.4 us
  starting transfers between devices: 61.1 us -> 51 us
    all_to_all x1, waiting for transfers between devices: 2.92 us -> 13.6 us  [body(): returned_in = lax.all_to_all(out_in, ('x', 'y'), 0, 0, tiled=True)]
    ppermute x3, starting transfers between devices: 31.8 us -> 23.9 us  [the longest x1 14.6 us: body(): tokens_other = lax.ppermute(tokens_give, 'core', [(1, 0)])]
    all_to_all x1, starting transfers between devices: 8.42 us -> 6.19 us  [body(): returned_in = lax.all_to_all(out_in, ('x', 'y'), 0, 0, tiled=True)]
  transfers between devices with their start and end apart: 7 -> 7, of which waited for: 6 -> 6; matrix products, arithmetic and copies ran while one was open for 1% -> 0% of each run, Pallas kernels for 16% -> 16%
where the time goes in v6:
time: 189 us; the launch traced here: 188 us
  blocking collectives  55.4 us (29%)
  starting transfers between devices  51 us (27%)
  waiting for transfers between devices  45.4 us (24%)
  Pallas kernels  34 us (18%)
    all_to_all x1, blocking collectives, body(): parts = lax.all_to_all(packed, 'z', 0, 0, tiled=True)  30.1 us
    pallas_call x9, Pallas kernels, call(): pl.pallas_call(wrapped, out_shape=[result(*out) for out in outs], in_spec...  26.2 us
    all_to_all x1, blocking collectives, body(): whole = lax.all_to_all(summed, 'z', 0, 0, tiled=True)  25.2 us
    ppermute x1, starting transfers between devices, body(): tokens_other = lax.ppermute(tokens_give, 'core', [(1, 0)])  14.6 us
    all_to_all x1, waiting for transfers between devices, body(): returned_in = lax.all_to_all(out_in, ('x', 'y'), 0, 0, tiled=True)  13.6 us
    all_to_all x1, waiting for transfers between devices, body(): rows_grad = lax.all_to_all(sent_grad, ('x', 'y'), 0, 0, tiled=True)  12.4 us
    all_to_all x1, waiting for transfers between devices, body(): rows_in = lax.all_to_all(sent, ('x', 'y'), 0, 0, tiled=True)  11.2 us
    ppermute x1, starting transfers between devices, body(): other = lax.ppermute(whole, 'core', [(0, 1), (1, 0)])  8.02 us
  transfers between devices with their start and end apart: 7, of which 6 were waited for; matrix products, arithmetic and copies ran while one was open for 0% of the time, Pallas kernels for 16%

profile of v6, /device:TPU:1, one launch (start us, length us, event | category | flops | bytes accessed | tf_op | source)
XLA Modules:
  0.0 188.0 jit_solution(9197113012950976979)
XLA Ops:
  0.7 0.8 dynamic-slice_bitcast_fusion.ids.refs_0_
  1.4 0.1 add_add_fusion
  1.5 0.5 shard_map.118
  2.1 2.6 %shard_map.119 = bf16[16,30,2048]{2,1,0:T(8,128)(2,1)} custom-call(s32[1]{0:T(128)} %bitcast.1.where, s32[6,64]{1,0:T(8,128)S(1)} %dynamic-slice_bitcast_fusion.ids.refs_0_, bf16[64,2048]{1,0:T(8,128)(2,1)} %refs_1_.1), custom_call_target="tpu_custom_call" | custom-call | tf_op jit(solution)/shard_map/pallas_call | solution.py:111
  4.7 7.6 %all-to-all-start = ((bf16[16,30,2048]{2,1,0:T(8,128)(2,1)}), bf16[16,30,2048]{2,1,0:T(8,128)(2,1)S(1)}, u32[]{:S(2)}, u32[]{:S(2)}) async-start(bf16[16,30,2048]{2,1,0:T(8,128)(2,1)} %shard_map.119), calls=%async_computation | async-start | bytes 4194304 | tf_op jit(solution)/shard_map/all_to_all | solution.py:411
  12.3 7.2 %shard_map.120 = (bf16[16,30,2048]{2,1,0:T(8,128)(2,1)}, f32[512,1]{1,0:T(8,128)}) custom-call(s32[4]{0:T(128)S(1)} %get-tuple-element.86.where, s32[6,64]{1,0:T(8,128)S(1)} %dynamic-slice_bitcast_fusion.ids.refs_0_, bf16[64,2048]{1,0:T(8,128)(2,1)} %refs_3_.1, s32[6,1024]{1,0:T(8,128)} %bitcast.21, ...), custom_call_target="tpu_custom_call", output_to_operand_aliasing={{0}: (5, {}), {1}: (6, {})} | custom-call | tf_op jit(solution)/shard_map/pallas_call | solution.py:185
  19.5 11.2 %all-to-all-done.refs_1_ = bf16[16,30,2048]{2,1,0:T(8,128)(2,1)S(1)} async-done(((bf16[16,30,2048]{2,1,0:T(8,128)(2,1)}), bf16[16,30,2048]{2,1,0:T(8,128)(2,1)S(1)}, u32[]{:S(2)}, u32[]{:S(2)}) %all-to-all-start) | async-done | bytes 1966112 | tf_op jit(solution)/shard_map/all_to_all | solution.py:411
  30.7 7.0 %all-to-all-start.1 = ((bf16[16,30,2048]{2,1,0:T(8,128)(2,1)}), bf16[16,30,2048]{2,1,0:T(8,128)(2,1)}, u32[]{:S(2)}, u32[]{:S(2)}) async-start(bf16[16,30,2048]{2,1,0:T(8,128)(2,1)} %get-tuple-element.55), calls=%async_computation.1 | async-start | bytes 4194304 | tf_op jit(solution)/shard_map/all_to_all | solution.py:415
  37.7 6.0 %shard_map.121 = (bf16[16,30,2048]{2,1,0:T(8,128)(2,1)}, bf16[512,2048]{1,0:T(8,128)(2,1)}, f32[512,176]{1,0:T(8,128)}, f32[512,176]{1,0:T(8,128)}, bf16[512,176]{1,0:T(8,128)(2,1)}) custom-call(s32[1]{0:T(128)} %bitcast.2.where, f32[512,1]{1,0:T(8,128)} %get-tuple-element.52.refs_0_, bf16[16,30,2048]{2,1,0:T(8,128)(2,1)S(1)} %all-to-all-done.refs_1_, ...), custom_call_target="tpu_custom_call" | custom-call | tf_op jit(solution)/shard_map/pallas_call | solution.py:111
  43.7 12.4 %all-to-all-done.1.refs_0_ = bf16[16,30,2048]{2,1,0:T(8,128)(2,1)} async-done(((bf16[16,30,2048]{2,1,0:T(8,128)(2,1)}), bf16[16,30,2048]{2,1,0:T(8,128)(2,1)}, u32[]{:S(2)}, u32[]{:S(2)}) %all-to-all-start.1) | async-done | bytes 1966112 | tf_op jit(solution)/shard_map/all_to_all | solution.py:415
  56.0 6.4 %all-to-all-start.2 = ((bf16[16,30,2048]{2,1,0:T(8,128)(2,1)}), bf16[16,30,2048]{2,1,0:T(8,128)(2,1)S(1)}, u32[]{:S(2)}, u32[]{:S(2)}) async-start(bf16[16,30,2048]{2,1,0:T(8,128)(2,1)} %get-tuple-element.56), calls=%async_computation.2 | async-start | bytes 4194304 | tf_op jit(solution)/shard_map/all_to_all | solution.py:437
  62.4 7.1 %shard_map.122 = (bf16[16,30,2048]{2,1,0:T(8,128)(2,1)}, bf16[512,2048]{1,0:T(8,128)(2,1)}, bf16[512,176]{1,0:T(8,128)(2,1)}, bf16[512,176]{1,0:T(8,128)(2,1)}) custom-call(s32[1]{0:T(128)} %bitcast.2.where, bf16[16,30,2048]{2,1,0:T(8,128)(2,1)} %all-to-all-done.1.refs_0_, bf16[176,2048]{1,0:T(8,128)(2,1)} %bitcast.19, ...), custom_call_target="tpu_custom_call" | custom-call | tf_op jit(solution)/shard_map/pallas_call | solution.py:111
  69.6 4.9 %shard_map.123 = (bf16[176,2048]{1,0:T(8,128)(2,1)}, bf16[176,2048]{1,0:T(8,128)(2,1)}, bf16[176,2048]{1,0:T(8,128)(2,1)}) custom-call(s32[1]{0:T(128)} %bitcast.2.where, bf16[512,2048]{1,0:T(8,128)(2,1)} %get-tuple-element.57.refs_0_, bf16[512,2048]{1,0:T(8,128)(2,1)} %get-tuple-element.61.refs_1_, bf16[512,176]{1,0:T(8,128)(2,1)} %get-tuple-element.62.refs_2_, ...), custom_call_target="tpu_custom_call" | custom-call | tf_op jit(solution)/shard_map/pallas_call | solution.py:111
  74.5 0.0 copy-start
  74.5 5.9 %all-to-all-done.2.refs_0_ = bf16[16,30,2048]{2,1,0:T(8,128)(2,1)S(1)} async-done(((bf16[16,30,2048]{2,1,0:T(8,128)(2,1)}), bf16[16,30,2048]{2,1,0:T(8,128)(2,1)S(1)}, u32[]{:S(2)}, u32[]{:S(2)}) %all-to-all-start.2) | async-done | bytes 1966112 | tf_op jit(solution)/shard_map/all_to_all | solution.py:437
  80.4 6.2 %all-to-all-start.3 = ((bf16[16,30,2048]{2,1,0:T(8,128)(2,1)}), bf16[16,30,2048]{2,1,0:T(8,128)(2,1)}, u32[]{:S(2)}, u32[]{:S(2)}) async-start(bf16[16,30,2048]{2,1,0:T(8,128)(2,1)} %get-tuple-element.76), calls=%async_computation.3 | async-start | bytes 4194304 | tf_op jit(solution)/shard_map/all_to_all | solution.py:468
  86.6 0.1 pad_add_fusion.where
  86.7 0.2 copy.15
  86.9 0.2 copy.16
  87.2 2.3 %shard_map.124 = (f32[64,2048]{1,0:T(8,128)S(1)}, bf16[64,2048]{1,0:T(8,128)(2,1)S(1)}, f32[64,128]{1,0:T(8,128)S(1)}, bf16[64,64]{1,0:T(8,128)(2,1)S(1)}) custom-call(s32[2]{0:T(128)S(1)} %pad_add_fusion.where, bf16[16,30,2048]{2,1,0:T(8,128)(2,1)S(1)} %all-to-all-done.2.refs_0_, s32[64,6]{1,0:T(8,128)S(1)} %constant_dynamic-slice_fusion.1.refs_1_, ...), custom_call_target="tpu_custom_call" | custom-call | tf_op jit(solution)/shard_map/pallas_call | solution.py:111
  89.5 1.3 collective-permute-start
  90.8 13.6 %all-to-all-done.3.refs_0_ = bf16[16,30,2048]{2,1,0:T(8,128)(2,1)} async-done(((bf16[16,30,2048]{2,1,0:T(8,128)(2,1)}), bf16[16,30,2048]{2,1,0:T(8,128)(2,1)}, u32[]{:S(2)}, u32[]{:S(2)}) %all-to-all-start.3) | async-done | bytes 1966112 | tf_op jit(solution)/shard_map/all_to_all | solution.py:468
  104.3 2.2 %shard_map.125 = (f32[64,2048]{1,0:T(8,128)S(1)}, bf16[64,2048]{1,0:T(8,128)(2,1)S(1)}) custom-call(s32[1]{0:T(128)} %bitcast.where, bf16[16,30,2048]{2,1,0:T(8,128)(2,1)} %all-to-all-done.3.refs_0_, bf16[64,64]{1,0:T(8,128)(2,1)S(1)} %get-tuple-element.77.refs_1_), custom_call_target="tpu_custom_call" | custom-call | tf_op jit(solution)/shard_map/pallas_call | solution.py:111
  106.5 14.6 %collective-permute-start.1 = (bf16[64,2048]{1,0:T(8,128)(2,1)S(1)}, bf16[64,2048]{1,0:T(8,128)(2,1)S(1)}, u32[]{:S(2)}, u32[]{:S(2)}) collective-permute-start(bf16[64,2048]{1,0:T(8,128)(2,1)S(1)} %get-tuple-element.79), channel_id=1, source_target_pairs={{1,0},{3,2},{5,4},{7,6},{9,8},{11,10},{13,12},{15,14},{17,16},{19,... | collective-permute-start | bytes 786440 | tf_op jit(solution)/shard_map/ppermute | solution.py:494
  121.2 1.1 collective-permute-done.1.refs_4_
  122.3 0.1 shard_map.126
  122.4 30.1 %all_to_all.30.refs_0_ = bf16[16,8,1152]{2,1,0:T(8,128)(2,1)S(1)} all-to-all(bf16[16,8,1152]{2,1,0:T(8,128)(2,1)S(1)} %shard_map.126), channel_id=1, replica_groups=mesh['x'=4,'y'=4,'z'=16,'core'=2] {'z'}, dimensions={0} | all-to-all | bytes 589824 | tf_op jit(solution)/shard_map/all_to_all | solution.py:507
  152.5 0.1 shard_map.127
  152.6 25.2 %all_to_all.31.refs_0_ = bf16[16,8,1152]{2,1,0:T(8,128)(2,1)S(1)} all-to-all(bf16[16,8,1152]{2,1,0:T(8,128)(2,1)S(1)} %shard_map.127), channel_id=1, replica_groups=mesh['x'=4,'y'=4,'z'=16,'core'=2] {'z'}, dimensions={0} | all-to-all | bytes 589824 | tf_op jit(solution)/shard_map/all_to_all | solution.py:511
  177.9 8.0 %collective-permute-start.2 = (bf16[16,8,1152]{2,1,0:T(8,128)(2,1)S(1)}, bf16[16,8,1152]{2,1,0:T(8,128)(2,1)S(1)}, u32[]{:S(2)}, u32[]{:S(2)}) collective-permute-start(bf16[16,8,1152]{2,1,0:T(8,128)(2,1)S(1)} %all_to_all.31.refs_0_), channel_id=1, source_target_pairs={{0,1},{1,0},{2,3},{3,2},{4,5},{5,4},{6,7},{7,6},{8,9},{9,8},{10,11... | collective-permute-start | bytes 884744 | tf_op jit(solution)/shard_map/ppermute | solution.py:512
  185.9 1.2 collective-permute-done.2.refs_1_
  187.1 0.9 shard_map.128
  (6 shorter events, 0.0 us)
Async XLA Ops:
  4.7 26.0 %all-to-all-start = ((bf16[16,30,2048]{2,1,0:T(8,128)(2,1)}), bf16[16,30,2048]{2,1,0:T(8,128)(2,1)S(1)}, u32[]{:S(2)}, u32[]{:S(2)}) async-start(bf16[16,30,2048]{2,1,0:T(8,128)(2,1)} %shard_map.119), calls=%async_computation | async-start | bytes 4194304 | tf_op jit(solution)/shard_map/all_to_all | solution.py:411
  30.7 25.3 %all-to-all-start.1 = ((bf16[16,30,2048]{2,1,0:T(8,128)(2,1)}), bf16[16,30,2048]{2,1,0:T(8,128)(2,1)}, u32[]{:S(2)}, u32[]{:S(2)}) async-start(bf16[16,30,2048]{2,1,0:T(8,128)(2,1)} %get-tuple-element.55), calls=%async_computation.1 | async-start | bytes 4194304 | tf_op jit(solution)/shard_map/all_to_all | solution.py:415
  56.0 24.4 %all-to-all-start.2 = ((bf16[16,30,2048]{2,1,0:T(8,128)(2,1)}), bf16[16,30,2048]{2,1,0:T(8,128)(2,1)S(1)}, u32[]{:S(2)}, u32[]{:S(2)}) async-start(bf16[16,30,2048]{2,1,0:T(8,128)(2,1)} %get-tuple-element.56), calls=%async_computation.2 | async-start | bytes 4194304 | tf_op jit(solution)/shard_map/all_to_all | solution.py:437
  74.5 12.2 %copy-start = (s32[1024,6]{0,1:T(8,128)S(1)}, s32[1024,6]{0,1:T(8,128)}, u32[]{:S(2)}) copy-start(s32[1024,6]{0,1:T(8,128)} %param.9) | copy-start | bytes 73732
  74.5 12.4 %copy-start.1 = (f32[1024,6]{0,1:T(8,128)S(1)}, f32[1024,6]{0,1:T(8,128)}, u32[]{:S(2)}) copy-start(f32[1024,6]{0,1:T(8,128)} %param.10) | copy-start | bytes 73732
  80.4 23.9 %all-to-all-start.3 = ((bf16[16,30,2048]{2,1,0:T(8,128)(2,1)}), bf16[16,30,2048]{2,1,0:T(8,128)(2,1)}, u32[]{:S(2)}, u32[]{:S(2)}) async-start(bf16[16,30,2048]{2,1,0:T(8,128)(2,1)} %get-tuple-element.76), calls=%async_computation.3 | async-start | bytes 4194304 | tf_op jit(solution)/shard_map/all_to_all | solution.py:468
  89.5 31.7 %collective-permute-start = (bf16[64,2048]{1,0:T(8,128)(2,1)S(1)}, bf16[64,2048]{1,0:T(8,128)(2,1)S(1)}, u32[]{:S(2)}, u32[]{:S(2)}) collective-permute-start(bf16[64,2048]{1,0:T(8,128)(2,1)S(1)} %get-tuple-element.74), channel_id=1, source_target_pairs={{0,1},{2,3},{4,5},{6,7},{8,9},{10,11},{12,13},{14,15},{16,17},{18,... | collective-permute-start | bytes 786440 | tf_op jit(solution)/shard_map/ppermute | solution.py:486
  106.5 15.7 %collective-permute-start.1 = (bf16[64,2048]{1,0:T(8,128)(2,1)S(1)}, bf16[64,2048]{1,0:T(8,128)(2,1)S(1)}, u32[]{:S(2)}, u32[]{:S(2)}) collective-permute-start(bf16[64,2048]{1,0:T(8,128)(2,1)S(1)} %get-tuple-element.79), channel_id=1, source_target_pairs={{1,0},{3,2},{5,4},{7,6},{9,8},{11,10},{13,12},{15,14},{17,16},{19,... | collective-permute-start | bytes 786440 | tf_op jit(solution)/shard_map/ppermute | solution.py:494
  177.9 9.2 %collective-permute-start.2 = (bf16[16,8,1152]{2,1,0:T(8,128)(2,1)S(1)}, bf16[16,8,1152]{2,1,0:T(8,128)(2,1)S(1)}, u32[]{:S(2)}, u32[]{:S(2)}) collective-permute-start(bf16[16,8,1152]{2,1,0:T(8,128)(2,1)S(1)} %all_to_all.31.refs_0_), channel_id=1, source_target_pairs={{0,1},{1,0},{2,3},{3,2},{4,5},{5,4},{6,7},{7,6},{8,9},{9,8},{10,11... | collective-permute-start | bytes 884744 | tf_op jit(solution)/shard_map/ppermute | solution.py:512
